TPU v7x, 32 devices: a whole 2x2x4 slice. The times are simulated.
32 devices in a mesh: section: 2 (over core), dp: 16 (over z, y, x).
Axes of the slice: x: 2, y: 2, z: 4, core: 2. Of those that a mesh axis runs over, the one named last changes fastest.
Arguments:
- embeddings: bfloat16 [2, 32, 512, 768], P('section', 'dp'), may hold values from -6 to 6
- cotangent: bfloat16 [32, 512, 768], P('dp'), may hold values from -6 to 6
- lengths: int32 [32], P('dp'), may hold values from 128 to 512, as said below
- qkv_weight: bfloat16 [2, 768, 2304], P('section'), may hold values from -0.3125 to 0.3125
- query_bias: float32 [2, 768], P('section'), may hold values from -3 to 3
- value_bias: float32 [2, 768], P('section'), may hold values from -3 to 3
- proj_weight: bfloat16 [2, 768, 768], P('section'), may hold values from -1.25 to 1.25
- proj_bias: float32 [2, 768], P('section'), may hold values from -3 to 3
- attn_gain: float32 [2, 768], P('section'), may hold values from 0.25 to 1.75
- attn_bias: float32 [2, 768], P('section'), may hold values from -2 to 2
- inner_weight: bfloat16 [2, 768, 3072], P('section'), may hold values from -0.21875 to 0.21875
- inner_bias: float32 [2, 3072], P('section'), may hold values from -3 to 3
- outer_weight: bfloat16 [2, 3072, 768], P('section'), may hold values from -0.15625 to 0.15625
- outer_bias: float32 [2, 768], P('section'), may hold values from -3 to 3
- ffn_gain: float32 [2, 768], P('section'), may hold values from 0.25 to 1.75
- ffn_bias: float32 [2, 768], P('section'), may hold values from -2 to 2
Outputs:
- block_output: bfloat16 [2, 32, 512, 768], P('section', 'dp')
- embedding_grads: float32 [2, 32, 512, 768], P('section', 'dp')
- grad_qkv_weight: float32 [2, 768, 2304], P('section')
- grad_query_bias: float32 [2, 768], P('section')
- grad_value_bias: float32 [2, 768], P('section')
- grad_proj_weight: float32 [2, 768, 768], P('section')
- grad_proj_bias: float32 [2, 768], P('section')
- grad_attn_gain: float32 [2, 768], P('section')
- grad_attn_bias: float32 [2, 768], P('section')
- grad_inner_weight: float32 [2, 768, 3072], P('section')
- grad_inner_bias: float32 [2, 3072], P('section')
- grad_outer_weight: float32 [2, 3072, 768], P('section')
- grad_outer_bias: float32 [2, 768], P('section')
- grad_ffn_gain: float32 [2, 768], P('section')
- grad_ffn_bias: float32 [2, 768], P('section')
Inputs may be any that keep to these rules, and one draw needn't show every extreme that they name: `lengths`: some passage has exactly 512 tokens.
All inputs are finite; a program needn't handle non-finite values.
Results may differ from a plain program's by a relative error of at most 0.015.
The roundings to bfloat16 on the way count: a program that leaves them out, or rounds other values in their place, can miss the bound.
Values may be sent and summed in bfloat16 or wider, within the bound.
No kernel may reach another device: no remote copies, remote signals or barrier semaphores. Data moves between devices by JAX's collectives and lax.ppermute only.
A program may use at most 320 MiB of HBM per device.

v0:
```python
from functools import partial

import jax
import jax.numpy as jnp
from jax import lax
from jax.sharding import PartitionSpec as P

HEADS = 12
HEAD_DIM = 64
MB = 2


EPSILON = 1e-06
BIG_NEG = -1e30


def from_behind(value, axis, steps):
    count = lax.axis_size(axis)
    leading, last = (max(0, -steps), min(count, count - steps))
    return lax.ppermute(value, axis, [(source, source + steps) for source in range(leading, last)])


def row_norm(hidden):
    centred = hidden - jnp.mean(hidden, axis=-1, keepdims=True)
    scale = lax.rsqrt(jnp.mean(centred * centred, axis=-1, keepdims=True) + EPSILON)
    return (centred * scale, scale)


def norm_back(grad, normal, scale, gain):
    scaled = grad * gain
    return scale * (
        scaled
        - jnp.mean(scaled, axis=-1, keepdims=True)
        - normal * jnp.mean(scaled * normal, axis=-1, keepdims=True)
    )


def split_heads(packed):
    batch_size, length = (packed.shape[0], packed.shape[1])
    split_parts = packed.reshape(batch_size, length, 3, HEADS, HEAD_DIM)
    return (split_parts[:, :, 0], split_parts[:, :, 1], split_parts[:, :, 2])


def score_block(query_part, key_part, key_mask):
    raw_scores = jnp.einsum(
        "bqhe,bkhe->bhqk", query_part, key_part, preferred_element_type=jnp.float32
    ) * HEAD_DIM ** (-0.5)
    return jnp.where(key_mask[:, None, None, :], raw_scores, BIG_NEG)


def layer_forward(params, inputs, key_mask):
    (
        qkv_weight,
        query_bias,
        value_bias,
        proj_weight,
        proj_bias,
        attn_gain,
        attn_bias,
        inner_weight,
        inner_bias,
        outer_weight,
        outer_bias,
        ffn_gain,
        ffn_bias,
    ) = params
    batch_size, length, model_width = inputs.shape
    qkv_shift = jnp.concatenate([query_bias, jnp.zeros_like(query_bias), value_bias])
    qkv_low = (
        jnp.einsum("bld,de->ble", inputs, qkv_weight, preferred_element_type=jnp.float32)
        + qkv_shift
    ).astype(jnp.bfloat16)
    query_part, key_part, value_part = split_heads(qkv_low)
    scores = score_block(query_part, key_part, key_mask)
    top_score = jnp.max(scores, axis=-1, keepdims=True)
    raised = jnp.exp(scores - top_score)
    total_mass = jnp.sum(raised, axis=-1, keepdims=True)
    attention = (raised / total_mass).astype(jnp.bfloat16)
    log_mass = (top_score + jnp.log(total_mass))[..., 0]
    context = jnp.einsum(
        "bhqk,bkhe->bqhe", attention, value_part, preferred_element_type=jnp.float32
    )
    context_low = context.reshape(batch_size, length, model_width).astype(jnp.bfloat16)
    attn_out = (
        jnp.einsum("bld,de->ble", context_low, proj_weight, preferred_element_type=jnp.float32)
        + proj_bias
    )
    first_normal, first_scale = row_norm(inputs.astype(jnp.float32) + attn_out)
    normed = first_normal * attn_gain + attn_bias
    inner_sum = (
        jnp.einsum(
            "bld,di->bli",
            normed.astype(jnp.bfloat16),
            inner_weight,
            preferred_element_type=jnp.float32,
        )
        + inner_bias
    )
    act_low = jax.nn.gelu(inner_sum, approximate=False).astype(jnp.bfloat16)
    outer_sum = (
        jnp.einsum("bli,id->bld", act_low, outer_weight, preferred_element_type=jnp.float32)
        + outer_bias
    )
    second_normal, second_scale = row_norm(normed + outer_sum)
    result = second_normal * ffn_gain + ffn_bias
    return (
        result,
        (
            inputs,
            qkv_low,
            log_mass,
            context_low,
            first_normal,
            first_scale,
            inner_sum,
            second_normal,
            second_scale,
        ),
    )


def backward_ffn(params, saved, grad_out):
    attn_gain, attn_bias, inner_weight, inner_bias, outer_weight, outer_bias, ffn_gain, ffn_bias = (
        params[5:]
    )
    (
        inputs,
        qkv_low,
        log_mass,
        context_low,
        first_normal,
        first_scale,
        inner_sum,
        second_normal,
        second_scale,
    ) = saved
    ffn_gain_grad = jnp.sum(grad_out * second_normal, axis=(0, 1))
    ffn_bias_grad = jnp.sum(grad_out, axis=(0, 1))
    second_grad = norm_back(grad_out, second_normal, second_scale, ffn_gain)
    outer_low = second_grad.astype(jnp.bfloat16)
    outer_bias_grad = jnp.sum(outer_low, axis=(0, 1), dtype=jnp.float32)
    act_low = jax.nn.gelu(inner_sum, approximate=False).astype(jnp.bfloat16)
    outer_weight_grad = jnp.einsum(
        "bli,bld->id", act_low, outer_low, preferred_element_type=jnp.float32
    )
    act_grad = jnp.einsum(
        "bld,id->bli", outer_low, outer_weight, preferred_element_type=jnp.float32
    )
    gelu_exact = partial(jax.nn.gelu, approximate=False)
    unused, pullback = jax.vjp(gelu_exact, inner_sum)
    inner_low = pullback(act_grad)[0].astype(jnp.bfloat16)
    inner_bias_grad = jnp.sum(inner_low, axis=(0, 1), dtype=jnp.float32)
    normed = first_normal * attn_gain + attn_bias
    inner_weight_grad = jnp.einsum(
        "bld,bli->di", normed.astype(jnp.bfloat16), inner_low, preferred_element_type=jnp.float32
    )
    normed_grad = second_grad + jnp.einsum(
        "bli,di->bld", inner_low, inner_weight, preferred_element_type=jnp.float32
    )
    return (
        (
            inner_weight_grad,
            inner_bias_grad,
            outer_weight_grad,
            outer_bias_grad,
            ffn_gain_grad,
            ffn_bias_grad,
        ),
        normed_grad,
    )


def backward_attn(params, saved, normed_grad, key_mask):
    qkv_weight, query_bias, value_bias, proj_weight, proj_bias, attn_gain, attn_bias = params[:7]
    inputs, qkv_low, log_mass, context_low, first_normal, first_scale = saved[:6]
    batch_size, length, model_width = inputs.shape
    attn_gain_grad = jnp.sum(normed_grad * first_normal, axis=(0, 1))
    attn_bias_grad = jnp.sum(normed_grad, axis=(0, 1))
    first_grad = norm_back(normed_grad, first_normal, first_scale, attn_gain)
    proj_low = first_grad.astype(jnp.bfloat16)
    proj_bias_grad = jnp.sum(proj_low, axis=(0, 1), dtype=jnp.float32)
    proj_weight_grad = jnp.einsum(
        "bld,ble->de", context_low, proj_low, preferred_element_type=jnp.float32
    )
    context_grad = jnp.einsum(
        "ble,de->bld", proj_low, proj_weight, preferred_element_type=jnp.float32
    )
    context_grad = context_grad.astype(jnp.bfloat16).reshape(batch_size, length, HEADS, HEAD_DIM)
    query_part, key_part, value_part = split_heads(qkv_low)
    attention = jnp.exp(score_block(query_part, key_part, key_mask) - log_mass[..., None])
    prob_grad = jnp.einsum(
        "bqhe,bkhe->bhqk", context_grad, value_part, preferred_element_type=jnp.float32
    )
    value_grad = jnp.einsum(
        "bhqk,bqhe->bkhe",
        attention.astype(jnp.bfloat16),
        context_grad,
        preferred_element_type=jnp.float32,
    )
    score_grad = attention * (prob_grad - jnp.sum(attention * prob_grad, axis=-1, keepdims=True))
    score_low = score_grad.astype(jnp.bfloat16)
    query_grad = jnp.einsum(
        "bhqk,bkhe->bqhe", score_low, key_part, preferred_element_type=jnp.float32
    ) * HEAD_DIM ** (-0.5)
    key_grad = jnp.einsum(
        "bhqk,bqhe->bkhe", score_low, query_part, preferred_element_type=jnp.float32
    ) * HEAD_DIM ** (-0.5)
    packed_grad = jnp.stack([query_grad, key_grad, value_grad], axis=2)
    packed_grad = packed_grad.reshape(batch_size, length, 3 * model_width).astype(jnp.bfloat16)
    packed_sums = jnp.sum(packed_grad, axis=(0, 1), dtype=jnp.float32)
    query_bias_grad = packed_sums[:model_width]
    value_bias_grad = packed_sums[2 * model_width :]
    qkv_weight_grad = jnp.einsum(
        "bld,ble->de", inputs, packed_grad, preferred_element_type=jnp.float32
    )
    input_grad = (
        jnp.einsum("ble,de->bld", packed_grad, qkv_weight, preferred_element_type=jnp.float32)
        + first_grad
    )
    return (
        (
            qkv_weight_grad,
            query_bias_grad,
            value_bias_grad,
            proj_weight_grad,
            proj_bias_grad,
            attn_gain_grad,
            attn_bias_grad,
        ),
        input_grad,
    )


def local(
    embeddings,
    cotangent,
    lengths,
    qkv_weight,
    query_bias,
    value_bias,
    proj_weight,
    proj_bias,
    attn_gain,
    attn_bias,
    inner_weight,
    inner_bias,
    outer_weight,
    outer_bias,
    ffn_gain,
    ffn_bias,
):
    params = tuple(
        (
            piece[0]
            for piece in (
                qkv_weight,
                query_bias,
                value_bias,
                proj_weight,
                proj_bias,
                attn_gain,
                attn_bias,
                inner_weight,
                inner_bias,
                outer_weight,
                outer_bias,
                ffn_gain,
                ffn_bias,
            )
        )
    )
    section_index = lax.axis_index("section")
    first_section = section_index == 0
    own_rows = embeddings[0]
    per_batch = own_rows.shape[0] // MB
    length = own_rows.shape[1]
    model_width = own_rows.shape[2]
    positions = jnp.arange(length, dtype=jnp.int32)
    key_masks = positions[None, :] < lengths[:, None]

    def take_rows(array, batch_index):
        return lax.dynamic_slice_in_dim(array, batch_index * per_batch, per_batch, 0)

    def layer_input(batch_index, head_rows):
        rows_now = take_rows(own_rows, batch_index)
        return jnp.where(first_section, rows_now, rows_now.at[:, 0].set(head_rows))

    outputs = jnp.zeros(own_rows.shape, jnp.bfloat16)
    arrived = jnp.zeros((per_batch, model_width), jnp.bfloat16)
    head_store = jnp.zeros((MB, per_batch, model_width), jnp.bfloat16)
    for moment in range(MB + 1):
        offset = moment - section_index
        active = (offset >= 0) & (offset < MB)
        batch_index = jnp.clip(offset, 0, MB - 1)
        head_store = jnp.where(
            active, lax.dynamic_update_index_in_dim(head_store, arrived, batch_index, 0), head_store
        )
        result, saved = layer_forward(
            params, layer_input(batch_index, arrived), take_rows(key_masks, batch_index)
        )
        outputs = jnp.where(
            active,
            lax.dynamic_update_slice_in_dim(
                outputs, result.astype(jnp.bfloat16), batch_index * per_batch, 0
            ),
            outputs,
        )
        if moment < MB:
            arrived = from_behind(result[:, 0].astype(jnp.bfloat16), "section", 1)
    attn_totals = tuple((jnp.zeros(piece.shape, jnp.float32) for piece in params[:7]))
    ffn_totals = tuple((jnp.zeros(piece.shape, jnp.float32) for piece in params[7:]))
    embed_grads = jnp.zeros(own_rows.shape, jnp.float32)
    returned = jnp.zeros((per_batch, model_width), jnp.bfloat16)
    for moment in range(MB + 1):
        offset = moment - 1 + section_index
        active = (offset >= 0) & (offset < MB)
        batch_index = jnp.clip(offset, 0, MB - 1)
        key_mask = take_rows(key_masks, batch_index)
        head_rows = lax.dynamic_index_in_dim(head_store, batch_index, 0, keepdims=False)
        unused, saved = layer_forward(params, layer_input(batch_index, head_rows), key_mask)
        row_weight = (key_mask & active).astype(jnp.float32)[..., None]
        later_grad = take_rows(cotangent, batch_index).astype(jnp.float32) * row_weight
        head_grad = (
            jnp.zeros(later_grad.shape, jnp.float32).at[:, 0].set(returned.astype(jnp.float32))
        )
        grad_out = jnp.where(first_section, head_grad, later_grad)
        ffn_grads, normed_grad = backward_ffn(params, saved, grad_out)
        ffn_totals = tuple((summed + term for summed, term in zip(ffn_totals, ffn_grads)))
        attn_grads, input_grad = backward_attn(params, saved, normed_grad, key_mask)
        attn_totals = tuple((summed + term for summed, term in zip(attn_totals, attn_grads)))
        if moment < MB:
            returned = from_behind(input_grad[:, 0].astype(jnp.bfloat16), "section", -1)
        kept_grad = jnp.where(first_section | (positions[None, :, None] > 0), input_grad, 0.0)
        embed_grads = jnp.where(
            active,
            lax.dynamic_update_slice_in_dim(embed_grads, kept_grad, batch_index * per_batch, 0),
            embed_grads,
        )
    gradients = lax.psum(attn_totals + ffn_totals, "dp")
    return (outputs[None], embed_grads[None]) + tuple((piece[None] for piece in gradients))


def solution(mesh):
    return jax.shard_map(
        local,
        mesh=mesh,
        in_specs=(
            P("section", "dp", None, None),
            P("dp", None, None),
            P("dp"),
            P("section", None, None),
            P("section", None),
            P("section", None),
            P("section", None, None),
            P("section", None),
            P("section", None),
            P("section", None),
            P("section", None, None),
            P("section", None),
            P("section", None, None),
            P("section", None),
            P("section", None),
            P("section", None),
        ),
        out_specs=(
            P("section", "dp", None, None),
            P("section", "dp", None, None),
            P("section", None, None),
            P("section", None),
            P("section", None),
            P("section", None, None),
            P("section", None),
            P("section", None),
            P("section", None),
            P("section", None, None),
            P("section", None),
            P("section", None, None),
            P("section", None),
            P("section", None),
            P("section", None),
        ),
        check_vma=False,
    )
```

profile of v0, /device:TPU:0, one launch (start us, length us, event | category | flops | bytes accessed | tf_op | source)
XLA Modules:
  0.0 1314.2 jit_solution(5540350646834725104)
XLA Ops:
  34.5 11.5 fusion.549
  46.0 6.1 fusion.292
  55.1 23.8 %fusion.551 = (f32[512]{0:T(512)}, f32[1,512,768]{2,1,0:T(8,128)}) fusion(f32[768]{0:T(1024)} %reduce.99, bf16[1,3072,768]{2,1,0:T(8,128)(2,1)} %param.46, bf16[1,768,3072]{2,1,0:T(8,128)(2,1)} %param.44, f32[3072]{0:T(1024)} %bitcast.716, f32[1,512,768]{2,1,0:T(8,128)} %copy-done.60, f32[768]{0:T(1024)S(1)} %copy-done.102, f32[768]{0:T(1024)S(1)} %reduce.97, ...), kind=kOutput, calls=%fused_computation.758 | convolution fusion | flops 4940365312 | bytes 12610560 | tf_op jit(solution)/shard_map/bli,id->bld/dot_general | solution.py:101
  101.4 11.5 fusion.556
  112.9 6.1 fusion.291
  122.0 23.8 %fusion.558 = (f32[512]{0:T(512)}, f32[1,512,768]{2,1,0:T(8,128)}) fusion(f32[768]{0:T(1024)} %reduce.99, bf16[1,3072,768]{2,1,0:T(8,128)(2,1)} %param.46, bf16[1,768,3072]{2,1,0:T(8,128)(2,1)} %param.44, f32[3072]{0:T(1024)} %bitcast.717, f32[1,512,768]{2,1,0:T(8,128)} %copy-done.61, f32[512]{0:T(512)} %add_rsqrt_fusion.9, f32[512]{0:T(512)} %copy-done.120, ...), kind=kOutput, calls=%fused_computation.761 | convolution fusion | flops 4940365312 | bytes 12610560 | tf_op jit(solution)/shard_map/bli,id->bld/dot_general | solution.py:101
  206.3 7.8 fusion.108
  243.0 48.6 %multiply_convert_fusion.3 = (bf16[512,3072]{1,0:T(8,128)(2,1)}, f32[512,3072]{1,0:T(8,128)}, bf16[512,3072]{1,0:T(8,128)(2,1)}, f32[512,3072]{1,0:T(8,128)}, bf...) fusion(f32[3072]{0:T(1024)S(1)} %bitcast.719, f32[512,3072]{1,0:T(8,128)} %fusion.108, ...), kind=kOutput, calls=%fused_computation.67 | convolution fusion | flops 2729312256 | bytes 53499904 | tf_op jit(solution)/shard_map/bld,di->bli/dot_general | solution.py:91
  297.7 10.3 convert_reduce_fusion.2
  319.9 6.9 fusion.320
  326.9 9.1 multiply_reduce_fusion.2
  336.0 6.8 multiply_convert_fusion.2
  381.2 10.1 convert_reduce_fusion.1
  403.3 6.9 fusion.317
  410.3 9.1 multiply_reduce_fusion.1
  419.4 7.0 multiply_convert_fusion.1
  456.5 9.1 convert_reduce_fusion
  465.6 7.2 multiply_reduce_fusion.6
  479.2 6.9 fusion.314
  486.2 9.1 multiply_reduce_fusion
  495.3 7.2 multiply_convert_fusion
  510.9 11.8 add_bitcast_fusion.1
  523.1 13.1 add_bitcast_fusion
  538.7 8.3 add_bitcast_fusion.2
  560.0 11.5 fusion.563
  571.5 6.1 fusion.290
  580.7 23.7 %fusion.565 = (f32[512]{0:T(512)}, f32[1,512,768]{2,1,0:T(8,128)}) fusion(f32[768]{0:T(1024)} %reduce.99, bf16[1,3072,768]{2,1,0:T(8,128)(2,1)} %param.46, bf16[1,768,3072]{2,1,0:T(8,128)(2,1)} %param.44, f32[3072]{0:T(1024)} %bitcast.718, f32[1,512,768]{2,1,0:T(8,128)} %copy-done.59, f32[512]{0:T(512)} %add_rsqrt_fusion.7, f32[512]{0:T(512)} %copy-done.118, ...), kind=kOutput, calls=%fused_computation.764 | convolution fusion | flops 4940365312 | bytes 12610560 | tf_op jit(solution)/shard_map/bli,id->bld/dot_general | solution.py:101
  619.8 84.4 %all-reduce.2 = (f32[1,768]{1,0:T(1,128)}, f32[1,768]{1,0:T(1,128)}, f32[1,768]{1,0:T(1,128)}, f32[1,768]{1,0:T(1,128)}, f32[1,768]{1,0:T(1,128)}, /*index=5*/f3...) all-reduce(f32[1,768]{1,0:T(1,128)} %broadcast_in_dim.243, ...), channel_id=1, replica_groups=mesh['section'=2,'dp'=16] {'dp'}, use_global_device_ids=true, to_apply=%region_55.56 | all-reduce | flops 9216 | bytes 73728 | tf_op jit(solution)/shard_map/psum | solution.py:339
  704.2 6.0 bitcast_dynamic-update-slice_fusion
  710.2 575.8 %all-reduce.6.cloned.1.call-done = (f32[1,768,2304]{2,1,0:T(8,128)}, f32[1,768,768]{2,1,0:T(8,128)}, f32[1,768,3072]{2,1,0:T(8,128)}, f32[1,3072,768]{2,1,0:T(8,128)}) async-done(((f32[1,768,2304]{2,1,0:T(8,128)}, f32[1,768,768]{2,1,0:T(8,128)}, f32[1,768,3072]{2,1,0:T(8,128)}, f32[1,3072,768]{2,1,0:T(8,128)}), (f32[1,768,2304]{2,1,0:T(8,128)}, f32[1,768,768]{2,1,0:T(8,128)}, f32[1,768,3072]{2,1,0:T(8,128)}, ...) | async-done | bytes 28311568 | tf_op jit(solution)/shard_map/psum | solution.py:339
  1286.0 6.6 copy.128
  1294.0 9.3 copy.130
  (551 shorter events, 296.2 us)
Async XLA Ops:
  7.2 15.8 %copy-start = (bf16[1,768,2304]{2,1,0:T(8,128)(2,1)S(1)}, bf16[1,768,2304]{2,1,0:T(8,128)(2,1)}, u32[]{:S(2)}) copy-start(bf16[1,768,2304]{2,1,0:T(8,128)(2,1)} %param.37) | copy-start | bytes 10616836
  7.2 1278.8 %all-reduce.6.cloned.1.call-start = ((), (), s32[]{:S(2)}) async-start(), calls=%async_computation | async-start | bytes 56623104 | tf_op jit(solution)/shard_map/psum | solution.py:339
  8.1 75.1 %copy-start.88 = (f32[768]{0:T(1024)}, f32[768]{0:T(1024)S(1)}, u32[]{:S(2)}) copy-start(f32[768]{0:T(1024)S(1)} %reduce.101) | copy-start | bytes 9220
  9.0 139.3 %copy-start.74 = (f32[768]{0:T(1024)}, f32[768]{0:T(1024)S(1)}, u32[]{:S(2)}) copy-start(f32[768]{0:T(1024)S(1)} %reduce.100) | copy-start | bytes 9220
  86.5 3.5 collective-permute-start
  151.9 3.3 collective-permute-start.1
  180.6 33.5 %copy-start.96 = (f32[512]{0:T(512)}, f32[512]{0:T(512)S(1)}, u32[]{:S(2)}) copy-start(f32[512]{0:T(512)S(1)} %broadcast_multiply_fusion.17) | copy-start | bytes 6148
  182.1 32.1 %copy-start.115 = (f32[512]{0:T(512)}, f32[512]{0:T(512)S(1)}, u32[]{:S(2)}) copy-start(f32[512]{0:T(512)S(1)} %add_rsqrt_fusion.5) | copy-start | bytes 6148
  241.5 50.1 %copy-start.62 = (bf16[12,64,512]{2,1,0:T(8,128)(2,1)}, bf16[12,64,512]{2,1,0:T(8,128)(2,1)S(1)}, u32[]{:S(2)}) copy-start(bf16[12,64,512]{2,1,0:T(8,128)(2,1)S(1)} %fusion.302) | copy-start | bytes 2359300
  241.6 50.0 %slice-start.17 = ((s8[4718592]{0:T(1024)(128)(4,1)}), s8[4194304]{0:T(1024)(128)(4,1)S(1)}, s32[]{:S(2)}) async-start(s8[4718592]{0:T(1024)(128)(4,1)} %bitcast.704), calls=%async_computation.18 | async-start | bytes 8388608
  242.5 49.1 %copy-start.7 = (f32[1,512,768]{2,1,0:T(8,128)}, f32[1,512,768]{2,1,0:T(8,128)S(1)}, u32[]{:S(2)}) copy-start(f32[1,512,768]{2,1,0:T(8,128)S(1)} %get-tuple-element.242) | copy-start | bytes 4718596
  242.9 130.7 %copy-start.91 = (f32[512]{0:T(512)}, f32[512]{0:T(512)S(1)}, u32[]{:S(2)}) copy-start(f32[512]{0:T(512)S(1)} %add_rsqrt_fusion.1) | copy-start | bytes 6148
  242.9 48.7 %copy-start.39 = (f32[1,512,768]{2,1,0:T(8,128)S(1)}, f32[1,512,768]{2,1,0:T(8,128)}, u32[]{:S(2)}) copy-start(f32[1,512,768]{2,1,0:T(8,128)} %copy-done.37) | copy-start | bytes 4718596
  242.9 48.7 %copy-start.97 = (f32[512]{0:T(512)S(1)}, f32[512]{0:T(512)}, u32[]{:S(2)}) copy-start(f32[512]{0:T(512)} %copy-done.96) | copy-start | bytes 6148
  242.9 48.7 %copy-start.116 = (f32[512]{0:T(512)S(1)}, f32[512]{0:T(512)}, u32[]{:S(2)}) copy-start(f32[512]{0:T(512)} %copy-done.115) | copy-start | bytes 6148
  242.9 48.7 %copy-start.121 = (f32[768]{0:T(1024)S(1)}, f32[768]{0:T(1024)}, u32[]{:S(2)}) copy-start(f32[768]{0:T(1024)} %reduce.99) | copy-start | bytes 9220
  243.0 48.7 %slice-start.18 = ((s8[4718592]{0:T(1024)(128)(4,1)}), s8[524288]{0:T(1024)(128)(4,1)S(1)}, s32[]{:S(2)}) async-start(s8[4718592]{0:T(1024)(128)(4,1)} %bitcast.704), calls=%async_computation.19 | async-start | bytes 1048576
  319.9 16.1 %slice-start.6 = ((s8[12582912]{0:T(1024)(128)(4,1)}), s8[4194304]{0:T(1024)(128)(4,1)S(1)}, s32[]{:S(2)}) async-start(s8[12582912]{0:T(1024)(128)(4,1)} %bitcast.645), calls=%async_computation.7 | async-start | bytes 8388608
  319.9 16.1 %slice-start.7 = ((s8[12582912]{0:T(1024)(128)(4,1)}), s8[4194304]{0:T(1024)(128)(4,1)S(1)}, s32[]{:S(2)}) async-start(s8[12582912]{0:T(1024)(128)(4,1)} %bitcast.645), calls=%async_computation.8 | async-start | bytes 8388608
  347.4 13.2 %slice-start.19 = ((s8[4718592]{0:T(1024)(128)(4,1)}), s8[4194304]{0:T(1024)(128)(4,1)S(1)}, s32[]{:S(2)}) async-start(s8[4718592]{0:T(1024)(128)(4,1)} %bitcast.706), calls=%async_computation.20 | async-start | bytes 8388608
  372.0 6.5 collective-permute-start.2
  403.3 16.1 %slice-start.3 = ((s8[12582912]{0:T(1024)(128)(4,1)}), s8[4194304]{0:T(1024)(128)(4,1)S(1)}, s32[]{:S(2)}) async-start(s8[12582912]{0:T(1024)(128)(4,1)} %bitcast.643), calls=%async_computation.4 | async-start | bytes 8388608
  403.3 16.1 %slice-start.4 = ((s8[12582912]{0:T(1024)(128)(4,1)}), s8[4194304]{0:T(1024)(128)(4,1)S(1)}, s32[]{:S(2)}) async-start(s8[12582912]{0:T(1024)(128)(4,1)} %bitcast.643), calls=%async_computation.5 | async-start | bytes 8388608
  449.9 3.8 collective-permute-start.3
  479.2 16.1 %slice-start = ((s8[12582912]{0:T(1024)(128)(4,1)}), s8[4194304]{0:T(1024)(128)(4,1)S(1)}, s32[]{:S(2)}) async-start(s8[12582912]{0:T(1024)(128)(4,1)} %bitcast.641), calls=%async_computation.1 | async-start | bytes 8388608
  479.2 16.1 %slice-start.1 = ((s8[12582912]{0:T(1024)(128)(4,1)}), s8[4194304]{0:T(1024)(128)(4,1)S(1)}, s32[]{:S(2)}) async-start(s8[12582912]{0:T(1024)(128)(4,1)} %bitcast.641), calls=%async_computation.2 | async-start | bytes 8388608
  508.7 14.0 %slice-start.9 = ((s8[9437184]{0:T(1024)(128)(4,1)}), s8[4194304]{0:T(1024)(128)(4,1)S(1)}, s32[]{:S(2)}) async-start(s8[9437184]{0:T(1024)(128)(4,1)} %bitcast.647), calls=%async_computation.10 | async-start | bytes 8388608
  510.9 27.7 %slice-start.12 = ((s8[7077888]{0:T(1024)(128)(4,1)}), s8[4194304]{0:T(1024)(128)(4,1)S(1)}, s32[]{:S(2)}) async-start(s8[7077888]{0:T(1024)(128)(4,1)} %bitcast.649), calls=%async_computation.13 | async-start | bytes 8388608
  523.1 13.1 copy-start.57
  523.1 15.6 %slice-start.13 = ((s8[7077888]{0:T(1024)(128)(4,1)}), s8[2883584]{0:T(1024)(128)(4,1)S(1)}, s32[]{:S(2)}) async-start(s8[7077888]{0:T(1024)(128)(4,1)} %bitcast.649), calls=%async_computation.14 | async-start | bytes 5767168
  580.7 26.7 %copy-start.76 = (f32[768]{0:T(1024)S(1)}, f32[768]{0:T(1024)}, u32[]{:S(2)}) copy-start(f32[768]{0:T(1024)} %copy-done.74) | copy-start | bytes 9220
  580.7 26.7 %copy-start.89 = (f32[768]{0:T(1024)S(1)}, f32[768]{0:T(1024)}, u32[]{:S(2)}) copy-start(f32[768]{0:T(1024)} %copy-done.88) | copy-start | bytes 9220
  (152 other events, 753.7 us)
Sparse Core Ops, SparseCore 0:
  547.1 738.8 all-reduce.5
where the time goes:
time: 1320 us; the launch traced here: 1310 us
  waiting for transfers between devices  577 us (44%)
  matrix products  444 us (34%)
  local copies, waits for them, and re-layouts  101 us (8%)
  blocking collectives  84.4 us (6%)
  other arithmetic  83.5 us (6%)
  between operations  16.3 us (1%)
    psum x1, waiting for transfers between devices, local(): gradients = lax.psum(attn_totals + ffn_totals, 'dp')  576 us
    psum x1, blocking collectives, local(): gradients = lax.psum(attn_totals + ffn_totals, 'dp')  84.4 us
    dot_general x6, matrix products, layer_forward(): jnp.einsum('bli,id->bld', act_low, outer_weight, preferred_element_type=j...  79.7 us
    dot_general x3, matrix products, layer_forward(): jnp.einsum('bld,di->bli', normed.astype(jnp.bfloat16), inner_weight, pref...  61.3 us
    unnamed x364, local copies, waits for them, and re-layouts  48 us
    sub x3, matrix products, layer_forward(): raised = jnp.exp(scores - top_score)  34.5 us
    dot_general x6, matrix products, layer_forward(): jnp.einsum('bhqk,bkhe->bqhe', attention, value_part, preferred_element_ty...  29.5 us
    dot_general x3, matrix products, backward_ffn(): jnp.einsum('bld,id->bli', outer_low, outer_weight, preferred_element_type...  29.5 us
  transfers between devices with their start and end apart: 5, of which 3 were waited for; matrix products, arithmetic and copies ran while one was open for 6% of the time, Pallas kernels for 0%

commit v1 on v0

v1 whole, which is shorter than its diff:
```python
from functools import partial

import jax
import jax.numpy as jnp
from jax import lax
from jax.sharding import PartitionSpec as P

HEADS = 12
HEAD_DIM = 64
EPSILON = 1e-06
BIG_NEG = -1e30
BF = jnp.bfloat16
F32 = jnp.float32


def row_norm(hidden):
    centred = hidden - jnp.mean(hidden, axis=-1, keepdims=True)
    scale = lax.rsqrt(jnp.mean(centred * centred, axis=-1, keepdims=True) + EPSILON)
    return (centred * scale, scale)


def norm_back(grad, normal, scale, gain):
    scaled = grad * gain
    return scale * (
        scaled
        - jnp.mean(scaled, axis=-1, keepdims=True)
        - normal * jnp.mean(scaled * normal, axis=-1, keepdims=True)
    )


def dot(form, left, right):
    return jnp.einsum(form, left, right, preferred_element_type=F32)


def gelu(value):
    return jax.nn.gelu(value, approximate=False)


def gelu_slope(value):
    unused, pullback = jax.vjp(gelu, value)
    return pullback(jnp.ones_like(value))[0]


def split_heads(packed):
    parts = packed.reshape(packed.shape[:-1] + (3, HEADS, HEAD_DIM))
    return (parts[..., 0, :, :], parts[..., 1, :, :], parts[..., 2, :, :])


def ffn_forward(params, inputs, context_low):
    proj_weight, proj_bias, attn_gain, attn_bias = params[3:7]
    inner_weight, inner_bias, outer_weight, outer_bias, ffn_gain, ffn_bias = params[7:]
    attn_out = dot("...d,de->...e", context_low, proj_weight) + proj_bias
    first_normal, first_scale = row_norm(inputs.astype(F32) + attn_out)
    normed = first_normal * attn_gain + attn_bias
    inner_sum = dot("...d,di->...i", normed.astype(BF), inner_weight) + inner_bias
    act_low = gelu(inner_sum).astype(BF)
    outer_sum = dot("...i,id->...d", act_low, outer_weight) + outer_bias
    second_normal, second_scale = row_norm(normed + outer_sum)
    result = second_normal * ffn_gain + ffn_bias
    return (result, (first_normal, first_scale, inner_sum, act_low, second_normal, second_scale))


def ffn_backward(params, saved, grad_out):
    proj_weight, proj_bias, attn_gain, attn_bias = params[3:7]
    inner_weight, inner_bias, outer_weight, outer_bias, ffn_gain, ffn_bias = params[7:]
    first_normal, first_scale, inner_sum, act_low, second_normal, second_scale = saved
    second_grad = norm_back(grad_out, second_normal, second_scale, ffn_gain)
    outer_low = second_grad.astype(BF)
    act_grad = dot("...d,id->...i", outer_low, outer_weight)
    inner_low = (act_grad * gelu_slope(inner_sum)).astype(BF)
    normed_grad = second_grad + dot("...i,di->...d", inner_low, inner_weight)
    first_grad = norm_back(normed_grad, first_normal, first_scale, attn_gain)
    proj_low = first_grad.astype(BF)
    context_grad = dot("...e,de->...d", proj_low, proj_weight).astype(BF)
    rows = tuple(range(grad_out.ndim - 1))
    small = (
        jnp.sum(proj_low.astype(F32), axis=rows),
        jnp.sum(normed_grad * first_normal, axis=rows),
        jnp.sum(normed_grad, axis=rows),
        jnp.sum(inner_low.astype(F32), axis=rows),
        jnp.sum(outer_low.astype(F32), axis=rows),
        jnp.sum(grad_out * second_normal, axis=rows),
        jnp.sum(grad_out, axis=rows),
    )
    return (outer_low, inner_low, first_grad, proj_low, context_grad, small)


def local(embeddings, cotangent, lengths, *weights):
    params = tuple(piece[0] for piece in weights)
    qkv_weight, query_bias, value_bias, proj_weight, proj_bias, attn_gain, attn_bias = params[:7]
    encoder = lax.axis_index("section") == 0
    inputs = embeddings[0]
    batch, length, width = inputs.shape
    scale = HEAD_DIM ** (-0.5)
    key_mask = jnp.arange(length, dtype=jnp.int32)[None, :] < lengths[:, None]
    qkv_shift = jnp.concatenate([query_bias, jnp.zeros_like(query_bias), value_bias])

    def project(rows):
        return (dot("...d,de->...e", rows, qkv_weight) + qkv_shift).astype(BF)

    qkv_low = project(inputs)
    query_part, key_part, value_part = split_heads(qkv_low)
    first_scores = dot("bhe,bkhe->bhk", query_part[:, 0], key_part) * scale
    first_scores = jnp.where(key_mask[:, None, :], first_scores, BIG_NEG)
    first_probs = jax.nn.softmax(first_scores, axis=-1)
    first_context = dot("bhk,bkhe->bhe", first_probs.astype(BF), value_part)
    first_context = first_context.reshape(batch, width).astype(BF)
    first_result, first_saved = ffn_forward(params, inputs[:, 0], first_context)
    arrived = lax.ppermute(first_result.astype(BF), "section", [(0, 1)])

    first_rows = jnp.where(encoder, inputs[:, 0], arrived)
    inputs = inputs.at[:, 0].set(first_rows)
    qkv_low = qkv_low.at[:, 0].set(project(first_rows))
    query_part, key_part, value_part = split_heads(qkv_low)
    scores = dot("bqhe,bkhe->bhqk", query_part, key_part) * scale
    scores = jnp.where(key_mask[:, None, None, :], scores, BIG_NEG)
    attention = jax.nn.softmax(scores, axis=-1)
    context = dot("bhqk,bkhe->bqhe", attention.astype(BF), value_part)
    context_low = context.reshape(batch, length, width).astype(BF)
    result, saved = ffn_forward(params, inputs, context_low)

    grad_out = cotangent.astype(F32) * key_mask[..., None].astype(F32)
    outer_low, inner_low, first_grad, proj_low, context_grad, small = ffn_backward(
        params, saved, grad_out
    )
    normed_low = (saved[0] * attn_gain + attn_bias).astype(BF)
    outer_weight_grad = dot("bli,bld->id", saved[3], outer_low)
    inner_weight_grad = dot("bld,bli->di", normed_low, inner_low)
    proj_weight_grad = dot("bld,ble->de", context_low, proj_low)
    context_grad = context_grad.reshape(batch, length, HEADS, HEAD_DIM)
    prob_grad = dot("bqhe,bkhe->bhqk", context_grad, value_part)
    value_grad = dot("bhqk,bqhe->bkhe", attention.astype(BF), context_grad)
    score_low = (
        attention * (prob_grad - jnp.sum(attention * prob_grad, axis=-1, keepdims=True))
    ).astype(BF)
    query_grad = dot("bhqk,bkhe->bqhe", score_low, key_part) * scale
    key_grad = dot("bhqk,bqhe->bkhe", score_low, query_part) * scale
    packed_grad = jnp.stack([query_grad, key_grad, value_grad], axis=2)
    packed_grad = packed_grad.reshape(batch, length, 3 * width).astype(BF)
    packed_sums = jnp.sum(packed_grad.astype(F32), axis=(0, 1))
    qkv_weight_grad = dot("bld,ble->de", inputs, packed_grad)
    input_grad = dot("ble,de->bld", packed_grad, qkv_weight) + first_grad
    returned = lax.ppermute(input_grad[:, 0].astype(BF), "section", [(1, 0)])
    decoder_grads = tuple(
        lax.psum(piece.astype(BF), "dp").astype(F32)
        for piece in (outer_weight_grad, inner_weight_grad, proj_weight_grad, qkv_weight_grad)
    )
    small = (packed_sums[:width], packed_sums[2 * width :]) + small

    e_outer, e_inner, e_first, e_proj, e_context, e_small = ffn_backward(
        params, first_saved, returned.astype(F32)
    )
    e_context = e_context.reshape(batch, HEADS, HEAD_DIM)
    e_query = query_part[:, 0]
    e_prob_grad = dot("bhe,bkhe->bhk", e_context, value_part)
    e_score = (
        first_probs
        * (e_prob_grad - jnp.sum(first_probs * e_prob_grad, axis=-1, keepdims=True))
    ).astype(BF)
    e_probs = first_probs.astype(BF)
    e_query_grad = (dot("bhk,bkhe->bhe", e_score, key_part) * scale).astype(BF)
    e_query = e_query * jnp.asarray(scale, BF)
    key_sums = dot("bhk,bkd->bhd", e_score, inputs).astype(BF)
    value_sums = dot("bhk,bkd->bhd", e_probs, inputs).astype(BF)
    qkv_heads = qkv_weight.reshape(width, 3, HEADS, HEAD_DIM)
    key_back = dot("dhe,bhe->bhd", qkv_heads[:, 1], e_query)
    value_back = dot("dhe,bhe->bhd", qkv_heads[:, 2], e_context)
    e_input_grad = jnp.einsum(
        "bhk,bhd->bkd", e_score, key_back.astype(BF), preferred_element_type=F32
    ) + jnp.einsum("bhk,bhd->bkd", e_probs, value_back.astype(BF), preferred_element_type=F32)
    e_first_grad = e_first + dot("bhe,dhe->bd", e_query_grad, qkv_heads[:, 0])
    e_input_grad = e_input_grad.at[:, 0].add(e_first_grad)
    value_mass = jnp.sum(e_probs.astype(F32), axis=-1, keepdims=True)
    e_small = (
        jnp.sum(e_query_grad.astype(F32), axis=0).reshape(width),
        jnp.sum(e_context.astype(F32) * value_mass, axis=0).reshape(width),
    ) + e_small

    factors = (
        first_saved[3],
        e_outer,
        (first_saved[0] * attn_gain + attn_bias).astype(BF),
        e_inner,
        first_context,
        e_proj,
        inputs[:, 0],
        e_query_grad.reshape(batch, width),
        e_query.reshape(batch, width),
        e_context.reshape(batch, width),
        key_sums.reshape(batch, HEADS * width),
        value_sums.reshape(batch, HEADS * width),
    )
    own_small = jnp.where(encoder, jnp.concatenate(e_small), jnp.concatenate(small))
    payload = jnp.concatenate([piece.reshape(-1) for piece in factors] + [own_small.astype(BF)])
    gathered = lax.all_gather(payload, "dp")
    everyone = []
    place = 0
    for piece in factors:
        everyone.append(gathered[:, place : place + piece.size].reshape((-1,) + piece.shape[1:]))
        place += piece.size
    small_sum = jnp.sum(gathered[:, place:].astype(F32), axis=0)
    small_out = []
    place = 0
    for piece in small:
        small_out.append(small_sum[place : place + piece.size])
        place += piece.size

    def heads(piece):
        return piece.reshape(piece.shape[0], HEADS, -1)

    qkv_pieces = (
        dot("bd,be->de", everyone[6], everyone[7]),
        dot("bhd,bhe->dhe", heads(everyone[10]), heads(everyone[8])).reshape(width, width),
        dot("bhd,bhe->dhe", heads(everyone[11]), heads(everyone[9])).reshape(width, width),
    )
    encoder_grads = (
        dot("bi,bd->id", everyone[0], everyone[1]),
        dot("bd,bi->di", everyone[2], everyone[3]),
        dot("bd,be->de", everyone[4], everyone[5]),
        jnp.concatenate(qkv_pieces, axis=1),
    )
    outer_out, inner_out, proj_out, qkv_out = (
        jnp.where(encoder, first, second) for first, second in zip(encoder_grads, decoder_grads)
    )
    later = jnp.where(jnp.arange(length)[None, :, None] > 0, input_grad, 0.0)
    embed_grads = jnp.where(encoder, e_input_grad, later)
    outputs = (
        result.astype(BF),
        embed_grads,
        qkv_out,
        small_out[0],
        small_out[1],
        proj_out,
        small_out[2],
        small_out[3],
        small_out[4],
        inner_out,
        small_out[5],
        outer_out,
        small_out[6],
        small_out[7],
        small_out[8],
    )
    return tuple(piece[None] for piece in outputs)


def solution(mesh):
    matrix = P("section", None, None)
    vector = P("section", None)
    return jax.shard_map(
        local,
        mesh=mesh,
        in_specs=(P("section", "dp", None, None), P("dp", None, None), P("dp"))
        + (matrix, vector, vector, matrix, vector, vector, vector)
        + (matrix, vector, matrix, vector, vector, vector),
        out_specs=(P("section", "dp", None, None), P("section", "dp", None, None))
        + (matrix, vector, vector, matrix, vector, vector, vector)
        + (matrix, vector, matrix, vector, vector, vector),
        check_vma=False,
    )
```

time: 1320 us -> 817 us (0.62)
  matrix products: 444 us -> 226 us
  waiting for transfers between devices: 577 us -> 387 us
  blocking collectives: 84.4 us -> 0 us
    psum x1, waiting for transfers between devices: 576 us -> 370 us  [local(): lax.psum(piece.astype(BF), 'dp').astype(F32)]
    dot_general x66 -> x41, matrix products: 410 us -> 210 us  [the longest x39 209 us: dot(): return jnp.einsum(form, left, right, preferred_element_type=F32)]
    psum x1 -> x0, blocking collectives: 84.4 us -> none  [local(): gradients = lax.psum(attn_totals + ffn_totals, 'dp')]
    convert_element_type x3 -> x6, other arithmetic: 21.1 us -> 50.4 us  [the longest x1 31.8 us: ffn_forward(): act_low = gelu(inner_sum).astype(BF)]
    convert_element_type x13 -> x5, local copies, waits for them, and re-layouts: 34.6 us -> 11.5 us  [the longest x1 6.62 us: project(): return (dot('...d,de->...e', rows, qkv_weight) + qkv_shift).astype(BF)]
    sub x3 -> x1, matrix products: 34.5 us -> 15.7 us  [local(): attention = jax.nn.softmax(scores, axis=-1)]
    all_gather x0 -> x1, waiting for transfers between devices: none -> 16.6 us  [local(): gathered = lax.all_gather(payload, 'dp')]
    unnamed x364 -> x190, local copies, waits for them, and re-layouts: 48 us -> 42.9 us
  transfers between devices with their start and end apart: 5 -> 4, of which waited for: 3 -> 2; matrix products, arithmetic and copies ran while one was open for 6% -> 11% of each run, Pallas kernels for 0% -> 0%
where the time goes in v1:
time: 817 us; the launch traced here: 810 us
  waiting for transfers between devices  387 us (47%)
  matrix products  226 us (28%)
  local copies, waits for them, and re-layouts  103 us (13%)
  other arithmetic  74.3 us (9%)
  between operations  15.7 us (2%)
    psum x1, waiting for transfers between devices, local(): lax.psum(piece.astype(BF), 'dp').astype(F32)  370 us
    dot_general x39, matrix products, dot(): return jnp.einsum(form, left, right, preferred_element_type=F32)  209 us
    unnamed x190, local copies, waits for them, and re-layouts  42.9 us
    convert_element_type x1, other arithmetic, ffn_forward(): act_low = gelu(inner_sum).astype(BF)  31.8 us
    convert_element_type x1, other arithmetic, local(): score_low = (attention * (prob_grad - jnp.sum(attention * prob_grad, axis...  17 us
    all_gather x1, waiting for transfers between devices, local(): gathered = lax.all_gather(payload, 'dp')  16.6 us
  transfers between devices with their start and end apart: 4, of which 2 were waited for; matrix products, arithmetic and copies ran while one was open for 11% of the time, Pallas kernels for 0%

profile of v1, /device:TPU:0, one launch (start us, length us, event | category | flops | bytes accessed | tf_op | source)
XLA Modules:
  0.0 809.9 jit_solution(14009815803308834047)
XLA Ops:
  10.5 7.5 add_convert_fusion
  17.9 6.6 copy.218
  36.0 3.3 fusion.186
  50.0 6.6 copy.222
  56.7 15.7 %fusion.187 = (f32[2,12,512]{2,1,0:T(8,128)S(1)}, f32[2,12,512,512]{2,3,1,0:T(8,128)}) fusion(pred[2,512]{1,0:T(4,128)(4,1)S(1)} %get-tuple-element.196, bf16[2,512,3,12,64]{1,4,3,2,0:T(8,128)(2,1)} %bitcast.300), kind=kOutput, calls=%fused_computation.293 | convolution fusion | flops 830472704 | bytes 28361728 | tf_op jit(solution)/shard_map/sub | solution.py:117
  72.4 10.9 %fusion.74 = bf16[2,12,64,512]{3,2,1,0:T(8,128)(2,1)S(1)} fusion(bf16[2,512,3,12,64]{1,4,3,2,0:T(8,128)(2,1)} %bitcast.301, f32[2,12,512,512]{2,3,1,0:T(8,128)} %get-tuple-element.204, f32[2,12,512]{2,1,0:T(8,128)S(1)} %get-tuple-element.203), kind=kOutput, calls=%fused_computation.107 | convolution fusion | flops 818675712 | bytes 28360704 | tf_op jit(solution)/shard_map/bhqk,bkhe->bqhe/dot_general | solution.py:32
  87.3 14.6 %fusion.61 = (u8[512,3072]{1,0:T(8,128)(4,1)S(1)}, u8[512,3072]{1,0:T(8,128)(4,1)S(1)}, f32[2,512,3072]{2,1,0:T(8,128)}) fusion(f32[3072]{0:T(1024)S(1)} %bitcast.337, bf16[1,768,3072]{2,1,0:T(8,128)(2,1)S(1)} %bitcast.311, f32[2,512,768]{2,1,0:T(8,128)} %copy-done.5, f32[768]{0:T(1024)S(1)} %reduce.12, f32[768]{0:T(1024)S(1)} %reduce.11, ...), kind=kOutput, calls=%fused_computation.96 | convolution fusion | flops 4876664832 | bytes 23619584 | tf_op jit(solution)/shard_map/...d,di->...i/dot_general | solution.py:32
  101.9 31.8 %multiply_convert_fusion.2 = (bf16[2,512,3072]{2,1,0:T(8,128)(2,1)S(1)}, f32[2,512,3072]{2,1,0:T(8,128)}) fusion(f32[2,512,3072]{2,1,0:T(8,128)} %get-tuple-element.207, f32[3072]{0:T(1024)S(1)} %bitcast.338, u8[512,3072]{1,0:T(8,128)(4,1)S(1)} %get-tuple-element.127, u8[512,3072]{1,0:T(8,128)(4,1)S(1)} %get-tuple-element.126), kind=kLoop, calls=%fused_computation.16 | loop fusion | flops 223346688 | bytes 34615296 | tf_op jit(solution)/shard_map/convert_element_type | solution.py:56
  133.7 5.4 fusion.189
  145.4 17.2 %convert_reduce_fusion = (f32[3072]{0:T(1024)S(1)}, bf16[2,512,3072]{2,1,0:T(8,128)(2,1)}) fusion(f32[2,512,3072]{2,1,0:T(8,128)} %get-tuple-element.165, f32[2,512,3072]{2,1,0:T(8,128)} %get-tuple-element.207, f32[3072]{0:T(1024)S(1)} %bitcast.339, bf16[2,512,768]{2,1,0:T(8,128)(2,1)} %get-tuple-element.149, bf16[1,3072,768]{2,1,0:T(8,128)(2,1)} %param.34), kind=kOutput, calls=%fused_computation.14 | convolution fusion | flops 4879021056 | bytes 37773312 | tf_op jit(solution)/shard_map/...d,id->...i/dot_general | solution.py:32
  162.7 10.7 %multiply_reduce_fusion.2 = (f32[768]{0:T(1024)S(1)}, f32[2,512]{1,0:T(2,128)S(1)}, f32[2,512]{1,0:T(2,128)S(1)}, f32[768]{0:T(1024)S(1)}, f32[2,512,768]{2,1,0:T(8,128)S(1)}) fusion(f32[2,512,768]{2,1,0:T(8,128)} %copy-done.5, f32[2,512]{1,0:T(2,128)S(1)} %add_rsqrt_fusion.1, f32[2,512]{1,0:T(2,128)S(1)} %broadcast_multiply_fusion.5, f32[768]{0:T(1024)S(1)} %reduce.11, ...), kind=kOutput, calls=%fused_computation.76 | convolution fusion | flops 4846776320 | bytes 22069248 | tf_op jit(solution)/shard_map/...i,di->...d/dot_general | solution.py:32
  180.6 16.8 %multiply_reduce_fusion = (f32[2,12,512]{2,1,0:T(8,128)S(1)}, f32[2,12,512,512]{2,3,1,0:T(8,128)}) fusion(f32[2,12,512,512]{2,3,1,0:T(8,128)} %get-tuple-element.204, f32[2,12,512]{2,1,0:T(8,128)S(1)} %get-tuple-element.203, bf16[2,512,12,64]{1,3,2,0:T(8,128)(2,1)S(1)} %bitcast.328, bf16[2,512,3,12,64]{1,4,3,2,0:T(8,128)(2,1)} %bitcast.302), kind=kOutput, calls=%fused_computation.3 | convolution fusion | flops 824168448 | bytes 53575680 | tf_op jit(solution)/shard_map/bqhe,bkhe->bhqk/dot_general | solution.py:32
  197.4 17.0 %multiply_convert_fusion = bf16[2,12,512,512]{2,3,1,0:T(8,128)(2,1)S(1)} fusion(f32[2,12,512,512]{2,3,1,0:T(8,128)} %get-tuple-element.212, f32[2,12,512]{2,1,0:T(8,128)S(1)} %get-tuple-element.211, f32[2,12,512,512]{2,3,1,0:T(8,128)} %get-tuple-element.204, f32[2,12,512]{2,1,0:T(8,128)S(1)} %get-tuple-element.203), kind=kLoop, calls=%fused_computation.2 | loop fusion | flops 25165824 | bytes 63012864 | tf_op jit(solution)/shard_map/convert_element_type | solution.py:135
  214.4 4.6 copy-done.1
  219.0 4.7 multiply_bitcast_fusion.1
  223.7 10.1 %multiply_bitcast_fusion = bf16[2,512,1,12,64]{1,4,3,0,2:T(8,128)(2,1)} fusion(bf16[2,12,512,512]{2,3,1,0:T(8,128)(2,1)} %copy-done.1, bf16[2,512,3,12,64]{1,4,3,2,0:T(8,128)(2,1)} %bitcast.304), kind=kOutput, calls=%fused_computation.79 | convolution fusion | flops 806879232 | bytes 15728640 | tf_op jit(solution)/shard_map/bhqk,bqhe->bkhe/dot_general | solution.py:32
  233.8 11.6 %fusion.63 = bf16[2,512,1,12,64]{1,4,3,0,2:T(8,128)(2,1)} fusion(bf16[2,512,12,64]{1,3,2,0:T(8,128)(2,1)S(1)} %bitcast.329, f32[2,12,512,512]{2,3,1,0:T(8,128)} %get-tuple-element.204, f32[2,12,512]{2,1,0:T(8,128)S(1)} %get-tuple-element.203), kind=kOutput, calls=%fused_computation.103 | convolution fusion | flops 817889280 | bytes 28360704 | tf_op jit(solution)/shard_map/bhqk,bqhe->bkhe/dot_general | solution.py:32
  245.4 4.4 bitcast_convert_fusion.3
  256.7 10.0 %fusion.71 = f32[2,512,768]{2,1,0:T(8,128)S(1)} fusion(bf16[2,512,2304]{1,2,0:T(8,128)(2,1)} %bitcast.326, bf16[1,768,2304]{2,1,0:T(8,128)(2,1)} %param.25, f32[2,512]{1,0:T(2,128)S(1)} %broadcast_multiply_fusion, f32[2,512,768]{2,1,0:T(8,128)} %copy-done.5, f32[2,512]{1,0:T(2,128)S(1)} %broadcast_multiply_fusion.5, ...), kind=kOutput, calls=%fused_computation.106 | convolution fusion | flops 3630170112 | bytes 17714176 | tf_op jit(solution)/shard_map/ble,de->bld/dot_general | solution.py:32
  273.8 3.7 convert_reduce_fusion.6
  278.1 4.3 multiply_reduce_fusion.8
  305.0 9.3 %bitcast_convert_fusion.2 = bf16[768,2304]{0,1:T(8,128)(2,1)} fusion(bf16[2,512,2304]{1,2,0:T(8,128)(2,1)} %bitcast.327, bf16[2,512,768]{2,0,1:T(2,128)(2,1)S(1)} %copy-done.3), kind=kOutput, calls=%fused_computation.42 | convolution fusion | flops 3625648128 | bytes 9830400 | tf_op jit(solution)/shard_map/bld,ble->de/dot_general | solution.py:32
  314.3 10.1 %bitcast_convert_fusion.1 = bf16[768,3072]{1,0:T(8,128)(2,1)} fusion(bf16[2,512,3072]{2,1,0:T(8,128)(2,1)} %get-tuple-element.219, f32[2,512,768]{2,1,0:T(8,128)S(1)} %copy-done.8, f32[768]{0:T(1024)S(1)} %copy-done.45, f32[768]{0:T(1024)S(1)} %reduce.11, f32[2,512]{1,0:T(2,128)S(1)} %copy-done.55, f32[2,512]{1,0:T(2,128)S(1)} %broadcast_multiply_fusion.5), kind=kOutput, calls=%fused_computation.35 | convolution fusion | flops 4838129664 | bytes 14170112 | tf_op jit(solution)/shard_map/bld,bli->di/dot_general | solution.py:32
  324.4 9.7 %bitcast_convert_fusion = bf16[3072,768]{1,0:T(8,128)(2,1)} fusion(bf16[2,512,3072]{2,1,0:T(8,128)(2,1)} %copy-done.9, bf16[2,512,768]{2,1,0:T(8,128)(2,1)S(1)} %copy-done.18), kind=kOutput, calls=%fused_computation.34 | convolution fusion | flops 4834197504 | bytes 12582912 | tf_op jit(solution)/shard_map/bli,bld->id/dot_general | solution.py:32
  334.1 5.8 copy.236
  349.2 4.9 select_bitcast_fusion.2
  354.1 16.6 %all-gather.3.cloned.1.call-done = bf16[1130496]{0:T(1024)(128)(2,1)} async-done(((bf16[70656]{0:T(1024)(128)(2,1)}), bf16[1130496]{0:T(1024)(128)(2,1)}) %all-gather.3.cloned.1.call-update) | async-done | bytes 2261008 | tf_op jit(solution)/shard_map/all_gather | solution.py:195
  404.0 370.1 %all-reduce.3.cloned.1.call-done = (bf16[768,2304]{0,1:T(8,128)(2,1)}, bf16[768,768]{1,0:T(8,128)(2,1)}, bf16[768,3072]{1,0:T(8,128)(2,1)}, bf16[3072,768]{1,0:T(8,128)(2,1)}) async-done(((bf16[768,2304]{0,1:T(8,128)(2,1)}, bf16[768,768]{1,0:T(8,128)(2,1)}, bf16[768,3072]{1,0:T(8,128)(2,1)}, bf16[3072,768]{1,0:T(8,128)(2,1)}), (bf16[768,2304]{0,1:T(8,128)(2,1)}, bf16[768,768]{1,0:T(8,128)(2,1)}, ...) | async-done | bytes 14155792 | tf_op jit(solution)/shard_map/psum | solution.py:145
  774.1 5.5 fusion.12
  779.7 8.0 copy.252
  787.8 7.7 select_bitcast_fusion
  795.5 5.2 select_bitcast_fusion.1
  (332 shorter events, 123.7 us)
Async XLA Ops:
  7.2 24.9 %copy-start = (bf16[1,768,768]{2,1,0:T(8,128)(2,1)S(1)}, bf16[1,768,768]{2,1,0:T(8,128)(2,1)}, u32[]{:S(2)}) copy-start(bf16[1,768,768]{2,1,0:T(8,128)(2,1)} %param.28) | copy-start | bytes 3538948
  7.2 363.5 %all-gather.3.cloned.1.call-start = ((), (), s32[]{:S(2)}) async-start(), calls=%async_computation | async-start | bytes 2402304 | tf_op jit(solution)/shard_map/all_gather | solution.py:195
  32.8 100.9 %copy-start.44 = (f32[768]{0:T(1024)}, f32[768]{0:T(1024)S(1)}, u32[]{:S(2)}) copy-start(f32[768]{0:T(1024)S(1)} %reduce.12) | copy-start | bytes 9220
  36.0 12.3 %copy-start.26 = (f32[2,3072]{1,0:T(2,128)}, f32[2,3072]{1,0:T(2,128)S(1)}, u32[]{:S(2)}) copy-start(f32[2,3072]{1,0:T(2,128)S(1)} %fusion.48) | copy-start | bytes 73732
  40.3 5.4 collective-permute-start
  45.7 11.0 %copy-start.42 = (bf16[2,768]{1,0:T(2,128)(2,1)}, bf16[2,768]{1,0:T(2,128)(2,1)S(1)}, u32[]{:S(2)}) copy-start(bf16[2,768]{1,0:T(2,128)(2,1)S(1)} %broadcast_select_fusion) | copy-start | bytes 9220
  48.3 35.1 %copy-start.2 = (bf16[2,512,768]{2,0,1:T(2,128)(2,1)}, bf16[2,512,768]{2,0,1:T(2,128)(2,1)S(1)}, u32[]{:S(2)}) copy-start(bf16[2,512,768]{2,0,1:T(2,128)(2,1)S(1)} %bitcast_dynamic-update-slice_fusion) | copy-start | bytes 4718596
  83.4 50.3 %slice-start = ((s8[4718592]{0:T(1024)(128)(4,1)}), s8[4194304]{0:T(1024)(128)(4,1)S(1)}, s32[]{:S(2)}) async-start(s8[4718592]{0:T(1024)(128)(4,1)} %bitcast.308), calls=%async_computation.2 | async-start | bytes 8388608
  87.2 169.4 %copy-start.54 = (f32[2,512]{1,0:T(2,128)}, f32[2,512]{1,0:T(2,128)S(1)}, u32[]{:S(2)}) copy-start(f32[2,512]{1,0:T(2,128)S(1)} %add_rsqrt_fusion.1) | copy-start | bytes 12292
  87.3 46.4 %slice-start.1 = ((s8[4718592]{0:T(1024)(128)(4,1)}), s8[524288]{0:T(1024)(128)(4,1)S(1)}, s32[]{:S(2)}) async-start(s8[4718592]{0:T(1024)(128)(4,1)} %bitcast.308), calls=%async_computation.3 | async-start | bytes 1048576
  101.9 31.8 %copy-start.6 = (f32[2,512,768]{2,1,0:T(8,128)S(1)}, f32[2,512,768]{2,1,0:T(8,128)}, u32[]{:S(2)}) copy-start(f32[2,512,768]{2,1,0:T(8,128)} %copy-done.5) | copy-start | bytes 9437188
  162.7 10.8 %copy-start.7 = (f32[2,512,768]{2,1,0:T(8,128)S(1)}, f32[2,512,768]{2,1,0:T(8,128)}, u32[]{:S(2)}) copy-start(f32[2,512,768]{2,1,0:T(8,128)} %copy-done.5) | copy-start | bytes 9437188
  256.7 14.3 %copy-start.47 = (f32[9216]{0:T(1024)S(1)}, f32[9216]{0:T(1024)}, u32[]{:S(2)}) copy-start(f32[9216]{0:T(1024)} %custom-call.1) | copy-start | bytes 110596
  256.7 14.4 %copy-start.43 = (bf16[2,768]{1,0:T(2,128)(2,1)S(1)}, bf16[2,768]{1,0:T(2,128)(2,1)}, u32[]{:S(2)}) copy-start(bf16[2,768]{1,0:T(2,128)(2,1)} %copy-done.42) | copy-start | bytes 9220
  256.7 15.8 %copy-start.40 = (f32[2,768]{1,0:T(2,128)S(1)}, f32[2,768]{1,0:T(2,128)}, u32[]{:S(2)}) copy-start(f32[2,768]{1,0:T(2,128)} %get-tuple-element.167) | copy-start | bytes 18436
  256.7 16.4 %copy-start.69 = (f32[2]{0:T(128)S(1)}, f32[2]{0:T(128)}, u32[]{:S(2)}) copy-start(f32[2]{0:T(128)} %copy-done.68) | copy-start | bytes 28
  256.7 17.1 %copy-start.27 = (f32[2,3072]{1,0:T(2,128)S(1)}, f32[2,3072]{1,0:T(2,128)}, u32[]{:S(2)}) copy-start(f32[2,3072]{1,0:T(2,128)} %copy-done.26) | copy-start | bytes 73732
  268.4 9.7 %copy-start.39 = (f32[2,768]{1,0:T(2,128)S(1)}, f32[2,768]{1,0:T(2,128)}, u32[]{:S(2)}) copy-start(f32[2,768]{1,0:T(2,128)} %copy-done.38) | copy-start | bytes 18436
  268.4 4.1 collective-permute-start.1
  278.1 9.7 %copy-start.22 = (f32[2,12,512]{2,1,0:T(8,128)S(1)}, f32[2,12,512]{2,1,0:T(8,128)}, u32[]{:S(2)}) copy-start(f32[2,12,512]{2,1,0:T(8,128)} %copy-done.21) | copy-start | bytes 147460
  278.1 9.7 %copy-start.53 = (f32[2,12]{1,0:T(2,128)S(1)}, f32[2,12]{1,0:T(2,128)}, u32[]{:S(2)}) copy-start(f32[2,12]{1,0:T(2,128)} %copy-done.52) | copy-start | bytes 292
  284.3 8.1 copy-start.46
  284.3 12.9 %copy-start.36 = (bf16[70656]{0:T(1024)(128)(2,1)S(1)}, bf16[70656]{0:T(1024)(128)(2,1)}, u32[]{:S(2)}) copy-start(bf16[70656]{0:T(1024)(128)(2,1)} %constant_dynamic-update-slice_fusion.2) | copy-start | bytes 423940
  304.9 9.4 %copy-start.45 = (f32[768]{0:T(1024)S(1)}, f32[768]{0:T(1024)}, u32[]{:S(2)}) copy-start(f32[768]{0:T(1024)} %copy-done.44) | copy-start | bytes 9220
  304.9 9.3 %copy-start.55 = (f32[2,512]{1,0:T(2,128)S(1)}, f32[2,512]{1,0:T(2,128)}, u32[]{:S(2)}) copy-start(f32[2,512]{1,0:T(2,128)} %copy-done.54) | copy-start | bytes 12292
  304.9 469.2 %all-reduce.3.cloned.1.call-start = ((), (), s32[]{:S(2)}) async-start(), calls=%async_computation.1 | async-start | bytes 28311552 | tf_op jit(solution)/shard_map/psum | solution.py:145
  304.9 9.3 %copy-start.8 = (f32[2,512,768]{2,1,0:T(8,128)S(1)}, f32[2,512,768]{2,1,0:T(8,128)}, u32[]{:S(2)}) copy-start(f32[2,512,768]{2,1,0:T(8,128)} %copy-done.5) | copy-start | bytes 9437188
  314.2 10.1 %copy-start.18 = (bf16[2,512,768]{2,1,0:T(8,128)(2,1)S(1)}, bf16[2,512,768]{2,1,0:T(8,128)(2,1)}, u32[]{:S(2)}) copy-start(bf16[2,512,768]{2,1,0:T(8,128)(2,1)} %get-tuple-element.149) | copy-start | bytes 4718596
  392.5 9.6 %copy-start.16 = (bf16[32,12,768]{2,1,0:T(8,128)(2,1)S(1)}, bf16[32,12,768]{2,1,0:T(8,128)(2,1)}, u32[]{:S(2)}) copy-start(bf16[32,12,768]{2,1,0:T(8,128)(2,1)} %reshape_reshape.28) | copy-start | bytes 1769476
  392.5 9.6 %copy-start.25 = (bf16[32,12,64]{2,1,0:T(8,128)(2,1)S(1)}, bf16[32,12,64]{2,1,0:T(8,128)(2,1)}, u32[]{:S(2)}) copy-start(bf16[32,12,64]{2,1,0:T(8,128)(2,1)} %reshape_reshape.27) | copy-start | bytes 147460
  779.7 8.1 copy-start.33
  779.7 15.7 %slice-start.4 = ((s8[4718592]{0:T(1024)(128)(4,1)}), s8[524288]{0:T(1024)(128)(4,1)S(1)}, s32[]{:S(2)}) async-start(s8[4718592]{0:T(1024)(128)(4,1)} %bitcast.319), calls=%async_computation.6 | async-start | bytes 1048576
  (50 other events, 219.5 us)
Sparse Core Ops, SparseCore 0:
  305.0 65.6 all-gather.2
  378.3 395.8 all-reduce.2

commit v2 on v1

v2 whole, which is shorter than its diff:
```python
import math

import jax
import jax.numpy as jnp
from jax import lax
from jax.experimental import pallas as pl
from jax.experimental.pallas import tpu as pltpu
from jax.sharding import PartitionSpec as P

HEADS = 12
HEAD_DIM = 64
PAIR = 2 * HEAD_DIM
EPSILON = 1e-06
BIG_NEG = -1e30
BF = jnp.bfloat16
F32 = jnp.float32
CHUNK = 768
STRIP = 512
GROUP = 16
ROW_TILE = 16
ORDERS = (((1, 4, 2, 8), (2, 8, 1, 4)), ((1, 2, 8, 4), (2, 1, 4, 8)), ((4, 1, 2, 8), (8, 2, 1, 4)))
SWAP = ((0, 1), (1, 0))
KEY_SUMS, VALUE_SUMS, VECTORS, ACTS, INNERS, SMALLS, PAYLOAD = 0, 32, 64, 80, 88, 96, 112
V_OUTER, V_NORMED, V_CONTEXT, V_PROJ, V_INPUT, V_GQUERY, V_QUERY, V_GCONTEXT = range(8)


def params_of(mebibytes):
    return pltpu.CompilerParams(vmem_limit_bytes=mebibytes * 1024 * 1024)


def cost(micros):
    return pl.CostEstimate(flops=int(micros * 1.1e9), bytes_accessed=int(micros * 2e6), transcendentals=0)


def nn(left, right):
    return lax.dot_general(left, right, (((1,), (0,)), ((), ())), preferred_element_type=F32)


def nt(left, right):
    return lax.dot_general(left, right, (((1,), (1,)), ((), ())), preferred_element_type=F32)


def tn(left, right):
    return lax.dot_general(left, right, (((0,), (0,)), ((), ())), preferred_element_type=F32)


def turned(value):
    return jnp.transpose(value.astype(F32)).astype(BF)


def col_sum(value):
    return jnp.sum(value.astype(F32), axis=0, keepdims=True)


def row_norm(hidden):
    centred = hidden - jnp.mean(hidden, axis=-1, keepdims=True)
    scale = lax.rsqrt(jnp.mean(centred * centred, axis=-1, keepdims=True) + EPSILON)
    return (centred * scale, scale)


def norm_back(grad, normal, scale, gain):
    scaled = grad * gain
    return scale * (
        scaled
        - jnp.mean(scaled, axis=-1, keepdims=True)
        - normal * jnp.mean(scaled * normal, axis=-1, keepdims=True)
    )


def gelu_pair(value):
    bell = jnp.exp(-0.5 * (value * value))
    t = 1.0 / (1.0 + (0.3275911 / math.sqrt(2.0)) * jnp.abs(value))
    series = 0.5307027145 * t - 0.7265760135
    series = series * t + 0.7107068705
    series = series * t - 0.142248368
    series = series * t + 0.127414796
    tail = (series * t) * bell
    mass = jnp.where(value >= 0.0, 1.0 - tail, tail)
    return (value * mass, mass + value * (bell * (1.0 / math.sqrt(2.0 * math.pi))))


def fetch(first, own, other, target, sem):
    @pl.when(first)
    def _():
        pltpu.make_async_copy(own, target, sem).start()

    @pl.when(jnp.logical_not(first))
    def _():
        pltpu.make_async_copy(other, target, sem).start()


def landed(own, target, sem):
    pltpu.make_async_copy(own, target, sem).wait()


FAR = pl.BlockSpec(memory_space=pltpu.HBM)
SCALARS = pl.BlockSpec(memory_space=pltpu.SMEM)
NEAR = pl.BlockSpec(memory_space=pltpu.VMEM)


def struct(shape, kind):
    return jax.ShapeDtypeStruct(tuple(shape), kind)


def near(shape, kind):
    return pltpu.VMEM(tuple(shape), kind)


def full(shape):
    return pl.BlockSpec(tuple(shape), lambda *_: (0,) * len(shape))


def far(*values):
    return tuple(pltpu.with_memory_space_constraint(value, pltpu.HBM) for value in values)


def stay(*values):
    return tuple(pltpu.with_memory_space_constraint(value, pltpu.VMEM) for value in values)


QUERY_B, VALUE_B, PROJ_B, ATTN_G, ATTN_B, INNER_B, OUTER_B, FFN_G, FFN_B = range(9)
TABLE_ROWS = (0, 1, 2, 3, 4, 5, 9, 10, 11)


def layer_vectors(mine, other, own):
    def pick(k, part=0):
        row = TABLE_ROWS[k] + part
        return jnp.where(own, mine[row : row + 1, :], other[row : row + 1, :])

    return pick


def qkv_kernel(info_ref, x_ref, w_ref, *refs):
    vectors = refs[:9]
    qb_ref, vb_ref = vectors[QUERY_B], vectors[VALUE_B]
    own_ref, other_ref, table_ref = refs[9:]
    step = pl.program_id(0)
    half = pl.num_programs(0) // 2
    width = x_ref.shape[2]
    x = x_ref[0]

    def put(ref):
        for k, shift in enumerate((qb_ref[...], None, vb_ref[...])):
            made = nn(x, w_ref[:, k * width : (k + 1) * width])
            ref[:, k * width : (k + 1) * width] = (made if shift is None else made + shift).astype(BF)
        ref[:, 3 * width :] = x

    pl.when(step < half)(lambda: put(other_ref))
    pl.when(step >= half)(lambda: put(own_ref))

    @pl.when(step == 0)
    def _():
        for ref, row in zip(vectors, TABLE_ROWS):
            for part in range(ref.shape[1] // width):
                table_ref[row + part : row + part + 1, :] = ref[:, part * width : (part + 1) * width]


def qkv_call(info, inputs, weight, vectors, rows=256):
    count, length, width = inputs.shape
    wide = weight.shape[1] + width
    half = length // rows
    return pl.pallas_call(
        qkv_kernel,
        grid_spec=pltpu.PrefetchScalarGridSpec(
            num_scalar_prefetch=1,
            grid=(2 * half,),
            in_specs=[
                pl.BlockSpec(
                    (1, rows, width),
                    lambda i, info: (jnp.where(i < half, 1 - info[0], info[0]), lax.rem(i, half), 0),
                ),
                pl.BlockSpec(weight.shape, lambda i, info: (0, 0), pipeline_mode=pl.Buffered(1)),
            ]
            + [full(v.shape) for v in vectors],
            out_specs=[
                pl.BlockSpec((rows, wide), lambda i, info: (jnp.maximum(i - half, 0), 0)),
                pl.BlockSpec((rows, wide), lambda i, info: (jnp.minimum(i, half - 1), 0)),
                full((ROW_TILE, width)),
            ],
        ),
        out_shape=[struct((length, wide), BF)] * 2 + [struct((ROW_TILE, width), F32)],
        compiler_params=params_of(16),
        cost_estimate=cost(6),
        name="qkv",
    )(info, *far(inputs, weight, *vectors))


def by_head(value, rows):
    width = value.shape[1]
    lane = lax.broadcasted_iota(jnp.int32, (rows, width), 1)
    row = lax.broadcasted_iota(jnp.int32, (rows, width), 0)
    return jnp.where((lane >= row * HEAD_DIM) & (lane < (row + 1) * HEAD_DIM), value, jnp.zeros((), value.dtype))


def heads_of(value):
    rows, width = value.shape
    lane = lax.broadcasted_iota(jnp.int32, (rows, width), 1)
    row = lax.broadcasted_iota(jnp.int32, (rows, width), 0)
    kept = jnp.where((lane >= row * HEAD_DIM) & (lane < (row + 1) * HEAD_DIM), value, 0.0)
    return jnp.sum(kept, axis=0, keepdims=True)


def two_rows(first, second):
    rows = lax.broadcasted_iota(jnp.int32, (ROW_TILE, first.shape[1]), 0)
    zero = jnp.zeros((), first.dtype)
    return jnp.where(rows == 0, first, jnp.where(rows == 1, second, zero))


def head_kernel(
    info_ref, own_ref, other_ref, wp_ref, wi_ref, wo_ref, table,
    e_ref, probs_ref, c_ref, n1_ref, r1_ref, a_ref, slope_ref, n2_ref, r2_ref,
    wp, wi, wo, sems,
):
    copies = [
        pltpu.make_async_copy(wp_ref, wp, sems.at[0]),
        pltpu.make_async_copy(wi_ref, wi, sems.at[1]),
        pltpu.make_async_copy(wo_ref, wo, sems.at[2]),
    ]
    for copy in copies:
        copy.start()
    pick = layer_vectors(table, table, info_ref[0] == 0)
    width, ff = wi.shape
    length = own_ref.shape[0]
    lane = lax.broadcasted_iota(jnp.int32, (ROW_TILE, length), 1)
    contexts = []
    for i, ref in enumerate((own_ref, other_ref)):
        query = by_head(ref[0:1, 0:width] * jnp.asarray(0.125, BF), ROW_TILE)
        scores = nt(query, ref[:, width : 2 * width])
        scores = jnp.where(lane < info_ref[1 + i], scores, BIG_NEG)
        raised = jnp.exp(scores - jnp.max(scores, axis=-1, keepdims=True))
        probs = raised / jnp.sum(raised, axis=-1, keepdims=True)
        probs_ref[i] = probs
        contexts.append(heads_of(nn(probs.astype(BF), ref[:, 2 * width : 3 * width])))
    context = two_rows(*contexts).astype(BF)
    c_ref[...] = context
    inputs = two_rows(own_ref[0:1, 3 * width :], other_ref[0:1, 3 * width :])
    copies[0].wait()
    n1, r1 = row_norm(inputs.astype(F32) + (nn(context, wp[...]) + pick(PROJ_B)))
    n1_ref[...] = n1
    r1_ref[...] = r1
    normed = n1 * pick(ATTN_G) + pick(ATTN_B)
    copies[1].wait()
    low = normed.astype(BF)
    for c in range(ff // width):
        cols = slice(c * width, (c + 1) * width)
        act, slope = gelu_pair(nn(low, wi[:, cols]) + pick(INNER_B, c))
        a_ref[:, cols] = act.astype(BF)
        slope_ref[:, cols] = slope
    copies[2].wait()
    n2, r2 = row_norm(normed + (nn(a_ref[...], wo[...]) + pick(OUTER_B)))
    n2_ref[...] = n2
    r2_ref[...] = r2
    e_ref[...] = (n2 * pick(FFN_G) + pick(FFN_B)).astype(BF)


def head_call(info, own, other, wp, wi, wo, table):
    length = own.shape[0]
    width, ff = wi.shape
    shapes = [
        struct((ROW_TILE, width), BF),
        struct((2, ROW_TILE, length), F32),
        struct((ROW_TILE, width), BF),
        struct((ROW_TILE, width), F32),
        struct((ROW_TILE, 1), F32),
        struct((ROW_TILE, ff), BF),
        struct((ROW_TILE, ff), F32),
        struct((ROW_TILE, width), F32),
        struct((ROW_TILE, 1), F32),
    ]
    return pl.pallas_call(
        head_kernel,
        in_specs=[SCALARS, NEAR, NEAR, FAR, FAR, FAR, NEAR],
        out_specs=[NEAR] * len(shapes),
        out_shape=shapes,
        scratch_shapes=[pltpu.VMEM(w.shape, BF) for w in (wp, wi, wo)] + [pltpu.SemaphoreType.DMA((3,))],
        compiler_params=params_of(24),
        cost_estimate=cost(7),
        name="head_rows",
    )(info, own, other, *far(wp, wi, wo), table)


def attention_parts(xq, j, width, lane, bias_col):
    base = pl.multiple_of(j * PAIR, PAIR)
    q = xq[:, pl.ds(base, PAIR)] * jnp.asarray(0.125, BF)
    k = xq[:, pl.ds(base + width, PAIR)]
    v = xq[:, pl.ds(base + 2 * width, PAIR)]
    zero = jnp.zeros_like(k)
    parts = []
    for h in range(2):
        mine = (lane >= HEAD_DIM * h) & (lane < HEAD_DIM * (h + 1))
        spare = lane == HEAD_DIM * (1 - h)
        qh = jnp.where(mine, q, jnp.where(spare, jnp.ones_like(q), zero))
        kh = jnp.where(mine, k, jnp.where(spare, bias_col, zero))
        parts.append((mine, qh, kh))
    return base, q, k, v, parts


def place_rows(ref, value, order):
    pieces, rows = ref.shape[0], ref.shape[1]
    for p in range(pieces):
        ref[jnp.bitwise_xor(p, order)] = value[p * rows : (p + 1) * rows, :]


def forward_kernel(train, info_ref, *refs):
    xq_a, xq_b, wq_a, wq_b, wp_a, wp_b, wi_a, wi_b, wo_a, wo_b, mine, table = refs[:12]
    if train:
        head_ref, arrived_ref, cot_ref = refs[12:15]
        (z_ref, xq, wp, wi, wo, ctx, lse_ref, n1_ref, r1_ref, slope_ref, gf_ref, sg_ref, small_ref, keep_ref, send_ref) = refs[15:30]
        wq, lse_scr, acts, cot, sems = refs[30:]
    else:
        z_ref, xq, wp, wi, wo, ctx, sems = refs[12:]
    section = info_ref[0]
    own = section == (1 if train else 0)
    fetch(own, xq_a, xq_b, xq, sems.at[0])
    if train:
        fetch(own, wq_a, wq_b, wq, sems.at[1])
        pltpu.make_async_copy(cot_ref.at[section], cot, sems.at[5]).start()
    fetch(own, wp_a, wp_b, wp, sems.at[2])
    width = wp.shape[0]
    length = xq.shape[0]
    ff = wi.shape[1]
    pick = layer_vectors(mine, table, own)
    count = info_ref[1]
    row = lax.broadcasted_iota(jnp.int32, (length, PAIR), 0)
    lane = lax.broadcasted_iota(jnp.int32, (length, PAIR), 1)
    bias_col = jnp.where(row < count, 0.0, BIG_NEG).astype(BF)
    if train:
        first = jnp.where(section == 0, head_ref[0:1, :], arrived_ref[1:2, :])
        many = jnp.broadcast_to(first, (ROW_TILE, width))
        landed(wq_a, wq, sems.at[1])
        fixed = []
        for k, shift in enumerate((pick(QUERY_B), None, pick(VALUE_B))):
            made = nn(many, wq[:, k * width : (k + 1) * width])
            fixed.append((made if shift is None else made + shift).astype(BF))
        fixed = jnp.concatenate(fixed + [many], axis=1)
    landed(xq_a, xq, sems.at[0])
    fetch(own, wi_a, wi_b, wi, sems.at[3])
    fetch(own, wo_a, wo_b, wo, sems.at[4])
    if train:
        top_rows = xq[0:ROW_TILE, :]
        at_first = lax.broadcasted_iota(jnp.int32, top_rows.shape, 0) == 0
        xq[0:ROW_TILE, :] = jnp.where(at_first, fixed, top_rows)

    def pair_body(j, carry):
        base, q, k, v, parts = attention_parts(xq, j, width, lane, bias_col)
        sides = []
        for h, (mine, qh, kh) in enumerate(parts):
            vh = jnp.where(mine, v, jnp.ones_like(v))
            for s in range(length // STRIP):
                rows = slice(s * STRIP, (s + 1) * STRIP)
                scores = nt(qh[rows, :], kh)
                top = jnp.max(scores, axis=-1, keepdims=True)
                made = nn(jnp.exp(scores - top).astype(BF), vh)
                mass = made[:, HEAD_DIM * (1 - h) : HEAD_DIM * (1 - h) + 1]
                sides.append(made * (1.0 / mass))
                if train:
                    spot = lane[rows, :] == 2 * j + h
                    lse_scr[rows, :] = jnp.where(spot, top + jnp.log(mass), lse_scr[rows, :])
        count_strips = length // STRIP
        for s in range(count_strips):
            rows = slice(s * STRIP, (s + 1) * STRIP)
            both = jnp.where(lane[rows, :] < HEAD_DIM, sides[s], sides[count_strips + s])
            ctx[rows, pl.ds(base, PAIR)] = both.astype(BF)
        return carry

    lax.fori_loop(0, HEADS // 2, pair_body, 0)
    if train:
        lse_ref[...] = jnp.transpose(lse_scr[...])[0:ROW_TILE, :]
    inputs = xq[:, 3 * width :]
    landed(wp_a, wp, sems.at[2])
    n1, r1 = row_norm(inputs.astype(F32) + (nn(ctx[...], wp[...]) + pick(PROJ_B)))
    normed = n1 * pick(ATTN_G) + pick(ATTN_B)
    low = normed.astype(BF)
    if train:
        n1_ref[...] = n1
        r1_ref[...] = r1
    landed(wi_a, wi, sems.at[3])
    landed(wo_a, wo, sems.at[4])
    total = None
    for c in range(ff // CHUNK):
        cols = slice(c * CHUNK, (c + 1) * CHUNK)
        act, slope = gelu_pair(nn(low, wi[:, cols]) + pick(INNER_B, c))
        act = act.astype(BF)
        if train:
            acts[:, cols] = act
            slope_ref[:, cols] = slope.astype(BF)
        term = nn(act, wo[cols, :])
        total = term if total is None else total + term
    n2, r2 = row_norm(normed + (total + pick(OUTER_B)))
    gain = pick(FFN_G)
    z_ref[...] = (n2 * gain + pick(FFN_B)).astype(BF)
    if not train:
        return
    wide_row = lax.broadcasted_iota(jnp.int32, n2.shape, 0)
    pltpu.make_async_copy(cot_ref.at[section], cot, sems.at[5]).wait()
    grad = jnp.where(wide_row < count, cot[...].astype(F32), 0.0)
    second = norm_back(grad, n2, r2, gain)
    sg_ref[...] = second
    gf = second.astype(BF)
    gf_ref[...] = gf
    small_ref[0:1, :] = col_sum(gf)
    small_ref[1:2, :] = col_sum(grad * n2)
    small_ref[2:3, :] = col_sum(grad)
    half_chunks = ff // CHUNK // 2
    rows = send_ref.shape[1]
    each = CHUNK // rows
    for ref, half, order in ((send_ref, 1 - section, info_ref[4]), (keep_ref, section, info_ref[3])):
        for c in range(half_chunks):
            cols = pl.ds(pl.multiple_of((half * half_chunks + c) * CHUNK, CHUNK), CHUNK)
            made = tn(acts[:, cols], gf).astype(BF)
            for p in range(each):
                ref[jnp.bitwise_xor(c * each + p, order)] = made[p * rows : (p + 1) * rows, :]


def forward_call(train, info, pairs, tables, head=None, arrived=None, cot=None):
    xq, wq, wp, wi, wo = (piece[0] for piece in pairs)
    length = xq.shape[0]
    width, ff = wi.shape
    flat = [piece for pair in pairs for piece in pair]
    args = [info] + list(far(*flat)) + list(tables)
    in_specs = [SCALARS] + [FAR] * 10 + [NEAR] * 2
    weights = [near(w.shape, BF) for w in (wp, wi, wo)]
    if train:
        args += [head, arrived] + list(far(cot))
        in_specs += [NEAR, NEAR, FAR]
        shapes = [struct((length, width), BF), near(xq.shape, BF)] + weights
        shapes += [
            near((length, width), BF),
            near((ROW_TILE, length), F32),
            near((length, width), F32),
            near((length, 1), F32),
            near((length, ff), BF),
            near((length, width), BF),
            near((length, width), F32),
            near((8, width), F32),
            near((GROUP, ff // 2 // GROUP, width), BF),
            near((GROUP, ff // 2 // GROUP, width), BF),
        ]
        scratch = [pltpu.VMEM(wq.shape, BF), pltpu.VMEM((length, PAIR), F32), pltpu.VMEM((length, ff), BF)]
        scratch.append(pltpu.VMEM((length, width), BF))
    else:
        shapes = [struct((length, width), BF)]
        scratch = [pltpu.VMEM(xq.shape, BF)] + weights + [pltpu.VMEM((length, width), BF)]
    scratch.append(pltpu.SemaphoreType.DMA((6,)))
    return pl.pallas_call(
        lambda *refs: forward_kernel(train, *refs),
        in_specs=in_specs,
        out_specs=[NEAR] * len(shapes),
        out_shape=shapes,
        scratch_shapes=scratch,
        compiler_params=params_of(20 if train else 24),
        cost_estimate=cost(26 if train else 19),
        name="layer_train" if train else "layer",
    )(*args)


def inner_kernel(
    info_ref, gf_ref, slope_ref, sg_ref, n1_ref, r1_ref, wi_ref, wo_ref, wp_ref, mine, table,
    keep_ref, send_ref, gh_ref, ga_ref, gc_ref, small_ref,
):
    section = info_ref[0]
    pick = layer_vectors(mine, table, section == 1)
    gain = pick(ATTN_G)
    low = jnp.transpose(n1_ref[...] * gain + pick(ATTN_B)).astype(BF)
    ff = wi_ref.shape[1]
    half_chunks = ff // CHUNK // 2
    gf = gf_ref[...]
    gn = sg_ref[...]
    for ref, half, order in ((send_ref, 1 - section, info_ref[6]), (keep_ref, section, info_ref[5])):
        for c in range(half_chunks):
            block = half * half_chunks + c
            cols = pl.ds(pl.multiple_of(block * CHUNK, CHUNK), CHUNK)
            gu = (nt(gf, wo_ref[cols, :]) * slope_ref[:, cols].astype(F32)).astype(BF)
            small_ref[pl.ds(3 + block, 1), :] = col_sum(gu)
            place_rows(ref.at[:, :, c * CHUNK : (c + 1) * CHUNK], nn(low, gu).astype(BF), order)
            gn = gn + nt(gu, wi_ref[:, cols])
    n1 = n1_ref[...]
    gh = norm_back(gn, n1, r1_ref[...], gain)
    gh_ref[...] = gh
    ga = gh.astype(BF)
    ga_ref[...] = ga
    gc_ref[...] = nt(ga, wp_ref[...]).astype(BF)
    small_ref[0:1, :] = col_sum(ga)
    small_ref[1:2, :] = col_sum(gn * n1)
    small_ref[2:3, :] = col_sum(gn)


def inner_call(info, gf, slope, sg, n1, r1, wi, wo, wp, tables):
    tokens, width = gf.shape
    ff = wi.shape[1]
    shapes = [
        near((GROUP, width // GROUP, ff // 2), BF),
        near((GROUP, width // GROUP, ff // 2), BF),
        near((tokens, width), F32),
        near((tokens, width), BF),
        near((tokens, width), BF),
        near((8, width), F32),
    ]
    return pl.pallas_call(
        inner_kernel,
        in_specs=[SCALARS] + [NEAR] * 10,
        out_specs=[NEAR] * len(shapes),
        out_shape=shapes,
        compiler_params=params_of(12),
        cost_estimate=cost(10),
        name="inner_grad",
    )(info, *stay(gf, slope, sg, n1, r1, wi, wo, wp), *tables)


def attention_kernel(
    info_ref, xq, gc_ref, ga_ref, c_ref, lse_ref, keep_ref, send_ref, g_ref, small_ref, xt_scr, ct_scr, mean_scr
):
    section = info_ref[0]
    length, width = gc_ref.shape
    row = lax.broadcasted_iota(jnp.int32, (length, PAIR), 0)
    lane = lax.broadcasted_iota(jnp.int32, (length, PAIR), 1)
    bias_col = jnp.where(row < info_ref[1], 0.0, BIG_NEG).astype(BF)
    ct_scr[...] = turned(c_ref[...])
    xt_scr[...] = turned(xq[:, 3 * width :])
    product = gc_ref[...].astype(F32) * c_ref[...].astype(F32)
    high = product.astype(BF)
    low = (product - high.astype(F32)).astype(BF)
    ones = by_head(jnp.ones((1, width), BF), ROW_TILE)
    mean_scr[...] = nt(ones, high) + nt(ones, low)

    def pair_body(j, carry):
        base, q, k, v, parts = attention_parts(xq, j, width, lane, bias_col)
        kt = turned(k)
        gc = gc_ref[:, pl.ds(base, PAIR)]
        zero = jnp.zeros_like(gc)
        strips = [slice(s * STRIP, (s + 1) * STRIP) for s in range(length // STRIP)]
        gk = [None] * len(strips)
        gv = [None] * len(strips)
        gqt = []
        for h, (mine, qh, kh) in enumerate(parts):
            gch = jnp.where(mine, gc, zero)
            qz = jnp.where(mine, q, zero)
            lse = lse_ref[pl.ds(2 * j + h, 1), :]
            mean = mean_scr[pl.ds(2 * j + h, 1), :]
            gq_h = None
            for s, rows in enumerate(strips):
                probs = jnp.exp(nt(kh[rows, :], qh) - lse)
                gs = (probs * (nt(v[rows, :], gch) - mean)).astype(BF)
                gv_h = nn(probs.astype(BF), gch)
                gk_h = nn(gs, qz)
                term = nn(kt[HEAD_DIM * h : HEAD_DIM * (h + 1), rows], gs)
                gq_h = term if gq_h is None else gq_h + term
                gk[s] = gk_h if h == 0 else gk[s] + gk_h
                gv[s] = gv_h if h == 0 else gv[s] + gv_h
            gqt.append(gq_h)
        gq = jnp.transpose(jnp.concatenate(gqt, axis=0)) * 0.125
        g_ref[:, pl.ds(base, PAIR)] = gq.astype(BF)
        for s, rows in enumerate(strips):
            g_ref[rows, pl.ds(base + width, PAIR)] = gk[s].astype(BF)
            g_ref[rows, pl.ds(base + 2 * width, PAIR)] = gv[s].astype(BF)
        return carry

    lax.fori_loop(0, HEADS // 2, pair_body, 0)
    small_ref[0:1, :] = col_sum(g_ref[:, 0:width])
    small_ref[1:2, :] = col_sum(g_ref[:, 2 * width : 3 * width])
    wide = 3 * width // 2
    for ref, half, order in ((send_ref, 1 - section, info_ref[8]), (keep_ref, section, info_ref[7])):
        cols = pl.ds(pl.multiple_of(half * wide, PAIR), wide)
        place_rows(ref.at[:, :, 0:wide], nn(xt_scr[...], g_ref[:, cols]).astype(BF), order)
        cols = pl.ds(pl.multiple_of(half * (width // 2), PAIR), width // 2)
        place_rows(ref.at[:, :, wide:], nn(ct_scr[...], ga_ref[:, cols]).astype(BF), order)


def attention_call(info, xq, gc, ga, context, lse):
    length, width = gc.shape
    shapes = [
        near((GROUP, width // GROUP, 2 * width), BF),
        near((GROUP, width // GROUP, 2 * width), BF),
        near((length, 3 * width), BF),
        near((8, width), F32),
    ]
    return pl.pallas_call(
        attention_kernel,
        in_specs=[SCALARS] + [NEAR] * 5,
        out_specs=[NEAR] * len(shapes),
        out_shape=shapes,
        scratch_shapes=[
            pltpu.VMEM((width, length), BF),
            pltpu.VMEM((width, length), BF),
            pltpu.VMEM((ROW_TILE, length), F32),
        ],
        compiler_params=params_of(16),
        cost_estimate=cost(14),
        name="attention_grad",
    )(info, *stay(xq, gc, ga, context, lse))


def input_kernel(info_ref, w_a, w_b, g_ref, gh_ref, small1_ref, small2_ref, small3_ref, o_ref, small_ref, w, sem):
    fetch(info_ref[0] == 1, w_a, w_b, w, sem)
    landed(w_a, w, sem)
    made = gh_ref[...] + nt(g_ref[...], w[...])
    o_ref[...] = made
    small_ref[0:2, :] = small3_ref[0:2, :]
    small_ref[2:9, :] = small2_ref[0:7, :]
    small_ref[9:12, :] = small1_ref[0:3, :]
    small_ref[12:16, :] = made[0:4, :]


def input_call(info, g, gh, w, small1, small2, small3):
    return pl.pallas_call(
        input_kernel,
        in_specs=[SCALARS, FAR, FAR] + [NEAR] * 5,
        out_specs=[NEAR] * 2,
        out_shape=[struct(gh.shape, F32), struct((ROW_TILE, gh.shape[1]), F32)],
        scratch_shapes=[pltpu.VMEM(w[0].shape, BF), pltpu.SemaphoreType.DMA(())],
        compiler_params=params_of(12),
        cost_estimate=cost(4),
        name="input_grad",
    )(info, *far(*w), *stay(g, gh, small1, small2, small3))


def head_back_kernel(
    info_ref, small_a, small_b, probs_ref, c_ref, n1_ref, r1_ref, a_ref, slope_ref, n2_ref, r2_ref, own_ref, other_ref,
    wq_ref, wp_ref, wi_ref, wo_ref, table, x_ref, pay_ref, wq, wp, wi, wo, sems,
):
    copies = [
        pltpu.make_async_copy(ref, scr, sems.at[i])
        for i, (ref, scr) in enumerate(((wo_ref, wo), (wi_ref, wi), (wp_ref, wp), (wq_ref, wq)))
    ]
    for copy in copies:
        copy.start()
    width = wp.shape[0]
    length = own_ref.shape[0]
    ff = wi.shape[1]
    n1, n2 = n1_ref[...], n2_ref[...]
    pick = layer_vectors(table, table, info_ref[0] == 0)
    grad = two_rows(small_a[12:13, :], small_b[12:13, :]).astype(BF).astype(F32)
    second = norm_back(grad, n2, r2_ref[...], pick(FFN_G))
    gf = second.astype(BF)
    copies[0].wait()
    gu = (nt(gf, wo[...]) * slope_ref[...]).astype(BF)
    copies[1].wait()
    gn = second + nt(gu, wi[...])
    gh = norm_back(gn, n1, r1_ref[...], pick(ATTN_G))
    ga = gh.astype(BF)
    copies[2].wait()
    gc = nt(ga, wp[...]).astype(BF)
    normed = (n1 * pick(ATTN_G) + pick(ATTN_B)).astype(BF)
    copies[3].wait()
    query_bias = value_bias = jnp.zeros((1, width), F32)
    vectors = {}
    for i, ref in enumerate((own_ref, other_ref)):
        mid = (1 - 2 * i) * info_ref[0] + i
        keys, values, inputs = ref[:, width : 2 * width], ref[:, 2 * width : 3 * width], ref[:, 3 * width :]
        query = ref[0:1, 0:width] * jnp.asarray(0.125, BF)
        gc_row = gc[i : i + 1, :]
        query_heads, gc_heads = by_head(query, ROW_TILE), by_head(gc_row, ROW_TILE)
        probs = probs_ref[i]
        gp = nt(gc_heads, values)
        gs = (probs * (gp - jnp.sum(probs * gp, axis=-1, keepdims=True))).astype(BF)
        low = probs.astype(BF)
        gq = (heads_of(nn(gs, keys)) * 0.125).astype(BF)
        pay_ref[KEY_SUMS + 16 * i : KEY_SUMS + 16 * i + 16, :] = nn(gs, inputs).astype(BF)
        pay_ref[VALUE_SUMS + 16 * i : VALUE_SUMS + 16 * i + 16, :] = nn(low, inputs).astype(BF)
        key_back = nt(query_heads, wq[:, width : 2 * width]).astype(BF)
        value_back = nt(gc_heads, wq[:, 2 * width :]).astype(BF)
        gx = tn(gs, key_back) + tn(low, value_back)
        top = gh[i : i + 1, :] + nt(jnp.broadcast_to(gq, (ROW_TILE, width)), wq[:, 0:width])[0:1, :]
        at_first = lax.broadcasted_iota(jnp.int32, gx.shape, 0) == 0
        x_ref[mid] = gx + jnp.where(at_first, top, 0.0)
        query_bias = query_bias + gq.astype(F32)
        mass = jnp.sum(low.astype(F32), axis=-1, keepdims=True)
        value_bias = value_bias + heads_of(gc_heads.astype(F32) * mass)
        for key, piece in (
            (V_OUTER, gf[i : i + 1, :]),
            (V_NORMED, normed[i : i + 1, :]),
            (V_CONTEXT, c_ref[i : i + 1, :]),
            (V_PROJ, ga[i : i + 1, :]),
            (V_INPUT, ref[0:1, 3 * width :]),
            (V_GQUERY, gq),
            (V_QUERY, query),
            (V_GCONTEXT, gc_row),
        ):
            vectors[2 * key + i] = piece
    gu_sum = col_sum(gu)
    act = a_ref[...]
    own_small = [query_bias, value_bias, col_sum(ga), col_sum(gn * n1), col_sum(gn)]
    own_small += [gu_sum[:, width * k : width * (k + 1)] for k in range(ff // width)]
    own_small += [col_sum(gf), col_sum(grad * n2), col_sum(grad)]

    def stack(pieces):
        row = lax.broadcasted_iota(jnp.int32, (ROW_TILE, width), 0)
        made = jnp.zeros((ROW_TILE, width), F32)
        for k, piece in enumerate(pieces):
            made = jnp.where(row == k, piece.astype(F32), made)
        return made

    pay_ref[VECTORS : VECTORS + 16, :] = stack([vectors[k] for k in range(16)]).astype(BF)
    wide = [value[i : i + 1, width * k : width * (k + 1)] for value in (act, gu) for i in range(2) for k in range(ff // width)]
    pay_ref[ACTS : ACTS + 16, :] = stack(wide).astype(BF)
    pay_ref[SMALLS : SMALLS + 16, :] = jnp.where(info_ref[0] == 0, stack(own_small), small_a[...] + small_b[...]).astype(BF)


def head_back_call(info, small_a, small_b, saved, own, other, wq, wp, wi, wo, table):
    length = own.shape[0]
    width, ff = wi.shape
    args = [small_a, small_b] + list(saved) + [own, other]
    return pl.pallas_call(
        head_back_kernel,
        in_specs=[SCALARS] + [NEAR] * len(args) + [FAR] * 4 + [NEAR],
        out_specs=[NEAR] * 2,
        out_shape=[struct((2, length, width), F32), struct((PAYLOAD, width), BF)],
        scratch_shapes=[pltpu.VMEM(w.shape, BF) for w in (wq, wp, wi, wo)] + [pltpu.SemaphoreType.DMA((4,))],
        compiler_params=params_of(28),
        cost_estimate=cost(12),
        name="head_rows_grad",
    )(info, *args, *far(wq, wp, wi, wo), table)


def outer_final_kernel(info_ref, low_ref, high_ref, gt_ref, o_ref):
    step = pl.program_id(0)
    rows = low_ref.shape[1]
    each = o_ref.shape[0] // rows
    per_half = pl.num_programs(0) // 2

    @pl.when(info_ref[0] == 1)
    def _():
        def fill(ref, first, order):
            for p in range(each):
                o_ref[p * rows : (p + 1) * rows, :] = ref[jnp.bitwise_xor(first + p, order)].astype(F32)

        pl.when(step < per_half)(lambda: fill(low_ref, step * each, info_ref[4]))
        pl.when(step >= per_half)(lambda: fill(high_ref, (step - per_half) * each, info_ref[3]))

    @pl.when(info_ref[0] == 0)
    def _():
        made = None
        for j in range(2):
            left = gt_ref[ACTS + 4 * j + step]
            term = tn(left, gt_ref[VECTORS + 2 * V_OUTER + j])
            made = term if made is None else made + term
        o_ref[...] = made


def outer_final_call(info, low, high, gt):
    width = low.shape[2]
    ff = 2 * low.shape[0] * low.shape[1]
    return pl.pallas_call(
        outer_final_kernel,
        grid=(ff // width,),
        in_specs=[SCALARS, full(low.shape), full(high.shape), full(gt.shape)],
        out_specs=pl.BlockSpec((width, width), lambda i: (i, 0)),
        out_shape=struct((ff, width), F32),
        compiler_params=params_of(32),
        cost_estimate=cost(5),
        name="outer_final",
    )(info, low, high, gt)


def unfold(ref, cols, order, target):
    rows = ref.shape[1]
    for p in range(ref.shape[0]):
        target[p * rows : (p + 1) * rows, :] = ref[jnp.bitwise_xor(p, order), :, cols].astype(F32)


def inner_final_kernel(info_ref, low_ref, high_ref, gt_ref, o_ref):
    step = pl.program_id(0)
    width = o_ref.shape[1]

    @pl.when(info_ref[0] == 1)
    def _():
        for k in range(4):
            ref, order = ((low_ref, info_ref[6]), (high_ref, info_ref[5]))[k // 2]
            cols = slice((k % 2) * width, (k % 2 + 1) * width)
            pl.when(step == k)(lambda ref=ref, order=order, cols=cols: unfold(ref, cols, order, o_ref))

    @pl.when(info_ref[0] == 0)
    def _():
        made = None
        for j in range(2):
            term = tn(gt_ref[VECTORS + 2 * V_NORMED + j], gt_ref[INNERS + 4 * j + step])
            made = term if made is None else made + term
        o_ref[...] = made


def inner_final_call(info, low, high, gt):
    width = gt.shape[2]
    ff = 2 * low.shape[2]
    return pl.pallas_call(
        inner_final_kernel,
        grid=(ff // width,),
        in_specs=[SCALARS, full(low.shape), full(high.shape), full(gt.shape)],
        out_specs=pl.BlockSpec((width, width), lambda i: (0, i)),
        out_shape=struct((width, ff), F32),
        compiler_params=params_of(32),
        cost_estimate=cost(5),
        name="inner_final",
    )(info, low, high, gt)


def qkv_final_kernel(info_ref, low_ref, high_ref, gt_ref, o_ref, p_ref):
    width = p_ref.shape[0]
    wide = 3 * width // 2
    half = width // 2

    @pl.when(info_ref[0] == 1)
    def _():
        for ref, order, k in ((low_ref, info_ref[8], 0), (high_ref, info_ref[7], 1)):
            unfold(ref, slice(0, wide), order, o_ref.at[:, k * wide : (k + 1) * wide])
            unfold(ref, slice(wide, wide + half), order, p_ref.at[:, k * half : (k + 1) * half])

    @pl.when(info_ref[0] == 0)
    def _():
        def pairs(left, right):
            return tn(gt_ref[VECTORS + 2 * left], gt_ref[VECTORS + 2 * right]) + tn(
                gt_ref[VECTORS + 2 * left + 1], gt_ref[VECTORS + 2 * right + 1]
            )

        p_ref[...] = pairs(V_CONTEXT, V_PROJ)
        o_ref[:, 0:width] = pairs(V_INPUT, V_GQUERY)
        chips = gt_ref.shape[1]
        lane = lax.broadcasted_iota(jnp.int32, (chips, width), 1)
        for place, base, key in ((1, KEY_SUMS, V_QUERY), (2, VALUE_SUMS, V_GCONTEXT)):
            made = None
            for j in range(2):
                left = gt_ref[base + 16 * j : base + 16 * j + HEADS].reshape(HEADS * chips, width)
                row = gt_ref[VECTORS + 2 * key + j]
                heads = [
                    jnp.where((lane >= HEAD_DIM * h) & (lane < HEAD_DIM * (h + 1)), row, jnp.zeros_like(row))
                    for h in range(HEADS)
                ]
                term = tn(left, jnp.concatenate(heads, axis=0))
                made = term if made is None else made + term
            o_ref[:, place * width : (place + 1) * width] = made


def qkv_final_call(info, low, high, gt):
    width = gt.shape[2]
    return pl.pallas_call(
        qkv_final_kernel,
        in_specs=[SCALARS, full(low.shape), full(high.shape), full(gt.shape)],
        out_specs=[full((width, 3 * width)), full((width, width))],
        out_shape=[struct((width, 3 * width), F32), struct((width, width), F32)],
        compiler_params=params_of(32),
        cost_estimate=cost(6),
        name="qkv_final",
    )(info, low, high, gt)


def swap(value):
    return lax.ppermute(value, "section", SWAP)


def add_low(left, right):
    return (left.astype(F32) + right.astype(F32)).astype(BF)


def hop(value, stage, orders):
    chips = lax.axis_size("dp")
    pairs = [
        (section * chips + chip, section * chips + (chip ^ orders[section][stage]))
        for section in range(2)
        for chip in range(chips)
    ]
    return lax.ppermute(value, ("section", "dp"), pairs)


def after(value, *others):
    return lax.optimization_barrier((value,) + others)[0]


def beside(made, *sums):
    tied = lax.optimization_barrier(tuple(made) + tuple(one.coming for one in sums))
    for one, coming in zip(sums, tied[len(made) :]):
        one.coming = coming
    return tied[: len(made)]


class Sum:
    def __init__(self, keep, send, group):
        self.part, self.coming, self.orders = keep, swap(send), ORDERS[group]

    def add(self):
        half = self.part.shape[0] if self.coming.shape[0] == self.part.shape[0] else self.part.shape[0] // 2
        self.part = add_low(self.part[:half], self.coming)
        return self.part

    def halve(self, stage):
        self.coming = hop(self.part[self.part.shape[0] // 2 :], stage, self.orders)

    def across(self):
        chips = lax.axis_size("dp")
        if chips > GROUP:
            groups = [[low + GROUP * high for high in range(chips // GROUP)] for low in range(GROUP)]
            self.part = lax.psum(self.part, "dp", axis_index_groups=groups)

    def double(self, stage):
        self.coming = hop(self.part, stage, self.orders)

    def join(self):
        self.part = jnp.concatenate([self.part, self.coming], axis=0)
        return self.part


def order_of(chip, orders):
    place = jnp.int32(0)
    for stage in range(4):
        bit = (chip // orders[stage]) % 2
        place = place + bit * (8 >> stage)
    return place


def local(embeddings, cotangent, lengths, *weights):
    (wq, query_bias, value_bias, wp, proj_bias, attn_gain, attn_bias, wi, inner_bias, wo, outer_bias, ffn_gain, ffn_bias) = (
        piece[0] for piece in weights
    )
    section = lax.axis_index("section")
    chip = lax.axis_index("dp")
    first_section = section == 0
    inputs = embeddings[0]
    width = inputs.shape[2]
    scalars = [section, jnp.where(first_section, lengths[0], lengths[1]), jnp.where(first_section, lengths[1], lengths[0])]
    for orders in ORDERS:
        places = [order_of(chip, order) for order in orders]
        scalars += [jnp.where(first_section, places[0], places[1]), jnp.where(first_section, places[1], places[0])]
    info = jnp.stack(scalars).astype(jnp.int32)
    vectors = [weights[k] for k in (1, 2, 4, 5, 6, 8, 10, 11, 12)]
    own, other, own_table = qkv_call(info, inputs, wq, vectors)
    tables = (own_table, swap(own_table))
    wp_pair = (wp, swap(wp))
    wi_pair = (wi, swap(wi))
    xq_pair = (own, swap(other))
    wq_pair = (wq, swap(wq))
    wo_pair = (wo, swap(wo))
    head = head_call(info, own, other, wp, wi, wo, own_table)
    arrived = swap(head[0])
    pairs = (xq_pair, wq_pair, wp_pair, wi_pair, wo_pair)
    (z, xq_d, wp_d, wi_d, wo_d, context, lse, n1, r1, slope, gf, sg, small1, outer_keep, outer_send) = forward_call(
        True, info, pairs, tables, head[0], arrived, cotangent
    )
    g1 = Sum(outer_keep, outer_send, 0)

    made = inner_call(info, gf, slope, sg, n1, r1, wi_d, wo_d, wp_d, tables)
    inner_keep, inner_send, gh, ga, gc, small2 = beside(made, g1)
    g1.add()
    g1.halve(0)
    g2 = Sum(inner_keep, inner_send, 1)

    made = attention_call(info, xq_d, after(gc, g1.part), ga, context, lse)
    qkv_keep, qkv_send, g_qkv, small3 = beside(made, g1, g2)
    g1.add()
    g1.halve(1)
    g2.add()
    g2.halve(0)
    g3 = Sum(qkv_keep, qkv_send, 2)

    made = input_call(info, after(g_qkv, g1.part, g2.part), gh, wq_pair, small1, small2, small3)
    gx, dsmall = beside(made, g3)
    g3.add()
    g3.halve(0)
    dsmall_other = after(swap(dsmall), g3.part)
    made = head_back_call(info, dsmall, dsmall_other, head[1:], own, other, wq, wp, wi, wo, own_table)
    encoder_gx, payload = beside(made, g1, g2, g3)
    gathered = lax.all_gather(payload, "dp")
    g1.add()
    g1.halve(2)
    g2.add()
    g2.halve(1)
    g3.add()
    g3.halve(1)
    gx_other = swap(gx)

    late = (own_table, after(tables[1], g1.part, g2.part, g3.part))
    made = forward_call(False, info, pairs, late)
    (e_low,) = beside(made, g1, g2, g3)
    g1.add()
    g1.halve(3)
    g2.add()
    g2.halve(2)
    g3.add()
    g3.halve(2)
    z_other = swap(jnp.where(first_section, z, e_low))
    z_mine = jnp.where(first_section, e_low, z)
    decoder_gx = jnp.stack([after(gx_other, g3.part), gx])
    later = jnp.arange(gx.shape[0])[None, :, None] > 0
    embed_grads = jnp.where(first_section, encoder_gx, jnp.where(later, decoder_gx, 0.0))
    (embed_grads,) = beside((embed_grads,), g1, g2, g3)

    g1.add()
    g1.across()
    g1.double(3)
    g2.add()
    g2.halve(3)
    g3.add()
    g3.halve(3)
    z_other = after(z_other, g3.part)
    outputs = jnp.where(first_section, jnp.stack([z_mine, z_other]), jnp.stack([z_other, z_mine]))
    (outputs,) = beside((outputs,), g1, g2, g3)
    g1.join()
    g1.double(2)
    g2.add()
    g2.across()
    g2.double(3)
    g3.add()
    g3.across()
    g3.double(3)
    g1.join()
    g1.double(1)
    g2.join()
    g2.double(2)
    g3.join()
    g3.double(2)
    g1.join()
    g1.double(0)
    g2.join()
    g2.double(1)
    g3.join()
    g3.double(1)
    gt = jnp.transpose(after(gathered, g3.part), (1, 0, 2))
    sums = jnp.sum(gt[SMALLS : SMALLS + 12].astype(F32), axis=1)
    gt, sums = beside((gt, sums), g1, g2, g3)
    outer_half = g1.join()
    outer_other = swap(outer_half)
    g2.join()
    g2.double(0)
    g3.join()
    g3.double(0)
    outer_grad = outer_final_call(info, after(outer_other, g2.part, g3.part), outer_half, gt)
    (outer_grad,) = beside((outer_grad,), g2, g3)
    inner_half = g2.join()
    inner_other = swap(inner_half)
    qkv_half = g3.join()
    qkv_other = swap(qkv_half)
    inner_grad = inner_final_call(info, after(inner_other, qkv_half), inner_half, gt)
    qkv_grad, proj_grad = qkv_final_call(info, after(qkv_other, inner_grad), qkv_half, gt)
    results = (
        outputs,
        embed_grads,
        qkv_grad,
        sums[0],
        sums[1],
        proj_grad,
        sums[2],
        sums[3],
        sums[4],
        inner_grad,
        sums[5:9].reshape(-1),
        outer_grad,
        sums[9],
        sums[10],
        sums[11],
    )
    return tuple(piece[None] for piece in results)


def solution(mesh):
    matrix = P("section", None, None)
    vector = P("section", None)
    return jax.shard_map(
        local,
        mesh=mesh,
        in_specs=(P("section", "dp", None, None), P("dp", None, None), P("dp"))
        + (matrix, vector, vector, matrix, vector, vector, vector)
        + (matrix, vector, matrix, vector, vector, vector),
        out_specs=(P("section", "dp", None, None), P("section", "dp", None, None))
        + (matrix, vector, vector, matrix, vector, vector, vector)
        + (matrix, vector, matrix, vector, vector, vector),
        check_vma=False,
    )
```

time: 817 us -> 335 us (0.41)
  waiting for transfers between devices: 387 us -> 113 us
  matrix products: 226 us -> 0 us
  Pallas kernels: 0 us -> 121 us
  local copies, waits for them, and re-layouts: 103 us -> 17.2 us
  other arithmetic: 74.3 us -> 22 us
  starting transfers between devices: 3.89 us -> 38.3 us
    psum x1 -> x0, waiting for transfers between devices: 370 us -> none  [local(): lax.psum(piece.astype(BF), 'dp').astype(F32)]
    dot_general x41 -> x0, matrix products: 210 us -> none  [the longest x39 209 us: dot(): return jnp.einsum(form, left, right, preferred_element_type=F32)]
    pallas_call x0 -> x11, Pallas kernels: none -> 121 us  [the longest x2 46.1 us: forward_call(): pl.pallas_call(lambda *refs: forward_kernel(train, *refs), in_specs=in_sp...]
    ppermute x2 -> x40, waiting for transfers between devices: 0.01 us -> 113 us  [the longest x24 105 us: hop(): return lax.ppermute(value, ('section', 'dp'), pairs)]
    convert_element_type x6 -> x12, other arithmetic: 50.4 us -> 9.3 us  [add_low(): return (left.astype(F32) + right.astype(F32)).astype(BF)]
    unnamed x190 -> x55, local copies, waits for them, and re-layouts: 42.9 us -> 8.13 us
    ppermute x2 -> x40, starting transfers between devices: 3.81 us -> 38.3 us  [the longest x24 33.2 us: hop(): return lax.ppermute(value, ('section', 'dp'), pairs)]
    all_gather x1, waiting for transfers between devices: 16.6 us -> 0.02 us  [local(): gathered = lax.all_gather(payload, 'dp')]
  transfers between devices with their start and end apart: 4 -> 41, of which waited for: 2 -> 15; matrix products, arithmetic and copies ran while one was open for 11% -> 10% of each run, Pallas kernels for 0% -> 27%
where the time goes in v2:
time: 335 us; the launch traced here: 330 us
  Pallas kernels  121 us (36%)
  waiting for transfers between devices  113 us (34%)
  starting transfers between devices  38.3 us (11%)
  other arithmetic  22 us (7%)
  between operations  17.8 us (5%)
  local copies, waits for them, and re-layouts  17.2 us (5%)
    ppermute x24, waiting for transfers between devices, hop(): return lax.ppermute(value, ('section', 'dp'), pairs)  105 us
    pallas_call x2, Pallas kernels, forward_call(): pl.pallas_call(lambda *refs: forward_kernel(train, *refs), in_specs=in_sp...  46.1 us
    ppermute x24, starting transfers between devices, hop(): return lax.ppermute(value, ('section', 'dp'), pairs)  33.2 us
    pallas_call x1, Pallas kernels, attention_call(): pl.pallas_call(attention_kernel, in_specs=[SCALARS] + [NEAR] * 5, out_spe...  14.5 us
    pallas_call x1, Pallas kernels, head_back_call(): pl.pallas_call(head_back_kernel, in_specs=[SCALARS] + [NEAR] * len(args)...  11.7 us
    pallas_call x1, Pallas kernels, inner_call(): pl.pallas_call(inner_kernel, in_specs=[SCALARS] + [NEAR] * 10, out_specs=...  10 us
    convert_element_type x12, other arithmetic, add_low(): return (left.astype(F32) + right.astype(F32)).astype(BF)  9.3 us
    ppermute x16, waiting for transfers between devices, swap(): return lax.ppermute(value, 'section', SWAP)  8.46 us
  transfers between devices with their start and end apart: 41, of which 15 were waited for; matrix products, arithmetic and copies ran while one was open for 10% of the time, Pallas kernels for 27%

profile of v2, /device:TPU:0, one launch (start us, length us, event | category | flops | bytes accessed | tf_op | source)
XLA Modules:
  0.0 329.8 jit_solution(9782178092208595971)
XLA Ops:
  12.3 7.5 %qkv.1 = (bf16[512,3072]{1,0:T(8,128)(2,1)S(1)}, bf16[512,3072]{1,0:T(8,128)(2,1)S(1)}, f32[16,768]{1,0:T(8,128)S(1)}) custom-call(s32[9]{0:T(128)S(1)} %stack.62.info_ref.refs_0_, bf16[2,512,768]{2,1,0:T(8,128)(2,1)} %bitcast.60, bf16[768,2304]{1,0:T(8,128)(2,1)} %bitcast.55, f32[1,768]{1,0:T(1,128)} %refs_0_.1, f32[1,768]{1,0:T(1,128)} %refs_1_.1, ...), custom_call_target="tpu_custom_call" | custom-call | flops 6600000000 | bytes 12000000 | tf_op jit(solution)/shard_map/qkv/pallas_call | solution.py:162
  20.0 7.1 %head_rows.1 = (bf16[16,768]{1,0:T(8,128)(2,1)S(1)}, f32[2,16,512]{2,1,0:T(8,128)S(1)}, bf16[16,768]{1,0:T(8,128)(2,1)S(1)}, f32[16,768]{1,0:T(8,128)S(1)}, f32[...) custom-call(s32[9]{0:T(128)S(1)} %stack.62.info_ref.refs_0_, ...), custom_call_target="tpu_custom_call" | custom-call | flops 7699999744 | bytes 14000000 | tf_op jit(solution)/shard_map/head_rows/pallas_call | solution.py:270
  27.5 3.5 %collective-permute-done.6.refs_14_ = bf16[16,768]{1,0:T(8,128)(2,1)S(1)} collective-permute-done((bf16[16,768]{1,0:T(8,128)(2,1)S(1)}, bf16[16,768]{1,0:T(8,128)(2,1)S(1)}, u32[]{:S(2)}, u32[]{:S(2)}) %collective-permute-start.6) | collective-permute-done | bytes 24608 | tf_op jit(solution)/shard_map/ppermute | solution.py:846
  32.7 2.5 collective-permute-done.2.refs_6_
  37.3 26.6 %layer_train.1 = (bf16[512,768]{1,0:T(8,128)(2,1)S(1)}, bf16[512,3072]{1,0:T(8,128)(2,1)S(1)}, bf16[768,768]{1,0:T(8,128)(2,1)S(1)}, bf16[768,3072]{1,0:T(8,128)...) custom-call(s32[9]{0:T(128)S(1)} %stack.62.info_ref.refs_0_, ...), custom_call_target="tpu_custom_call" | custom-call | flops 28600000512 | bytes 52000000 | tf_op jit(solution)/shard_map/layer_train/pallas_call | solution.py:445
  65.1 10.0 %inner_grad.1 = (bf16[16,48,1536]{2,1,0:T(8,128)(2,1)S(1)}, bf16[16,48,1536]{2,1,0:T(8,128)(2,1)S(1)}, f32[512,768]{1,0:T(8,128)S(1)}, bf16[512,768]{1,0:T(8,128...) custom-call(s32[9]{0:T(128)S(1)} %stack.62.info_ref.refs_0_, ...), custom_call_target="tpu_custom_call" | custom-call | flops 11000000512 | bytes 20000000 | tf_op jit(solution)/shard_map/inner_grad/pallas_call | solution.py:499
  76.1 2.9 collective-permute-start.8
  79.0 14.5 %attention_grad.1 = (bf16[16,48,1536]{2,1,0:T(8,128)(2,1)S(1)}, bf16[16,48,1536]{2,1,0:T(8,128)(2,1)S(1)}, bf16[512,2304]{1,0:T(8,128)(2,1)S(1)}, f32[8,768]{1,0:T(8,128)S(1)}) custom-call(s32[9]{0:T(128)S(1)} %stack.62.info_ref.refs_0_, bf16[512,3072]{1,0:T(8,128)(2,1)S(1)} %get-tuple-element.130.xq, bf16[512,768]{1,0:T(8,128)(2,1)S(1)} %get-tuple-element.132.gc_ref, ...), custom_call_target="tpu_custom_call" | custom-call | flops 15399999488 | bytes 28000000 | tf_op jit(solution)/shard_map/attention_grad/pallas_call | solution.py:577
  99.1 5.7 %input_grad.1 = (f32[512,768]{1,0:T(8,128)}, f32[16,768]{1,0:T(8,128)S(1)}) custom-call(s32[9]{0:T(128)S(1)} %stack.62.info_ref.refs_0_, bf16[768,2304]{1,0:T(8,128)(2,1)} %bitcast.57, bf16[768,2304]{1,0:T(8,128)(2,1)} %collective-permute-done.1.refs_4_.w_b, bf16[512,2304]{1,0:T(8,128)(2,1)S(1)} %get-tuple-element.145.g_ref, ...), custom_call_target="tpu_custom_call" | custom-call | flops 4400000000 | bytes 8000000 | tf_op jit(solution)/shard_map/input_grad/pallas_call | solution.py:605
  108.7 11.7 %head_rows_grad.1 = (f32[2,512,768]{2,1,0:T(8,128)S(1)}, bf16[112,768]{1,0:T(8,128)(2,1)}) custom-call(s32[9]{0:T(128)S(1)} %stack.62.info_ref.refs_0_, f32[16,768]{1,0:T(8,128)S(1)} %get-tuple-element.153.small_a, f32[16,768]{1,0:T(8,128)S(1)} %collective-permute-done.11.small_b, f32[2,16,512]{2,1,0:T(8,128)S(1)} %get-tuple-element.157.probs_ref, ...), custom_call_target="tpu_custom_call" | custom-call | flops 13200000000 | bytes 24000000 | tf_op jit(solution)/shard_map/head_rows_grad/pallas_call | solution.py:703
  120.5 18.6 %collective-permute-done.14 = bf16[8,48,1536]{2,1,0:T(8,128)(2,1)} collective-permute-done((bf16[8,48,1536]{2,1,0:T(8,128)(2,1)S(1)}, bf16[8,48,1536]{2,1,0:T(8,128)(2,1)}, u32[]{:S(2)}, u32[]{:S(2)}) %collective-permute-start.14) | collective-permute-done | bytes 1179680 | tf_op jit(solution)/shard_map/ppermute | solution.py:860
  139.1 2.1 add_convert_fusion.3
  148.8 19.5 %layer.1 = bf16[512,768]{1,0:T(8,128)(2,1)S(1)} custom-call(s32[9]{0:T(128)S(1)} %stack.62.info_ref.refs_0_, bf16[512,3072]{1,0:T(8,128)(2,1)} %copy-done.4, bf16[512,3072]{1,0:T(8,128)(2,1)} %copy-done.19, bf16[768,2304]{1,0:T(8,128)(2,1)} %bitcast.59, bf16[768,2304]{1,0:T(8,128)(2,1)} %collective-permute-done.1.refs_4_.w_b, bf16[768,768]{1,0:T(8,128)(2,1)} %bitcast.64, ...), custom_call_target="tpu_custom_call" | custom-call | flops 20899999744 | bytes 38000000 | tf_op jit(solution)/shard_map/layer/pallas_call | solution.py:445
  169.7 2.8 collective-permute-start.21
  176.2 4.1 %fusion = f32[2,512,768]{2,1,0:T(8,128)} fusion(f32[2,512,768]{2,1,0:T(8,128)S(1)} %get-tuple-element.174, f32[1,512,768]{2,1,0:T(8,128)} %bitcast.18, f32[1,512,768]{2,1,0:T(8,128)} %bitcast.17, pred[512]{0:T(512)(128)(4,1)S(1)} %iota_compare_fusion, pred[]{:T(512)S(6)} %eq.28), kind=kLoop, calls=%fused_computation.4 | loop fusion | flops 2359296 | bytes 9437697 | tf_op jit(solution)/shard_map/jit(_where)/select_n | solution.py:981
  180.3 12.5 %collective-permute-done.20 = bf16[1,96,768]{2,1,0:T(8,128)(2,1)S(1)} collective-permute-done((bf16[1,96,768]{2,1,0:T(8,128)(2,1)S(1)}, bf16[1,96,768]{2,1,0:T(8,128)(2,1)S(1)}, u32[]{:S(2)}, u32[]{:S(2)}) %collective-permute-start.20) | collective-permute-done | bytes 147488 | tf_op jit(solution)/shard_map/ppermute | solution.py:860
  192.9 2.1 collective-permute-start.24
  195.1 3.5 %collective-permute-start.23 = (bf16[1,96,768]{2,1,0:T(8,128)(2,1)S(1)}, bf16[1,96,768]{2,1,0:T(8,128)(2,1)S(1)}, u32[]{:S(2)}, u32[]{:S(2)}) collective-permute-start(bf16[1,96,768]{2,1,0:T(8,128)(2,1)S(1)} %get-tuple-element.206), channel_id=1, source_target_pairs={{0,8},{1,9},{2,10},{3,11},{4,12},{5,13},{6,14},{7,15},{8,0},{9,1},... | collective-permute-start | bytes 442376 | tf_op jit(solution)/shard_map/ppermute | solution.py:860
  200.2 16.5 %collective-permute-done.23 = bf16[1,96,768]{2,1,0:T(8,128)(2,1)S(1)} collective-permute-done((bf16[1,96,768]{2,1,0:T(8,128)(2,1)S(1)}, bf16[1,96,768]{2,1,0:T(8,128)(2,1)S(1)}, u32[]{:S(2)}, u32[]{:S(2)}) %collective-permute-start.23) | collective-permute-done | bytes 147488 | tf_op jit(solution)/shard_map/ppermute | solution.py:860
  216.7 11.5 %collective-permute-done.25 = bf16[1,48,1536]{2,1,0:T(8,128)(2,1)S(1)} collective-permute-done((bf16[1,48,1536]{2,1,0:T(8,128)(2,1)S(1)}, bf16[1,48,1536]{2,1,0:T(8,128)(2,1)S(1)}, u32[]{:S(2)}, u32[]{:S(2)}) %collective-permute-start.25) | collective-permute-done | bytes 147488 | tf_op jit(solution)/shard_map/ppermute | solution.py:860
  228.2 2.2 collective-permute-start.28
  231.0 4.0 %collective-permute-done.28 = bf16[2,96,768]{2,1,0:T(8,128)(2,1)S(1)} collective-permute-done((bf16[2,96,768]{2,1,0:T(8,128)(2,1)S(1)}, bf16[2,96,768]{2,1,0:T(8,128)(2,1)S(1)}, u32[]{:S(2)}, u32[]{:S(2)}) %collective-permute-start.28) | collective-permute-done | bytes 294944 | tf_op jit(solution)/shard_map/ppermute | solution.py:860
  235.9 3.9 %collective-permute-start.26 = (bf16[1,48,1536]{2,1,0:T(8,128)(2,1)S(1)}, bf16[1,48,1536]{2,1,0:T(8,128)(2,1)S(1)}, u32[]{:S(2)}, u32[]{:S(2)}) collective-permute-start(bf16[1,48,1536]{2,1,0:T(8,128)(2,1)S(1)} %get-tuple-element.208), channel_id=1, source_target_pairs={{0,8},{1,9},{2,10},{3,11},{4,12},{5,13},{6,14},{7,15},{8,0},{9,1},... | collective-permute-start | bytes 442376 | tf_op jit(solution)/shard_map/ppermute | solution.py:860
  240.6 9.2 %collective-permute-done.29 = bf16[4,96,768]{2,1,0:T(8,128)(2,1)S(1)} collective-permute-done((bf16[4,96,768]{2,1,0:T(8,128)(2,1)S(1)}, bf16[4,96,768]{2,1,0:T(8,128)(2,1)S(1)}, u32[]{:S(2)}, u32[]{:S(2)}) %collective-permute-start.29) | collective-permute-done | bytes 589856 | tf_op jit(solution)/shard_map/ppermute | solution.py:860
  255.6 7.0 %collective-permute-done.27 = bf16[2,48,1536]{2,1,0:T(8,128)(2,1)S(1)} collective-permute-done((bf16[2,48,1536]{2,1,0:T(8,128)(2,1)S(1)}, bf16[2,48,1536]{2,1,0:T(8,128)(2,1)S(1)}, u32[]{:S(2)}, u32[]{:S(2)}) %collective-permute-start.27) | collective-permute-done | bytes 294944 | tf_op jit(solution)/shard_map/ppermute | solution.py:860
  264.2 2.6 copy.34
  267.0 2.4 collective-permute-done.33
  269.4 4.3 %collective-permute-done.34 = bf16[4,48,1536]{2,1,0:T(8,128)(2,1)} collective-permute-done((bf16[4,48,1536]{2,1,0:T(8,128)(2,1)}, bf16[4,48,1536]{2,1,0:T(8,128)(2,1)}, u32[]{:S(2)}, u32[]{:S(2)}) %collective-permute-start.34) | collective-permute-done | bytes 589856 | tf_op jit(solution)/shard_map/ppermute | solution.py:860
  280.7 5.8 %outer_final.1 = f32[3072,768]{1,0:T(8,128)} custom-call(s32[9]{0:T(128)S(1)} %stack.62.info_ref.refs_0_, bf16[16,96,768]{2,1,0:T(8,128)(2,1)S(1)} %collective-permute-done.35.low_ref, bf16[16,96,768]{2,1,0:T(8,128)(2,1)S(1)} %constant_dynamic-update-slice_fusion.high_ref, bf16[112,16,768]{2,1,0:T(8,128)(2,1)S(1)} %bitcast.36), custom_call_target="tpu_custom_call" | custom-call | flops 5500000256 | bytes 10000000 | tf_op jit(solution)/shard_map/outer_final/pallas_call | solution.py:743
  286.6 18.5 %collective-permute-done.37 = bf16[8,48,1536]{2,1,0:T(8,128)(2,1)S(1)} collective-permute-done((bf16[8,48,1536]{2,1,0:T(8,128)(2,1)S(1)}, bf16[8,48,1536]{2,1,0:T(8,128)(2,1)S(1)}, u32[]{:S(2)}, u32[]{:S(2)}) %collective-permute-start.37) | collective-permute-done | bytes 1179680 | tf_op jit(solution)/shard_map/ppermute | solution.py:860
  309.7 5.8 %inner_final.1 = f32[768,3072]{1,0:T(8,128)} custom-call(s32[9]{0:T(128)S(1)} %stack.62.info_ref.refs_0_, bf16[16,48,1536]{2,1,0:T(8,128)(2,1)S(1)} %collective-permute-done.39.low_ref, bf16[16,48,1536]{2,1,0:T(8,128)(2,1)S(1)} %constant_dynamic-update-slice_fusion.10.high_ref, bf16[112,16,768]{2,1,0:T(8,128)(2,1)S(1)} %bitcast.37), custom_call_target="tpu_custom_call" | custom-call | flops 5500000256 | bytes 10000000 | tf_op jit(solution)/shard_map/inner_final/pallas_call | solution.py:784
  315.6 7.0 %qkv_final.1 = (f32[768,2304]{1,0:T(8,128)}, f32[768,768]{1,0:T(8,128)}) custom-call(s32[9]{0:T(128)S(1)} %stack.62.info_ref.refs_0_, bf16[16,48,1536]{2,1,0:T(8,128)(2,1)S(1)} %collective-permute-done.38.low_ref, bf16[16,48,1536]{2,1,0:T(8,128)(2,1)S(1)} %constant_dynamic-update-slice_fusion.5.high_ref, bf16[112,16,768]{2,1,0:T(8,128)(2,1)S(1)} %bitcast.38), custom_call_target="tpu_custom_call" | custom-call | flops 6600000000 | bytes 12000000 | tf_op jit(solution)/shard_map/qkv_final/pallas_call | solution.py:834
  (165 shorter events, 53.9 us)
Async XLA Ops:
  7.2 257.0 %all-gather.3.cloned.1.call-start = ((), (), s32[]{:S(2)}) async-start(), calls=%async_computation | async-start | bytes 2924544 | tf_op jit(solution)/shard_map/all_gather | solution.py:959
  7.2 28.0 %collective-permute-start.3 = (bf16[768,3072]{1,0:T(8,128)(2,1)}, bf16[768,3072]{1,0:T(8,128)(2,1)}, u32[]{:S(2)}, u32[]{:S(2)}) collective-permute-start(bf16[768,3072]{1,0:T(8,128)(2,1)} %bitcast.44), channel_id=1, source_target_pairs={{0,16},{16,0},{1,17},{17,1},{2,18},{18,2},{3,19},{19,3},{4,20},{20... | collective-permute-start | bytes 14155784 | tf_op jit(solution)/shard_map/ppermute | solution.py:846
  7.7 27.5 %collective-permute-start.4 = (bf16[3072,768]{1,0:T(8,128)(2,1)}, bf16[3072,768]{1,0:T(8,128)(2,1)}, u32[]{:S(2)}, u32[]{:S(2)}) collective-permute-start(bf16[3072,768]{1,0:T(8,128)(2,1)} %bitcast.49), channel_id=1, source_target_pairs={{0,16},{16,0},{1,17},{17,1},{2,18},{18,2},{3,19},{19,3},{4,20},{20... | collective-permute-start | bytes 14155784 | tf_op jit(solution)/shard_map/ppermute | solution.py:846
  7.8 27.4 %collective-permute-start.1 = (bf16[768,2304]{1,0:T(8,128)(2,1)}, bf16[768,2304]{1,0:T(8,128)(2,1)}, u32[]{:S(2)}, u32[]{:S(2)}) collective-permute-start(bf16[768,2304]{1,0:T(8,128)(2,1)} %bitcast.54), channel_id=1, source_target_pairs={{0,16},{16,0},{1,17},{17,1},{2,18},{18,2},{3,19},{19,3},{4,20},{20... | collective-permute-start | bytes 10616840 | tf_op jit(solution)/shard_map/ppermute | solution.py:846
  19.8 15.4 %collective-permute-start = (bf16[512,3072]{1,0:T(8,128)(2,1)S(1)}, bf16[512,3072]{1,0:T(8,128)(2,1)S(1)}, u32[]{:S(2)}, u32[]{:S(2)}) collective-permute-start(bf16[512,3072]{1,0:T(8,128)(2,1)S(1)} %get-tuple-element.110.other_ref), channel_id=1, source_target_pairs={{0,16},{16,0},{1,17},{17,1},{2,18},{18,2},{3,19},{19,3},{4,20},{20... | collective-permute-start | bytes 9437192 | tf_op jit(solution)/shard_map/ppermute | solution.py:846
  64.7 10.4 %collective-permute-start.7 = (bf16[16,96,768]{2,1,0:T(8,128)(2,1)S(1)}, bf16[16,96,768]{2,1,0:T(8,128)(2,1)S(1)}, u32[]{:S(2)}, u32[]{:S(2)}) collective-permute-start(bf16[16,96,768]{2,1,0:T(8,128)(2,1)S(1)} %get-tuple-element.128), channel_id=1, source_target_pairs={{0,16},{16,0},{1,17},{17,1},{2,18},{18,2},{3,19},{19,3},{4,20},{20... | collective-permute-start | bytes 7077896 | tf_op jit(solution)/shard_map/ppermute | solution.py:846
  75.1 18.4 %collective-permute-start.9 = (bf16[16,48,1536]{2,1,0:T(8,128)(2,1)S(1)}, bf16[16,48,1536]{2,1,0:T(8,128)(2,1)S(1)}, u32[]{:S(2)}, u32[]{:S(2)}) collective-permute-start(bf16[16,48,1536]{2,1,0:T(8,128)(2,1)S(1)} %get-tuple-element.140), channel_id=1, source_target_pairs={{0,16},{16,0},{1,17},{17,1},{2,18},{18,2},{3,19},{19,3},{4,20},{20... | collective-permute-start | bytes 7077896 | tf_op jit(solution)/shard_map/ppermute | solution.py:846
  76.1 17.4 %collective-permute-start.8 = (bf16[8,96,768]{2,1,0:T(8,128)(2,1)S(1)}, bf16[8,96,768]{2,1,0:T(8,128)(2,1)S(1)}, u32[]{:S(2)}, u32[]{:S(2)}) collective-permute-start(bf16[8,96,768]{2,1,0:T(8,128)(2,1)S(1)} %slice.147), channel_id=1, source_target_pairs={{0,1},{1,0},{2,3},{3,2},{4,5},{5,4},{6,7},{7,6},{8,9},{9,8},{10,11... | collective-permute-start | bytes 3538952 | tf_op jit(solution)/shard_map/ppermute | solution.py:860
  93.5 11.4 %collective-permute-start.10 = (bf16[16,48,1536]{2,1,0:T(8,128)(2,1)S(1)}, bf16[16,48,1536]{2,1,0:T(8,128)(2,1)S(1)}, u32[]{:S(2)}, u32[]{:S(2)}) collective-permute-start(bf16[16,48,1536]{2,1,0:T(8,128)(2,1)S(1)} %get-tuple-element.152), channel_id=1, source_target_pairs={{0,16},{16,0},{1,17},{17,1},{2,18},{18,2},{3,19},{19,3},{4,20},{20... | collective-permute-start | bytes 7077896 | tf_op jit(solution)/shard_map/ppermute | solution.py:846
  95.8 24.6 %collective-permute-start.13 = (bf16[8,48,1536]{2,1,0:T(8,128)(2,1)S(1)}, bf16[8,48,1536]{2,1,0:T(8,128)(2,1)}, u32[]{:S(2)}, u32[]{:S(2)}) collective-permute-start(bf16[8,48,1536]{2,1,0:T(8,128)(2,1)S(1)} %slice.150), channel_id=1, source_target_pairs={{0,1},{1,0},{2,3},{3,2},{4,5},{5,4},{6,7},{7,6},{8,9},{9,8},{10,11... | collective-permute-start | bytes 3538952 | tf_op jit(solution)/shard_map/ppermute | solution.py:860
  97.5 22.9 %collective-permute-start.12 = (bf16[4,96,768]{2,1,0:T(8,128)(2,1)S(1)}, bf16[4,96,768]{2,1,0:T(8,128)(2,1)S(1)}, u32[]{:S(2)}, u32[]{:S(2)}) collective-permute-start(bf16[4,96,768]{2,1,0:T(8,128)(2,1)S(1)} %slice.149), channel_id=1, source_target_pairs={{0,4},{1,5},{2,6},{3,7},{4,0},{5,1},{6,2},{7,3},{8,12},{9,13},{10,... | collective-permute-start | bytes 1769480 | tf_op jit(solution)/shard_map/ppermute | solution.py:860
  106.8 32.3 %collective-permute-start.14 = (bf16[8,48,1536]{2,1,0:T(8,128)(2,1)S(1)}, bf16[8,48,1536]{2,1,0:T(8,128)(2,1)}, u32[]{:S(2)}, u32[]{:S(2)}) collective-permute-start(bf16[8,48,1536]{2,1,0:T(8,128)(2,1)S(1)} %slice.151), channel_id=1, source_target_pairs={{0,4},{1,5},{2,6},{3,7},{4,0},{5,1},{6,2},{7,3},{8,12},{9,13},{10,... | collective-permute-start | bytes 3538952 | tf_op jit(solution)/shard_map/ppermute | solution.py:860
  108.5 65.7 %collective-permute-start.19 = (f32[512,768]{1,0:T(8,128)}, f32[512,768]{1,0:T(8,128)}, u32[]{:S(2)}, u32[]{:S(2)}) collective-permute-start(f32[512,768]{1,0:T(8,128)} %get-tuple-element.175), channel_id=1, source_target_pairs={{0,16},{16,0},{1,17},{17,1},{2,18},{18,2},{3,19},{19,3},{4,20},{20... | collective-permute-start | bytes 4718600 | tf_op jit(solution)/shard_map/ppermute | solution.py:846
  142.0 26.3 %collective-permute-start.17 = (bf16[4,48,1536]{2,1,0:T(8,128)(2,1)}, bf16[4,48,1536]{2,1,0:T(8,128)(2,1)}, u32[]{:S(2)}, u32[]{:S(2)}) collective-permute-start(bf16[4,48,1536]{2,1,0:T(8,128)(2,1)} %slice.156), channel_id=1, source_target_pairs={{0,1},{1,0},{2,3},{3,2},{4,5},{5,4},{6,7},{7,6},{8,9},{9,8},{10,11... | collective-permute-start | bytes 1769480 | tf_op jit(solution)/shard_map/ppermute | solution.py:860
  146.7 21.6 %collective-permute-start.16 = (bf16[4,48,1536]{2,1,0:T(8,128)(2,1)}, bf16[4,48,1536]{2,1,0:T(8,128)(2,1)}, u32[]{:S(2)}, u32[]{:S(2)}) collective-permute-start(bf16[4,48,1536]{2,1,0:T(8,128)(2,1)} %slice.155), channel_id=1, source_target_pairs={{0,2},{1,3},{2,0},{3,1},{4,6},{5,7},{6,4},{7,5},{8,10},{9,11},{10,... | collective-permute-start | bytes 1769480 | tf_op jit(solution)/shard_map/ppermute | solution.py:860
  148.5 19.8 %collective-permute-start.15 = (bf16[2,96,768]{2,1,0:T(8,128)(2,1)}, bf16[2,96,768]{2,1,0:T(8,128)(2,1)S(1)}, u32[]{:S(2)}, u32[]{:S(2)}) collective-permute-start(bf16[2,96,768]{2,1,0:T(8,128)(2,1)} %slice.154), channel_id=1, source_target_pairs={{0,2},{1,3},{2,0},{3,1},{4,6},{5,7},{6,4},{7,5},{8,10},{9,11},{10,... | collective-permute-start | bytes 884744 | tf_op jit(solution)/shard_map/ppermute | solution.py:860
  169.7 23.1 %collective-permute-start.21 = (bf16[2,48,1536]{2,1,0:T(8,128)(2,1)S(1)}, bf16[2,48,1536]{2,1,0:T(8,128)(2,1)S(1)}, u32[]{:S(2)}, u32[]{:S(2)}) collective-permute-start(bf16[2,48,1536]{2,1,0:T(8,128)(2,1)S(1)} %slice.162), channel_id=1, source_target_pairs={{0,8},{1,9},{2,10},{3,11},{4,12},{5,13},{6,14},{7,15},{8,0},{9,1},... | collective-permute-start | bytes 884744 | tf_op jit(solution)/shard_map/ppermute | solution.py:860
  172.7 20.1 %collective-permute-start.20 = (bf16[1,96,768]{2,1,0:T(8,128)(2,1)S(1)}, bf16[1,96,768]{2,1,0:T(8,128)(2,1)S(1)}, u32[]{:S(2)}, u32[]{:S(2)}) collective-permute-start(bf16[1,96,768]{2,1,0:T(8,128)(2,1)S(1)} %slice.160), channel_id=1, source_target_pairs={{0,8},{1,9},{2,10},{3,11},{4,12},{5,13},{6,14},{7,15},{8,0},{9,1},... | collective-permute-start | bytes 442376 | tf_op jit(solution)/shard_map/ppermute | solution.py:860
  174.2 18.6 %collective-permute-start.22 = (bf16[2,48,1536]{2,1,0:T(8,128)(2,1)S(1)}, bf16[2,48,1536]{2,1,0:T(8,128)(2,1)S(1)}, u32[]{:S(2)}, u32[]{:S(2)}) collective-permute-start(bf16[2,48,1536]{2,1,0:T(8,128)(2,1)S(1)} %slice.163), channel_id=1, source_target_pairs={{0,2},{1,3},{2,0},{3,1},{4,6},{5,7},{6,4},{7,5},{8,10},{9,11},{10,... | collective-permute-start | bytes 884744 | tf_op jit(solution)/shard_map/ppermute | solution.py:860
  176.1 22.7 %collective-permute-start.18 = (bf16[512,768]{1,0:T(8,128)(2,1)S(1)}, bf16[512,768]{1,0:T(8,128)(2,1)S(1)}, u32[]{:S(2)}, u32[]{:S(2)}) collective-permute-start(bf16[512,768]{1,0:T(8,128)(2,1)S(1)} %get-tuple-element.210), channel_id=1, source_target_pairs={{0,16},{16,0},{1,17},{17,1},{2,18},{18,2},{3,19},{19,3},{4,20},{20... | collective-permute-start | bytes 2359304 | tf_op jit(solution)/shard_map/ppermute | solution.py:846
  195.1 21.6 %collective-permute-start.23 = (bf16[1,96,768]{2,1,0:T(8,128)(2,1)S(1)}, bf16[1,96,768]{2,1,0:T(8,128)(2,1)S(1)}, u32[]{:S(2)}, u32[]{:S(2)}) collective-permute-start(bf16[1,96,768]{2,1,0:T(8,128)(2,1)S(1)} %get-tuple-element.206), channel_id=1, source_target_pairs={{0,8},{1,9},{2,10},{3,11},{4,12},{5,13},{6,14},{7,15},{8,0},{9,1},... | collective-permute-start | bytes 442376 | tf_op jit(solution)/shard_map/ppermute | solution.py:860
  198.7 29.5 %collective-permute-start.25 = (bf16[1,48,1536]{2,1,0:T(8,128)(2,1)S(1)}, bf16[1,48,1536]{2,1,0:T(8,128)(2,1)S(1)}, u32[]{:S(2)}, u32[]{:S(2)}) collective-permute-start(bf16[1,48,1536]{2,1,0:T(8,128)(2,1)S(1)} %slice.167), channel_id=1, source_target_pairs={{0,8},{1,9},{2,10},{3,11},{4,12},{5,13},{6,14},{7,15},{8,0},{9,1},... | collective-permute-start | bytes 442376 | tf_op jit(solution)/shard_map/ppermute | solution.py:860
  231.0 8.9 %collective-permute-start.31 = (bf16[1,48,1536]{2,1,0:T(8,128)(2,1)S(1)}, bf16[1,48,1536]{2,1,0:T(8,128)(2,1)S(1)}, u32[]{:S(2)}, u32[]{:S(2)}) collective-permute-start(bf16[1,48,1536]{2,1,0:T(8,128)(2,1)S(1)} %get-tuple-element.204), channel_id=1, source_target_pairs={{0,4},{1,5},{2,6},{3,7},{4,0},{5,1},{6,2},{7,3},{8,12},{9,13},{10,... | collective-permute-start | bytes 442376 | tf_op jit(solution)/shard_map/ppermute | solution.py:860
  235.1 14.7 %collective-permute-start.29 = (bf16[4,96,768]{2,1,0:T(8,128)(2,1)S(1)}, bf16[4,96,768]{2,1,0:T(8,128)(2,1)S(1)}, u32[]{:S(2)}, u32[]{:S(2)}) collective-permute-start(bf16[4,96,768]{2,1,0:T(8,128)(2,1)S(1)} %pad_maximum_fusion.4), channel_id=1, source_target_pairs={{0,4},{1,5},{2,6},{3,7},{4,0},{5,1},{6,2},{7,3},{8,12},{9,13},{10,... | collective-permute-start | bytes 1769480 | tf_op jit(solution)/shard_map/ppermute | solution.py:860
  235.9 16.7 %collective-permute-start.26 = (bf16[1,48,1536]{2,1,0:T(8,128)(2,1)S(1)}, bf16[1,48,1536]{2,1,0:T(8,128)(2,1)S(1)}, u32[]{:S(2)}, u32[]{:S(2)}) collective-permute-start(bf16[1,48,1536]{2,1,0:T(8,128)(2,1)S(1)} %get-tuple-element.208), channel_id=1, source_target_pairs={{0,8},{1,9},{2,10},{3,11},{4,12},{5,13},{6,14},{7,15},{8,0},{9,1},... | collective-permute-start | bytes 442376 | tf_op jit(solution)/shard_map/ppermute | solution.py:860
  240.0 14.0 %collective-permute-start.32 = (bf16[2,48,1536]{2,1,0:T(8,128)(2,1)S(1)}, bf16[2,48,1536]{2,1,0:T(8,128)(2,1)S(1)}, u32[]{:S(2)}, u32[]{:S(2)}) collective-permute-start(bf16[2,48,1536]{2,1,0:T(8,128)(2,1)S(1)} %pad_maximum_fusion.8), channel_id=1, source_target_pairs={{0,8},{1,9},{2,10},{3,11},{4,12},{5,13},{6,14},{7,15},{8,0},{9,1},... | collective-permute-start | bytes 884744 | tf_op jit(solution)/shard_map/ppermute | solution.py:860
  250.9 22.8 %collective-permute-start.30 = (bf16[8,96,768]{2,1,0:T(8,128)(2,1)}, bf16[8,96,768]{2,1,0:T(8,128)(2,1)}, u32[]{:S(2)}, u32[]{:S(2)}) collective-permute-start(bf16[8,96,768]{2,1,0:T(8,128)(2,1)} %pad_maximum_fusion), channel_id=1, source_target_pairs={{0,1},{1,0},{2,3},{3,2},{4,5},{5,4},{6,7},{7,6},{8,9},{9,8},{10,11... | collective-permute-start | bytes 3538952 | tf_op jit(solution)/shard_map/ppermute | solution.py:860
  252.6 10.0 %collective-permute-start.27 = (bf16[2,48,1536]{2,1,0:T(8,128)(2,1)S(1)}, bf16[2,48,1536]{2,1,0:T(8,128)(2,1)S(1)}, u32[]{:S(2)}, u32[]{:S(2)}) collective-permute-start(bf16[2,48,1536]{2,1,0:T(8,128)(2,1)S(1)} %pad_maximum_fusion.6), channel_id=1, source_target_pairs={{0,2},{1,3},{2,0},{3,1},{4,6},{5,7},{6,4},{7,5},{8,10},{9,11},{10,... | collective-permute-start | bytes 884744 | tf_op jit(solution)/shard_map/ppermute | solution.py:860
  254.9 14.5 %collective-permute-start.33 = (bf16[4,48,1536]{2,1,0:T(8,128)(2,1)}, bf16[4,48,1536]{2,1,0:T(8,128)(2,1)}, u32[]{:S(2)}, u32[]{:S(2)}) collective-permute-start(bf16[4,48,1536]{2,1,0:T(8,128)(2,1)} %pad_maximum_fusion.5), channel_id=1, source_target_pairs={{0,2},{1,3},{2,0},{3,1},{4,6},{5,7},{6,4},{7,5},{8,10},{9,11},{10,... | collective-permute-start | bytes 1769480 | tf_op jit(solution)/shard_map/ppermute | solution.py:860
  263.5 10.2 %collective-permute-start.34 = (bf16[4,48,1536]{2,1,0:T(8,128)(2,1)}, bf16[4,48,1536]{2,1,0:T(8,128)(2,1)}, u32[]{:S(2)}, u32[]{:S(2)}) collective-permute-start(bf16[4,48,1536]{2,1,0:T(8,128)(2,1)} %pad_maximum_fusion.3), channel_id=1, source_target_pairs={{0,1},{1,0},{2,3},{3,2},{4,5},{5,4},{6,7},{7,6},{8,9},{9,8},{10,11... | collective-permute-start | bytes 1769480 | tf_op jit(solution)/shard_map/ppermute | solution.py:860
  276.6 28.5 %collective-permute-start.37 = (bf16[8,48,1536]{2,1,0:T(8,128)(2,1)S(1)}, bf16[8,48,1536]{2,1,0:T(8,128)(2,1)S(1)}, u32[]{:S(2)}, u32[]{:S(2)}) collective-permute-start(bf16[8,48,1536]{2,1,0:T(8,128)(2,1)S(1)} %pad_maximum_fusion.2), channel_id=1, source_target_pairs={{0,4},{1,5},{2,6},{3,7},{4,0},{5,1},{6,2},{7,3},{8,12},{9,13},{10,... | collective-permute-start | bytes 3538952 | tf_op jit(solution)/shard_map/ppermute | solution.py:860
  277.8 27.2 %collective-permute-start.36 = (bf16[8,48,1536]{2,1,0:T(8,128)(2,1)S(1)}, bf16[8,48,1536]{2,1,0:T(8,128)(2,1)S(1)}, u32[]{:S(2)}, u32[]{:S(2)}) collective-permute-start(bf16[8,48,1536]{2,1,0:T(8,128)(2,1)S(1)} %pad_maximum_fusion.1), channel_id=1, source_target_pairs={{0,1},{1,0},{2,3},{3,2},{4,5},{5,4},{6,7},{7,6},{8,9},{9,8},{10,11... | collective-permute-start | bytes 3538952 | tf_op jit(solution)/shard_map/ppermute | solution.py:860
  (31 other events, 175.1 us)
Sparse Core Ops, SparseCore 0:
  148.9 84.9 all-gather.2

commit v3 on v2

--- a/solution.py
+++ b/solution.py
@@ -18,9 +18,9 @@
 STRIP = 512
 GROUP = 16
 ROW_TILE = 16
-ORDERS = (((1, 4, 2, 8), (2, 8, 1, 4)), ((1, 2, 8, 4), (2, 1, 4, 8)), ((4, 1, 2, 8), (8, 2, 1, 4)))
+ORDERS = (((2, 1, 8, 4), (1, 4, 2, 8)), ((8, 1, 2, 4), (2, 4, 8, 1)), ((1, 2, 4, 8), (2, 1, 8, 4)))
 SWAP = ((0, 1), (1, 0))
-KEY_SUMS, VALUE_SUMS, VECTORS, ACTS, INNERS, SMALLS, PAYLOAD = 0, 32, 64, 80, 88, 96, 112
+KEY_SUMS, VALUE_SUMS, VECTORS, ACTS, INNERS, FACTORS = 0, 24, 48, 64, 72, 80
 V_OUTER, V_NORMED, V_CONTEXT, V_PROJ, V_INPUT, V_GQUERY, V_QUERY, V_GCONTEXT = range(8)
 
 
@@ -94,6 +94,7 @@
 
 
 FAR = pl.BlockSpec(memory_space=pltpu.HBM)
+ANYWHERE = pl.BlockSpec(memory_space=pl.ANY)
 SCALARS = pl.BlockSpec(memory_space=pltpu.SMEM)
 NEAR = pl.BlockSpec(memory_space=pltpu.VMEM)
 
@@ -179,7 +180,7 @@
             ],
         ),
         out_shape=[struct((length, wide), BF)] * 2 + [struct((ROW_TILE, width), F32)],
-        compiler_params=params_of(16),
+        compiler_params=params_of(50),
         cost_estimate=cost(6),
         name="qkv",
     )(info, *far(inputs, weight, *vectors))
@@ -206,10 +207,18 @@
     return jnp.where(rows == 0, first, jnp.where(rows == 1, second, zero))
 
 
+def kept_places(width, ff, length):
+    sizes = (("n1", width), ("n2", width), ("context", width), ("acts", ff), ("slope", ff), ("probs", 2 * length))
+    places, start = {}, 0
+    for name, size in sizes + (("r1", PAIR), ("r2", PAIR)):
+        places[name] = (start, size)
+        start += size
+    return places
+
+
 def head_kernel(
     info_ref, own_ref, other_ref, wp_ref, wi_ref, wo_ref, table,
-    e_ref, probs_ref, c_ref, n1_ref, r1_ref, a_ref, slope_ref, n2_ref, r2_ref,
-    wp, wi, wo, sems,
+    e_ref, kept_ref, acts, wp, wi, wo, sems,
 ):
     copies = [
         pltpu.make_async_copy(wp_ref, wp, sems.at[0]),
@@ -221,6 +230,12 @@
     pick = layer_vectors(table, table, info_ref[0] == 0)
     width, ff = wi.shape
     length = own_ref.shape[0]
+    places = kept_places(width, ff, length)
+
+    def put(name, value, offset=0):
+        start = places[name][0] + offset
+        kept_ref[:, start : start + value.shape[1]] = value.astype(F32)
+
     lane = lax.broadcasted_iota(jnp.int32, (ROW_TILE, length), 1)
     contexts = []
     for i, ref in enumerate((own_ref, other_ref)):
@@ -229,54 +244,55 @@
         scores = jnp.where(lane < info_ref[1 + i], scores, BIG_NEG)
         raised = jnp.exp(scores - jnp.max(scores, axis=-1, keepdims=True))
         probs = raised / jnp.sum(raised, axis=-1, keepdims=True)
-        probs_ref[i] = probs
+        put("probs", probs, i * length)
         contexts.append(heads_of(nn(probs.astype(BF), ref[:, 2 * width : 3 * width])))
     context = two_rows(*contexts).astype(BF)
-    c_ref[...] = context
+    put("context", context)
     inputs = two_rows(own_ref[0:1, 3 * width :], other_ref[0:1, 3 * width :])
     copies[0].wait()
     n1, r1 = row_norm(inputs.astype(F32) + (nn(context, wp[...]) + pick(PROJ_B)))
-    n1_ref[...] = n1
-    r1_ref[...] = r1
+    put("n1", n1)
+    put("r1", r1)
     normed = n1 * pick(ATTN_G) + pick(ATTN_B)
     copies[1].wait()
     low = normed.astype(BF)
     for c in range(ff // width):
         cols = slice(c * width, (c + 1) * width)
         act, slope = gelu_pair(nn(low, wi[:, cols]) + pick(INNER_B, c))
-        a_ref[:, cols] = act.astype(BF)
-        slope_ref[:, cols] = slope
+        act = act.astype(BF)
+        acts[:, cols] = act
+        put("acts", act, c * width)
+        put("slope", slope, c * width)
     copies[2].wait()
-    n2, r2 = row_norm(normed + (nn(a_ref[...], wo[...]) + pick(OUTER_B)))
-    n2_ref[...] = n2
-    r2_ref[...] = r2
+    n2, r2 = row_norm(normed + (nn(acts[...], wo[...]) + pick(OUTER_B)))
+    put("n2", n2)
+    put("r2", r2)
     e_ref[...] = (n2 * pick(FFN_G) + pick(FFN_B)).astype(BF)
 
 
 def head_call(info, own, other, wp, wi, wo, table):
     length = own.shape[0]
     width, ff = wi.shape
-    shapes = [
-        struct((ROW_TILE, width), BF),
-        struct((2, ROW_TILE, length), F32),
-        struct((ROW_TILE, width), BF),
-        struct((ROW_TILE, width), F32),
-        struct((ROW_TILE, 1), F32),
-        struct((ROW_TILE, ff), BF),
-        struct((ROW_TILE, ff), F32),
-        struct((ROW_TILE, width), F32),
-        struct((ROW_TILE, 1), F32),
-    ]
+    kept = max(place + size for place, size in kept_places(width, ff, length).values())
+    shapes = [struct((ROW_TILE, width), BF), struct((ROW_TILE, kept), F32)]
     return pl.pallas_call(
         head_kernel,
         in_specs=[SCALARS, NEAR, NEAR, FAR, FAR, FAR, NEAR],
         out_specs=[NEAR] * len(shapes),
         out_shape=shapes,
-        scratch_shapes=[pltpu.VMEM(w.shape, BF) for w in (wp, wi, wo)] + [pltpu.SemaphoreType.DMA((3,))],
-        compiler_params=params_of(24),
+        scratch_shapes=[pltpu.VMEM((ROW_TILE, ff), BF)]
+        + [pltpu.VMEM(w.shape, BF) for w in (wp, wi, wo)]
+        + [pltpu.SemaphoreType.DMA((3,))],
+        compiler_params=params_of(22),
         cost_estimate=cost(7),
         name="head_rows",
     )(info, own, other, *far(wp, wi, wo), table)
+
+
+def replace_first(xq, fixed):
+    top_rows = xq[0:ROW_TILE, :]
+    at_first = lax.broadcasted_iota(jnp.int32, top_rows.shape, 0) == 0
+    xq[0:ROW_TILE, :] = jnp.where(at_first, fixed, top_rows)
 
 
 def attention_parts(xq, j, width, lane, bias_col):
@@ -301,79 +317,104 @@
         ref[jnp.bitwise_xor(p, order)] = value[p * rows : (p + 1) * rows, :]
 
 
-def forward_kernel(train, info_ref, *refs):
-    xq_a, xq_b, wq_a, wq_b, wp_a, wp_b, wi_a, wi_b, wo_a, wo_b, mine, table = refs[:12]
-    if train:
-        head_ref, arrived_ref, cot_ref = refs[12:15]
-        (z_ref, xq, wp, wi, wo, ctx, lse_ref, n1_ref, r1_ref, slope_ref, gf_ref, sg_ref, small_ref, keep_ref, send_ref) = refs[15:30]
-        wq, lse_scr, acts, cot, sems = refs[30:]
-    else:
-        z_ref, xq, wp, wi, wo, ctx, sems = refs[12:]
-    section = info_ref[0]
-    own = section == (1 if train else 0)
-    fetch(own, xq_a, xq_b, xq, sems.at[0])
-    if train:
-        fetch(own, wq_a, wq_b, wq, sems.at[1])
-        pltpu.make_async_copy(cot_ref.at[section], cot, sems.at[5]).start()
-    fetch(own, wp_a, wp_b, wp, sems.at[2])
-    width = wp.shape[0]
-    length = xq.shape[0]
-    ff = wi.shape[1]
-    pick = layer_vectors(mine, table, own)
-    count = info_ref[1]
-    row = lax.broadcasted_iota(jnp.int32, (length, PAIR), 0)
-    lane = lax.broadcasted_iota(jnp.int32, (length, PAIR), 1)
-    bias_col = jnp.where(row < count, 0.0, BIG_NEG).astype(BF)
-    if train:
-        first = jnp.where(section == 0, head_ref[0:1, :], arrived_ref[1:2, :])
-        many = jnp.broadcast_to(first, (ROW_TILE, width))
-        landed(wq_a, wq, sems.at[1])
-        fixed = []
-        for k, shift in enumerate((pick(QUERY_B), None, pick(VALUE_B))):
-            made = nn(many, wq[:, k * width : (k + 1) * width])
-            fixed.append((made if shift is None else made + shift).astype(BF))
-        fixed = jnp.concatenate(fixed + [many], axis=1)
-    landed(xq_a, xq, sems.at[0])
-    fetch(own, wi_a, wi_b, wi, sems.at[3])
-    fetch(own, wo_a, wo_b, wo, sems.at[4])
-    if train:
-        top_rows = xq[0:ROW_TILE, :]
-        at_first = lax.broadcasted_iota(jnp.int32, top_rows.shape, 0) == 0
-        xq[0:ROW_TILE, :] = jnp.where(at_first, fixed, top_rows)
-
+def attend(xq, ctx, lse_scr, width, lane, bias_col):
     def pair_body(j, carry):
         base, q, k, v, parts = attention_parts(xq, j, width, lane, bias_col)
         sides = []
         for h, (mine, qh, kh) in enumerate(parts):
             vh = jnp.where(mine, v, jnp.ones_like(v))
-            for s in range(length // STRIP):
-                rows = slice(s * STRIP, (s + 1) * STRIP)
-                scores = nt(qh[rows, :], kh)
-                top = jnp.max(scores, axis=-1, keepdims=True)
-                made = nn(jnp.exp(scores - top).astype(BF), vh)
-                mass = made[:, HEAD_DIM * (1 - h) : HEAD_DIM * (1 - h) + 1]
-                sides.append(made * (1.0 / mass))
-                if train:
-                    spot = lane[rows, :] == 2 * j + h
-                    lse_scr[rows, :] = jnp.where(spot, top + jnp.log(mass), lse_scr[rows, :])
-        count_strips = length // STRIP
-        for s in range(count_strips):
-            rows = slice(s * STRIP, (s + 1) * STRIP)
-            both = jnp.where(lane[rows, :] < HEAD_DIM, sides[s], sides[count_strips + s])
-            ctx[rows, pl.ds(base, PAIR)] = both.astype(BF)
+            scores = nt(qh, kh)
+            top = jnp.max(scores, axis=-1, keepdims=True)
+            made = nn(jnp.exp(scores - top).astype(BF), vh)
+            mass = made[:, HEAD_DIM * (1 - h) : HEAD_DIM * (1 - h) + 1]
+            sides.append(made * (1.0 / mass))
+            if lse_scr is not None:
+                lse_scr[...] = jnp.where(lane == 2 * j + h, top + jnp.log(mass), lse_scr[...])
+        ctx[:, pl.ds(base, PAIR)] = jnp.where(lane < HEAD_DIM, sides[0], sides[1]).astype(BF)
         return carry
 
     lax.fori_loop(0, HEADS // 2, pair_body, 0)
-    if train:
-        lse_ref[...] = jnp.transpose(lse_scr[...])[0:ROW_TILE, :]
-    inputs = xq[:, 3 * width :]
+
+
+def mixing_kernel(info_ref, xq_a, xq_b, wp_a, wp_b, mine, table, normed_ref, xq, wp, ctx, sems):
+    own = info_ref[0] == 0
+    fetch(own, xq_a, xq_b, xq, sems.at[0])
+    fetch(own, wp_a, wp_b, wp, sems.at[1])
+    width = wp.shape[0]
+    length = xq.shape[0]
+    pick = layer_vectors(mine, table, own)
+    lane = lax.broadcasted_iota(jnp.int32, (length, PAIR), 1)
+    row = lax.broadcasted_iota(jnp.int32, (length, PAIR), 0)
+    bias_col = jnp.where(row < info_ref[1], 0.0, BIG_NEG).astype(BF)
+    landed(xq_a, xq, sems.at[0])
+    attend(xq, ctx, None, width, lane, bias_col)
+    landed(wp_a, wp, sems.at[1])
+    n1, r1 = row_norm(xq[:, 3 * width :].astype(F32) + (nn(ctx[...], wp[...]) + pick(PROJ_B)))
+    normed_ref[...] = n1 * pick(ATTN_G) + pick(ATTN_B)
+
+
+def mixing_call(info, xq, wp, tables):
+    length = xq[0].shape[0]
+    width = wp[0].shape[0]
+    return pl.pallas_call(
+        mixing_kernel,
+        in_specs=[SCALARS] + [FAR] * 4 + [NEAR] * 2,
+        out_specs=NEAR,
+        out_shape=struct((length, width), F32),
+        scratch_shapes=[
+            pltpu.VMEM(xq[0].shape, BF),
+            pltpu.VMEM(wp[0].shape, BF),
+            pltpu.VMEM((length, width), BF),
+            pltpu.SemaphoreType.DMA((2,)),
+        ],
+        compiler_params=params_of(16),
+        cost_estimate=cost(10),
+        name="mixing",
+    )(info, *far(*xq, *wp), *tables)
+
+
+def train_kernel(
+    info_ref, xq_a, xq_b, wq_a, wq_b, wp_a, wp_b, wi_a, wi_b, wo_a, wo_b, mine, table, head_ref, arrived_ref, cot_ref,
+    z_ref, wp, wi, wo, ctx, lse_ref, fixed_ref, n1_ref, r1_ref, slope_ref, gf_ref, sg_ref, small_ref, keep_ref, send_ref,
+    xq, lse_scr, sems,
+):
+    section = info_ref[0]
+    own = section == 1
+    fetch(own, xq_a, xq_b, xq, sems.at[0])
+    width = wp.shape[0]
+    length = xq.shape[0]
+    ff = wi.shape[1]
+    thirds = [(pl.ds(k * width, width), wo.at[pl.ds(k * width, width)]) for k in range(3)]
+    for k, (cols, place) in enumerate(thirds):
+        fetch(own, wq_a.at[:, cols], wq_b.at[:, cols], place, sems.at[5 + k])
+    fetch(own, wp_a, wp_b, wp, sems.at[2])
+    pick = layer_vectors(mine, table, own)
+    lane = lax.broadcasted_iota(jnp.int32, (length, PAIR), 1)
+    row = lax.broadcasted_iota(jnp.int32, (length, PAIR), 0)
+    bias_col = jnp.where(row < info_ref[1], 0.0, BIG_NEG).astype(BF)
+    many = jnp.broadcast_to(jnp.where(section == 0, head_ref[0:1, :], arrived_ref[1:2, :]), (ROW_TILE, width))
+    fixed = []
+    for k, shift in enumerate((pick(QUERY_B), None, pick(VALUE_B))):
+        cols, place = thirds[k]
+        landed(wq_a.at[:, cols], place, sems.at[5 + k])
+        made = nn(many, place[...])
+        fixed.append((made if shift is None else made + shift).astype(BF))
+    fixed = jnp.concatenate(fixed + [many], axis=1)
+    fixed_ref[...] = fixed
+    landed(xq_a, xq, sems.at[0])
+    fetch(own, wi_a, wi_b, wi, sems.at[3])
+    fetch(own, wo_a, wo_b, wo, sems.at[4])
+    copy = pltpu.make_async_copy(cot_ref.at[section], gf_ref, sems.at[1])
+    copy.start()
+    replace_first(xq, fixed)
+    attend(xq, ctx, lse_scr, width, lane, bias_col)
+    lse_ref[...] = jnp.transpose(lse_scr[...])[0:ROW_TILE, :]
     landed(wp_a, wp, sems.at[2])
-    n1, r1 = row_norm(inputs.astype(F32) + (nn(ctx[...], wp[...]) + pick(PROJ_B)))
+    n1, r1 = row_norm(xq[:, 3 * width :].astype(F32) + (nn(ctx[...], wp[...]) + pick(PROJ_B)))
+    n1_ref[...] = n1
+    r1_ref[...] = r1
     normed = n1 * pick(ATTN_G) + pick(ATTN_B)
     low = normed.astype(BF)
-    if train:
-        n1_ref[...] = n1
-        r1_ref[...] = r1
     landed(wi_a, wi, sems.at[3])
     landed(wo_a, wo, sems.at[4])
     total = None
@@ -381,19 +422,16 @@
         cols = slice(c * CHUNK, (c + 1) * CHUNK)
         act, slope = gelu_pair(nn(low, wi[:, cols]) + pick(INNER_B, c))
         act = act.astype(BF)
-        if train:
-            acts[:, cols] = act
-            slope_ref[:, cols] = slope.astype(BF)
+        xq[:, cols] = act
+        slope_ref[:, cols] = slope.astype(BF)
         term = nn(act, wo[cols, :])
         total = term if total is None else total + term
     n2, r2 = row_norm(normed + (total + pick(OUTER_B)))
     gain = pick(FFN_G)
     z_ref[...] = (n2 * gain + pick(FFN_B)).astype(BF)
-    if not train:
-        return
     wide_row = lax.broadcasted_iota(jnp.int32, n2.shape, 0)
-    pltpu.make_async_copy(cot_ref.at[section], cot, sems.at[5]).wait()
-    grad = jnp.where(wide_row < count, cot[...].astype(F32), 0.0)
+    copy.wait()
+    grad = jnp.where(wide_row < info_ref[1], gf_ref[...].astype(F32), 0.0)
     second = norm_back(grad, n2, r2, gain)
     sg_ref[...] = second
     gf = second.astype(BF)
@@ -407,51 +445,84 @@
     for ref, half, order in ((send_ref, 1 - section, info_ref[4]), (keep_ref, section, info_ref[3])):
         for c in range(half_chunks):
             cols = pl.ds(pl.multiple_of((half * half_chunks + c) * CHUNK, CHUNK), CHUNK)
-            made = tn(acts[:, cols], gf).astype(BF)
+            made = tn(xq[:, cols], gf).astype(BF)
             for p in range(each):
                 ref[jnp.bitwise_xor(c * each + p, order)] = made[p * rows : (p + 1) * rows, :]
 
 
-def forward_call(train, info, pairs, tables, head=None, arrived=None, cot=None):
+def train_call(info, pairs, tables, head, arrived, cot):
     xq, wq, wp, wi, wo = (piece[0] for piece in pairs)
     length = xq.shape[0]
     width, ff = wi.shape
-    flat = [piece for pair in pairs for piece in pair]
-    args = [info] + list(far(*flat)) + list(tables)
-    in_specs = [SCALARS] + [FAR] * 10 + [NEAR] * 2
-    weights = [near(w.shape, BF) for w in (wp, wi, wo)]
-    if train:
-        args += [head, arrived] + list(far(cot))
-        in_specs += [NEAR, NEAR, FAR]
-        shapes = [struct((length, width), BF), near(xq.shape, BF)] + weights
-        shapes += [
-            near((length, width), BF),
-            near((ROW_TILE, length), F32),
-            near((length, width), F32),
-            near((length, 1), F32),
-            near((length, ff), BF),
-            near((length, width), BF),
-            near((length, width), F32),
-            near((8, width), F32),
-            near((GROUP, ff // 2 // GROUP, width), BF),
-            near((GROUP, ff // 2 // GROUP, width), BF),
-        ]
-        scratch = [pltpu.VMEM(wq.shape, BF), pltpu.VMEM((length, PAIR), F32), pltpu.VMEM((length, ff), BF)]
-        scratch.append(pltpu.VMEM((length, width), BF))
-    else:
-        shapes = [struct((length, width), BF)]
-        scratch = [pltpu.VMEM(xq.shape, BF)] + weights + [pltpu.VMEM((length, width), BF)]
-    scratch.append(pltpu.SemaphoreType.DMA((6,)))
+    args = [info]
+    in_specs = [SCALARS]
+    for pair in pairs:
+        args += far(*pair)
+        in_specs += [FAR, FAR]
+    args += [*tables, head, arrived, *far(cot)]
+    shapes = [
+        struct((length, width), BF),
+        near(wp.shape, BF),
+        near(wi.shape, BF),
+        near(wo.shape, BF),
+        near((length, width), BF),
+        near((ROW_TILE, length), F32),
+        near((ROW_TILE, 4 * width), BF),
+        near((length, width), F32),
+        near((length, 1), F32),
+        near((length, ff), BF),
+        near((length, width), BF),
+        near((length, width), F32),
+        near((8, width), F32),
+        near((GROUP, ff // 2 // GROUP, width), BF),
+        near((GROUP, ff // 2 // GROUP, width), BF),
+    ]
     return pl.pallas_call(
-        lambda *refs: forward_kernel(train, *refs),
-        in_specs=in_specs,
+        train_kernel,
+        in_specs=in_specs + [NEAR] * 4 + [FAR],
         out_specs=[NEAR] * len(shapes),
         out_shape=shapes,
-        scratch_shapes=scratch,
-        compiler_params=params_of(20 if train else 24),
-        cost_estimate=cost(26 if train else 19),
-        name="layer_train" if train else "layer",
+        scratch_shapes=[
+            pltpu.VMEM(xq.shape, BF),
+            pltpu.VMEM((length, PAIR), F32),
+            pltpu.SemaphoreType.DMA((8,)),
+        ],
+        compiler_params=params_of(14),
+        cost_estimate=cost(26),
+        name="layer_train",
     )(*args)
+
+
+def feed_kernel(info_ref, normed_ref, wi_a, wi_b, wo_a, wo_b, mine, other, z_ref, wi, wo, sems):
+    own = info_ref[0] == 0
+    fetch(own, wi_a, wi_b, wi, sems.at[0])
+    fetch(own, wo_a, wo_b, wo, sems.at[1])
+    pick = layer_vectors(mine, other, own)
+    normed = normed_ref[...]
+    low = normed.astype(BF)
+    landed(wi_a, wi, sems.at[0])
+    landed(wo_a, wo, sems.at[1])
+    total = None
+    for c in range(wi.shape[1] // CHUNK):
+        cols = slice(c * CHUNK, (c + 1) * CHUNK)
+        act, slope = gelu_pair(nn(low, wi[:, cols]) + pick(INNER_B, c))
+        term = nn(act.astype(BF), wo[cols, :])
+        total = term if total is None else total + term
+    n2, r2 = row_norm(normed + (total + pick(OUTER_B)))
+    z_ref[...] = (n2 * pick(FFN_G) + pick(FFN_B)).astype(BF)
+
+
+def feed_call(info, normed, wi, wo, tables):
+    return pl.pallas_call(
+        feed_kernel,
+        in_specs=[SCALARS, NEAR] + [FAR] * 4 + [NEAR] * 2,
+        out_specs=NEAR,
+        out_shape=struct(normed.shape, BF),
+        scratch_shapes=[pltpu.VMEM(wi[0].shape, BF), pltpu.VMEM(wo[0].shape, BF), pltpu.SemaphoreType.DMA((2,))],
+        compiler_params=params_of(24),
+        cost_estimate=cost(11),
+        name="layer_feed",
+    )(info, normed, *far(*wi, *wo), *tables)
 
 
 def inner_kernel(
@@ -508,20 +579,24 @@
 
 
 def attention_kernel(
-    info_ref, xq, gc_ref, ga_ref, c_ref, lse_ref, keep_ref, send_ref, g_ref, small_ref, xt_scr, ct_scr, mean_scr
+    info_ref, xq_a, xq_b, fixed_ref, gc_ref, ga_ref, c_ref, lse_ref, keep_ref, send_ref, g_ref, small_ref,
+    xq, xt_scr, ct_scr, mean_scr, sem,
 ):
     section = info_ref[0]
+    fetch(section == 1, xq_a, xq_b, xq, sem)
     length, width = gc_ref.shape
     row = lax.broadcasted_iota(jnp.int32, (length, PAIR), 0)
     lane = lax.broadcasted_iota(jnp.int32, (length, PAIR), 1)
     bias_col = jnp.where(row < info_ref[1], 0.0, BIG_NEG).astype(BF)
     ct_scr[...] = turned(c_ref[...])
-    xt_scr[...] = turned(xq[:, 3 * width :])
     product = gc_ref[...].astype(F32) * c_ref[...].astype(F32)
     high = product.astype(BF)
     low = (product - high.astype(F32)).astype(BF)
     ones = by_head(jnp.ones((1, width), BF), ROW_TILE)
     mean_scr[...] = nt(ones, high) + nt(ones, low)
+    landed(xq_a, xq, sem)
+    replace_first(xq, fixed_ref[...])
+    xt_scr[...] = turned(xq[:, 3 * width :])
 
     def pair_body(j, carry):
         base, q, k, v, parts = attention_parts(xq, j, width, lane, bias_col)
@@ -566,7 +641,7 @@
         place_rows(ref.at[:, :, wide:], nn(ct_scr[...], ga_ref[:, cols]).astype(BF), order)
 
 
-def attention_call(info, xq, gc, ga, context, lse):
+def attention_call(info, xq, fixed, gc, ga, context, lse):
     length, width = gc.shape
     shapes = [
         near((GROUP, width // GROUP, 2 * width), BF),
@@ -576,18 +651,20 @@
     ]
     return pl.pallas_call(
         attention_kernel,
-        in_specs=[SCALARS] + [NEAR] * 5,
+        in_specs=[SCALARS, FAR, FAR] + [NEAR] * 5,
         out_specs=[NEAR] * len(shapes),
         out_shape=shapes,
         scratch_shapes=[
+            pltpu.VMEM(xq[0].shape, BF),
             pltpu.VMEM((width, length), BF),
             pltpu.VMEM((width, length), BF),
             pltpu.VMEM((ROW_TILE, length), F32),
+            pltpu.SemaphoreType.DMA(()),
         ],
-        compiler_params=params_of(16),
+        compiler_params=params_of(18),
         cost_estimate=cost(14),
         name="attention_grad",
-    )(info, *stay(xq, gc, ga, context, lse))
+    )(info, *far(*xq), *stay(fixed, gc, ga, context, lse))
 
 
 def input_kernel(info_ref, w_a, w_b, g_ref, gh_ref, small1_ref, small2_ref, small3_ref, o_ref, small_ref, w, sem):
@@ -615,8 +692,8 @@
 
 
 def head_back_kernel(
-    info_ref, small_a, small_b, probs_ref, c_ref, n1_ref, r1_ref, a_ref, slope_ref, n2_ref, r2_ref, own_ref, other_ref,
-    wq_ref, wp_ref, wi_ref, wo_ref, table, x_ref, pay_ref, wq, wp, wi, wo, sems,
+    info_ref, small_a, small_b, kept_ref, own_ref, other_ref,
+    wq_ref, wp_ref, wi_ref, wo_ref, table, x_ref, pay_ref, later_ref, sums_ref, wq, wp, wi, wo, sems,
 ):
     copies = [
         pltpu.make_async_copy(ref, scr, sems.at[i])
@@ -627,16 +704,23 @@
     width = wp.shape[0]
     length = own_ref.shape[0]
     ff = wi.shape[1]
-    n1, n2 = n1_ref[...], n2_ref[...]
+    places = kept_places(width, ff, length)
+
+    def kept(name, offset=0, size=None):
+        start = places[name][0] + offset
+        return kept_ref[:, start : start + (places[name][1] if size is None else size)]
+
+    n1, n2 = kept("n1"), kept("n2")
+    context = kept("context").astype(BF)
     pick = layer_vectors(table, table, info_ref[0] == 0)
     grad = two_rows(small_a[12:13, :], small_b[12:13, :]).astype(BF).astype(F32)
-    second = norm_back(grad, n2, r2_ref[...], pick(FFN_G))
+    second = norm_back(grad, n2, kept("r2", 0, 1), pick(FFN_G))
     gf = second.astype(BF)
     copies[0].wait()
-    gu = (nt(gf, wo[...]) * slope_ref[...]).astype(BF)
+    gu = (nt(gf, wo[...]) * kept("slope")).astype(BF)
     copies[1].wait()
     gn = second + nt(gu, wi[...])
-    gh = norm_back(gn, n1, r1_ref[...], pick(ATTN_G))
+    gh = norm_back(gn, n1, kept("r1", 0, 1), pick(ATTN_G))
     ga = gh.astype(BF)
     copies[2].wait()
     gc = nt(ga, wp[...]).astype(BF)
@@ -644,19 +728,19 @@
     copies[3].wait()
     query_bias = value_bias = jnp.zeros((1, width), F32)
     vectors = {}
+    sums_of = []
     for i, ref in enumerate((own_ref, other_ref)):
         mid = (1 - 2 * i) * info_ref[0] + i
         keys, values, inputs = ref[:, width : 2 * width], ref[:, 2 * width : 3 * width], ref[:, 3 * width :]
         query = ref[0:1, 0:width] * jnp.asarray(0.125, BF)
         gc_row = gc[i : i + 1, :]
         query_heads, gc_heads = by_head(query, ROW_TILE), by_head(gc_row, ROW_TILE)
-        probs = probs_ref[i]
+        probs = kept("probs", i * length, length)
         gp = nt(gc_heads, values)
         gs = (probs * (gp - jnp.sum(probs * gp, axis=-1, keepdims=True))).astype(BF)
         low = probs.astype(BF)
         gq = (heads_of(nn(gs, keys)) * 0.125).astype(BF)
-        pay_ref[KEY_SUMS + 16 * i : KEY_SUMS + 16 * i + 16, :] = nn(gs, inputs).astype(BF)
-        pay_ref[VALUE_SUMS + 16 * i : VALUE_SUMS + 16 * i + 16, :] = nn(low, inputs).astype(BF)
+        sums_of += [(KEY_SUMS + HEADS * i, nn(gs, inputs)), (VALUE_SUMS + HEADS * i, nn(low, inputs))]
         key_back = nt(query_heads, wq[:, width : 2 * width]).astype(BF)
         value_back = nt(gc_heads, wq[:, 2 * width :]).astype(BF)
         gx = tn(gs, key_back) + tn(low, value_back)
@@ -669,7 +753,7 @@
         for key, piece in (
             (V_OUTER, gf[i : i + 1, :]),
             (V_NORMED, normed[i : i + 1, :]),
-            (V_CONTEXT, c_ref[i : i + 1, :]),
+            (V_CONTEXT, context[i : i + 1, :]),
             (V_PROJ, ga[i : i + 1, :]),
             (V_INPUT, ref[0:1, 3 * width :]),
             (V_GQUERY, gq),
@@ -678,7 +762,7 @@
         ):
             vectors[2 * key + i] = piece
     gu_sum = col_sum(gu)
-    act = a_ref[...]
+    act = kept("acts").astype(BF)
     own_small = [query_bias, value_bias, col_sum(ga), col_sum(gn * n1), col_sum(gn)]
     own_small += [gu_sum[:, width * k : width * (k + 1)] for k in range(ff // width)]
     own_small += [col_sum(gf), col_sum(grad * n2), col_sum(grad)]
@@ -690,21 +774,28 @@
             made = jnp.where(row == k, piece.astype(F32), made)
         return made
 
-    pay_ref[VECTORS : VECTORS + 16, :] = stack([vectors[k] for k in range(16)]).astype(BF)
     wide = [value[i : i + 1, width * k : width * (k + 1)] for value in (act, gu) for i in range(2) for k in range(ff // width)]
-    pay_ref[ACTS : ACTS + 16, :] = stack(wide).astype(BF)
-    pay_ref[SMALLS : SMALLS + 16, :] = jnp.where(info_ref[0] == 0, stack(own_small), small_a[...] + small_b[...]).astype(BF)
-
-
-def head_back_call(info, small_a, small_b, saved, own, other, wq, wp, wi, wo, table):
+    rows = [value[h : h + 1, :] for place, value in sums_of for h in range(HEADS)]
+    rows = rows[0:HEADS] + rows[2 * HEADS : 3 * HEADS] + rows[HEADS : 2 * HEADS] + rows[3 * HEADS :]
+    rows += [vectors[k] for k in range(16)] + wide
+    half = FACTORS // 2
+    for ref, start in ((pay_ref, 0), (later_ref, half)):
+        for k in range(0, half, 8):
+            ref[k : k + 8, :] = stack(rows[start + k : start + k + 8])[0:8, :].astype(BF)
+    sums_ref[...] = jnp.where(info_ref[0] == 0, stack(own_small), small_a[...] + small_b[...]).astype(BF)
+
+
+def head_back_call(info, small_a, small_b, kept, own, other, wq, wp, wi, wo, table):
     length = own.shape[0]
     width, ff = wi.shape
-    args = [small_a, small_b] + list(saved) + [own, other]
+    args = [small_a, small_b, kept, own, other]
     return pl.pallas_call(
         head_back_kernel,
         in_specs=[SCALARS] + [NEAR] * len(args) + [FAR] * 4 + [NEAR],
-        out_specs=[NEAR] * 2,
-        out_shape=[struct((2, length, width), F32), struct((PAYLOAD, width), BF)],
+        out_specs=[NEAR] * 4,
+        out_shape=[struct((2, length, width), F32)]
+        + [struct((FACTORS // 2, width), BF)] * 2
+        + [struct((ROW_TILE, width), BF)],
         scratch_shapes=[pltpu.VMEM(w.shape, BF) for w in (wq, wp, wi, wo)] + [pltpu.SemaphoreType.DMA((4,))],
         compiler_params=params_of(28),
         cost_estimate=cost(12),
@@ -712,20 +803,21 @@
     )(info, *args, *far(wq, wp, wi, wo), table)
 
 
-def outer_final_kernel(info_ref, low_ref, high_ref, gt_ref, o_ref):
+def outer_final_kernel(info_ref, a_low, a_high, b_low, b_high, gt_ref, o_ref):
     step = pl.program_id(0)
-    rows = low_ref.shape[1]
+    rows = a_low.shape[1]
     each = o_ref.shape[0] // rows
     per_half = pl.num_programs(0) // 2
 
     @pl.when(info_ref[0] == 1)
     def _():
-        def fill(ref, first, order):
+        def fill(low, high, first, order):
             for p in range(each):
-                o_ref[p * rows : (p + 1) * rows, :] = ref[jnp.bitwise_xor(first + p, order)].astype(F32)
-
-        pl.when(step < per_half)(lambda: fill(low_ref, step * each, info_ref[4]))
-        pl.when(step >= per_half)(lambda: fill(high_ref, (step - per_half) * each, info_ref[3]))
+                piece = piece_at(low, high, jnp.bitwise_xor(first + p, order))
+                o_ref[p * rows : (p + 1) * rows, :] = piece.astype(F32)
+
+        pl.when(step < per_half)(lambda: fill(a_low, a_high, step * each, info_ref[4]))
+        pl.when(step >= per_half)(lambda: fill(b_low, b_high, (step - per_half) * each, info_ref[3]))
 
     @pl.when(info_ref[0] == 0)
     def _():
@@ -737,35 +829,42 @@
         o_ref[...] = made
 
 
-def outer_final_call(info, low, high, gt):
-    width = low.shape[2]
-    ff = 2 * low.shape[0] * low.shape[1]
+def outer_final_call(info, quarters, gt):
+    width = quarters[0].shape[2]
+    ff = 4 * quarters[0].shape[0] * quarters[0].shape[1]
     return pl.pallas_call(
         outer_final_kernel,
         grid=(ff // width,),
-        in_specs=[SCALARS, full(low.shape), full(high.shape), full(gt.shape)],
+        in_specs=[SCALARS] + [full(a.shape) for a in quarters] + [full(gt.shape)],
         out_specs=pl.BlockSpec((width, width), lambda i: (i, 0)),
         out_shape=struct((ff, width), F32),
         compiler_params=params_of(32),
         cost_estimate=cost(5),
         name="outer_final",
-    )(info, low, high, gt)
-
-
-def unfold(ref, cols, order, target):
-    rows = ref.shape[1]
-    for p in range(ref.shape[0]):
-        target[p * rows : (p + 1) * rows, :] = ref[jnp.bitwise_xor(p, order), :, cols].astype(F32)
-
-
-def inner_final_kernel(info_ref, low_ref, high_ref, gt_ref, o_ref):
+    )(info, *quarters, gt)
+
+
+def piece_at(low, high, place, cols=slice(None)):
+    half = low.shape[0]
+    inside = lax.rem(place, half)
+    return jnp.where(place < half, low[inside, :, cols], high[inside, :, cols])
+
+
+def unfold(halves, cols, order, target):
+    low, high = halves
+    rows = low.shape[1]
+    for p in range(GROUP):
+        target[p * rows : (p + 1) * rows, :] = piece_at(low, high, jnp.bitwise_xor(p, order), cols).astype(F32)
+
+
+def inner_final_kernel(info_ref, a_low, a_high, b_low, b_high, gt_ref, o_ref):
     step = pl.program_id(0)
     width = o_ref.shape[1]
 
     @pl.when(info_ref[0] == 1)
     def _():
         for k in range(4):
-            ref, order = ((low_ref, info_ref[6]), (high_ref, info_ref[5]))[k // 2]
+            ref, order = (((a_low, a_high), info_ref[6]), ((b_low, b_high), info_ref[5]))[k // 2]
             cols = slice((k % 2) * width, (k % 2 + 1) * width)
             pl.when(step == k)(lambda ref=ref, order=order, cols=cols: unfold(ref, cols, order, o_ref))
 
@@ -778,29 +877,29 @@
         o_ref[...] = made
 
 
-def inner_final_call(info, low, high, gt):
+def inner_final_call(info, quarters, gt):
     width = gt.shape[2]
-    ff = 2 * low.shape[2]
+    ff = 2 * quarters[0].shape[2]
     return pl.pallas_call(
         inner_final_kernel,
         grid=(ff // width,),
-        in_specs=[SCALARS, full(low.shape), full(high.shape), full(gt.shape)],
+        in_specs=[SCALARS] + [full(a.shape) for a in quarters] + [full(gt.shape)],
         out_specs=pl.BlockSpec((width, width), lambda i: (0, i)),
         out_shape=struct((width, ff), F32),
         compiler_params=params_of(32),
         cost_estimate=cost(5),
         name="inner_final",
-    )(info, low, high, gt)
-
-
-def qkv_final_kernel(info_ref, low_ref, high_ref, gt_ref, o_ref, p_ref):
+    )(info, *quarters, gt)
+
+
+def qkv_final_kernel(info_ref, a_low, a_high, b_low, b_high, gt_ref, o_ref, p_ref):
     width = p_ref.shape[0]
     wide = 3 * width // 2
     half = width // 2
 
     @pl.when(info_ref[0] == 1)
     def _():
-        for ref, order, k in ((low_ref, info_ref[8], 0), (high_ref, info_ref[7], 1)):
+        for ref, order, k in (((a_low, a_high), info_ref[8], 0), ((b_low, b_high), info_ref[7], 1)):
             unfold(ref, slice(0, wide), order, o_ref.at[:, k * wide : (k + 1) * wide])
             unfold(ref, slice(wide, wide + half), order, p_ref.at[:, k * half : (k + 1) * half])
 
@@ -818,7 +917,7 @@
         for place, base, key in ((1, KEY_SUMS, V_QUERY), (2, VALUE_SUMS, V_GCONTEXT)):
             made = None
             for j in range(2):
-                left = gt_ref[base + 16 * j : base + 16 * j + HEADS].reshape(HEADS * chips, width)
+                left = gt_ref[base + HEADS * j : base + HEADS * j + HEADS].reshape(HEADS * chips, width)
                 row = gt_ref[VECTORS + 2 * key + j]
                 heads = [
                     jnp.where((lane >= HEAD_DIM * h) & (lane < HEAD_DIM * (h + 1)), row, jnp.zeros_like(row))
@@ -829,17 +928,17 @@
             o_ref[:, place * width : (place + 1) * width] = made
 
 
-def qkv_final_call(info, low, high, gt):
+def qkv_final_call(info, quarters, gt):
     width = gt.shape[2]
     return pl.pallas_call(
         qkv_final_kernel,
-        in_specs=[SCALARS, full(low.shape), full(high.shape), full(gt.shape)],
+        in_specs=[SCALARS] + [full(a.shape) for a in quarters] + [full(gt.shape)],
         out_specs=[full((width, 3 * width)), full((width, width))],
         out_shape=[struct((width, 3 * width), F32), struct((width, width), F32)],
         compiler_params=params_of(32),
         cost_estimate=cost(6),
         name="qkv_final",
-    )(info, low, high, gt)
+    )(info, *quarters, gt)
 
 
 def swap(value):
@@ -873,15 +972,18 @@
 
 class Sum:
     def __init__(self, keep, send, group):
-        self.part, self.coming, self.orders = keep, swap(send), ORDERS[group]
+        self.low, self.coming, self.orders = keep, swap(send), ORDERS[group]
 
     def add(self):
-        half = self.part.shape[0] if self.coming.shape[0] == self.part.shape[0] else self.part.shape[0] // 2
-        self.part = add_low(self.part[:half], self.coming)
-        return self.part
+        half = self.coming.shape[0] // 2
+        if half == 0:
+            self.part = add_low(self.low, self.coming)
+            return
+        self.high = add_low(self.low[half:], self.coming[half:])
+        self.low = self.part = add_low(self.low[:half], self.coming[:half])
 
     def halve(self, stage):
-        self.coming = hop(self.part[self.part.shape[0] // 2 :], stage, self.orders)
+        self.coming = hop(self.high, stage, self.orders)
 
     def across(self):
         chips = lax.axis_size("dp")
@@ -894,7 +996,67 @@
 
     def join(self):
         self.part = jnp.concatenate([self.part, self.coming], axis=0)
-        return self.part
+
+    def quarters(self):
+        return (swap(self.part), swap(self.coming), self.part, self.coming)
+
+
+class Line:
+    def __init__(self):
+        self.token = None
+
+    def __call__(self, value):
+        return value if self.token is None else after(value, self.token)
+
+    def run(self, work, *args):
+        made = work(*args)
+        tied = lax.optimization_barrier(tuple(made))
+        self.token = tied[0]
+        return tied
+
+    def take(self, group):
+        group.coming = self(group.coming)
+        self.token = group.coming
+
+    def halve(self, group, stage):
+        self.take(group)
+        group.add()
+        group.halve(stage)
+        self.token = group.part
+
+    def double(self, group, stage):
+        self.take(group)
+        group.add()
+        group.across()
+        group.double(stage)
+        self.token = group.part
+
+    def join(self, group, stage):
+        self.take(group)
+        group.join()
+        if stage is not None:
+            group.double(stage)
+        self.token = group.part
+
+
+class Gather:
+    ORDERS = ((8, 4, 2, 1), (4, 8, 1, 2))
+
+    def __init__(self, value):
+        self.part = value[None]
+
+    def double(self, stage):
+        self.coming = hop(self.part, stage, self.ORDERS)
+
+    def join(self):
+        self.part = lax.optimization_barrier(jnp.concatenate([self.part, self.coming], axis=0))
+
+    def across(self):
+        chips = lax.axis_size("dp")
+        if chips > GROUP:
+            groups = [[low + GROUP * high for high in range(chips // GROUP)] for low in range(GROUP)]
+            every = lax.all_gather(self.part, "dp", axis_index_groups=groups)
+            self.part = every.reshape((-1,) + self.part.shape[1:])
 
 
 def order_of(chip, orders):
@@ -922,16 +1084,16 @@
     vectors = [weights[k] for k in (1, 2, 4, 5, 6, 8, 10, 11, 12)]
     own, other, own_table = qkv_call(info, inputs, wq, vectors)
     tables = (own_table, swap(own_table))
+    wq_pair = (wq, swap(wq))
     wp_pair = (wp, swap(wp))
+    xq_pair = (own, swap(other))
     wi_pair = (wi, swap(wi))
-    xq_pair = (own, swap(other))
-    wq_pair = (wq, swap(wq))
     wo_pair = (wo, swap(wo))
     head = head_call(info, own, other, wp, wi, wo, own_table)
     arrived = swap(head[0])
     pairs = (xq_pair, wq_pair, wp_pair, wi_pair, wo_pair)
-    (z, xq_d, wp_d, wi_d, wo_d, context, lse, n1, r1, slope, gf, sg, small1, outer_keep, outer_send) = forward_call(
-        True, info, pairs, tables, head[0], arrived, cotangent
+    (z, wp_d, wi_d, wo_d, context, lse, fixed, n1, r1, slope, gf, sg, small1, outer_keep, outer_send) = train_call(
+        info, pairs, tables, head[0], arrived, cotangent
     )
     g1 = Sum(outer_keep, outer_send, 0)
 
@@ -941,93 +1103,73 @@
     g1.halve(0)
     g2 = Sum(inner_keep, inner_send, 1)
 
-    made = attention_call(info, xq_d, after(gc, g1.part), ga, context, lse)
+    made = attention_call(info, xq_pair, fixed, after(gc, g1.part), ga, context, lse)
     qkv_keep, qkv_send, g_qkv, small3 = beside(made, g1, g2)
-    g1.add()
-    g1.halve(1)
-    g2.add()
-    g2.halve(0)
     g3 = Sum(qkv_keep, qkv_send, 2)
-
-    made = input_call(info, after(g_qkv, g1.part, g2.part), gh, wq_pair, small1, small2, small3)
-    gx, dsmall = beside(made, g3)
-    g3.add()
-    g3.halve(0)
-    dsmall_other = after(swap(dsmall), g3.part)
-    made = head_back_call(info, dsmall, dsmall_other, head[1:], own, other, wq, wp, wi, wo, own_table)
-    encoder_gx, payload = beside(made, g1, g2, g3)
-    gathered = lax.all_gather(payload, "dp")
-    g1.add()
-    g1.halve(2)
-    g2.add()
-    g2.halve(1)
-    g3.add()
-    g3.halve(1)
+    line = Line()
+    line.halve(g2, 0)
+    line.halve(g1, 1)
+    gx, dsmall = line.run(input_call, info, line(g_qkv), gh, wq_pair, small1, small2, small3)
+    dsmall_other = swap(dsmall)
+    line.halve(g3, 0)
+    encoder_gx, factors_a, factors_b, own_sums = line.run(
+        head_back_call, info, dsmall, line(dsmall_other), head[1], own, other, wq, wp, wi, wo, own_table
+    )
+    factors_b = swap(factors_b)
     gx_other = swap(gx)
-
-    late = (own_table, after(tables[1], g1.part, g2.part, g3.part))
-    made = forward_call(False, info, pairs, late)
-    (e_low,) = beside(made, g1, g2, g3)
-    g1.add()
-    g1.halve(3)
-    g2.add()
-    g2.halve(2)
-    g3.add()
-    g3.halve(2)
+    line.halve(g1, 2)
+    line.halve(g2, 1)
+    line.halve(g3, 1)
+    factors = Gather(jnp.concatenate([jnp.where(first_section, factors_a, line(factors_b)), own_sums]))
+    factors.double(0)
+    line.token = factors.part
+    line.halve(g1, 3)
+    line.halve(g2, 2)
+    line.join(factors, 1)
+    line.halve(g3, 2)
+    line.double(g1, 3)
+    line.join(factors, 2)
+    line.halve(g2, 3)
+    line.halve(g3, 3)
+    line.join(g1, 2)
+    line.double(g2, 3)
+    line.join(factors, 3)
+    line.double(g3, 3)
+    line.join(g2, 2)
+    line.join(g1, 1)
+    line.join(g3, 2)
+    line.join(g2, 1)
+    line.join(g1, 0)
+    (normed,) = line.run(lambda *a: (mixing_call(*a),), info, xq_pair, wp_pair, (own_table, line(tables[1])))
+    line.join(g3, 1)
+    line.join(g2, 0)
+    line.join(factors, None)
+    factors.across()
+    factors_half = factors.part[:, : FACTORS // 2]
+    factors_more = swap(factors_half)
+    line.take(g1)
+    outer_quarters = g1.quarters()
+    (e_low,) = line.run(lambda *a: (feed_call(*a),), info, line(normed), wi_pair, wo_pair, tables)
     z_other = swap(jnp.where(first_section, z, e_low))
     z_mine = jnp.where(first_section, e_low, z)
-    decoder_gx = jnp.stack([after(gx_other, g3.part), gx])
+    line.join(g3, 0)
+    decoder_gx = jnp.stack([line(gx_other), gx])
     later = jnp.arange(gx.shape[0])[None, :, None] > 0
-    embed_grads = jnp.where(first_section, encoder_gx, jnp.where(later, decoder_gx, 0.0))
-    (embed_grads,) = beside((embed_grads,), g1, g2, g3)
-
-    g1.add()
-    g1.across()
-    g1.double(3)
-    g2.add()
-    g2.halve(3)
-    g3.add()
-    g3.halve(3)
-    z_other = after(z_other, g3.part)
-    outputs = jnp.where(first_section, jnp.stack([z_mine, z_other]), jnp.stack([z_other, z_mine]))
-    (outputs,) = beside((outputs,), g1, g2, g3)
-    g1.join()
-    g1.double(2)
-    g2.add()
-    g2.across()
-    g2.double(3)
-    g3.add()
-    g3.across()
-    g3.double(3)
-    g1.join()
-    g1.double(1)
-    g2.join()
-    g2.double(2)
-    g3.join()
-    g3.double(2)
-    g1.join()
-    g1.double(0)
-    g2.join()
-    g2.double(1)
-    g3.join()
-    g3.double(1)
-    gt = jnp.transpose(after(gathered, g3.part), (1, 0, 2))
-    sums = jnp.sum(gt[SMALLS : SMALLS + 12].astype(F32), axis=1)
-    gt, sums = beside((gt, sums), g1, g2, g3)
-    outer_half = g1.join()
-    outer_other = swap(outer_half)
-    g2.join()
-    g2.double(0)
-    g3.join()
-    g3.double(0)
-    outer_grad = outer_final_call(info, after(outer_other, g2.part, g3.part), outer_half, gt)
-    (outer_grad,) = beside((outer_grad,), g2, g3)
-    inner_half = g2.join()
-    inner_other = swap(inner_half)
-    qkv_half = g3.join()
-    qkv_other = swap(qkv_half)
-    inner_grad = inner_final_call(info, after(inner_other, qkv_half), inner_half, gt)
-    qkv_grad, proj_grad = qkv_final_call(info, after(qkv_other, inner_grad), qkv_half, gt)
+    (embed_grads,) = line.run(lambda a: (jnp.where(first_section, encoder_gx, jnp.where(later, a, 0.0)),), decoder_gx)
+    more = line(factors_more).reshape((-1, 2, 2, 2, 2) + factors_half.shape[1:])
+    more = jnp.transpose(more, (0, 2, 1, 4, 3, 5, 6)).reshape(factors_half.shape)
+    gt = jnp.transpose(jnp.concatenate([factors_half, more], axis=1), (1, 0, 2))
+    sums = jnp.sum(factors.part[:, FACTORS // 2 :].astype(F32), axis=0)
+    gt, sums = line.run(lambda *a: a, gt, sums)
+    outputs = jnp.where(first_section, jnp.stack([z_mine, line(z_other)]), jnp.stack([z_other, z_mine]))
+    (outputs,) = line.run(lambda a: (a,), outputs)
+    (outer_grad,) = line.run(lambda *a: (outer_final_call(*a),), info, outer_quarters, line(gt))
+    line.take(g2)
+    inner_quarters = g2.quarters()
+    line.take(g3)
+    qkv_quarters = g3.quarters()
+    (inner_grad,) = line.run(lambda *a: (inner_final_call(*a),), info, inner_quarters, line(gt))
+    qkv_grad, proj_grad = qkv_final_call(info, qkv_quarters, line(gt))
     results = (
         outputs,
         embed_grads,

time: 335 us -> 289 us (0.86)
  waiting for transfers between devices: 113 us -> 55.7 us
  starting transfers between devices: 38.3 us -> 60.1 us
  between operations: 17.8 us -> 3.97 us
  other arithmetic: 22 us -> 14.3 us
  Pallas kernels: 121 us -> 128 us
  local copies, waits for them, and re-layouts: 17.2 us -> 21.2 us
    ppermute x24 -> x28, waiting for transfers between devices: 105 us -> 49.6 us  [hop(): return lax.ppermute(value, ('section', 'dp'), pairs)]
    ppermute x16 -> x21, starting transfers between devices: 5.12 us -> 20.5 us  [swap(): return lax.ppermute(value, 'section', SWAP)]
    reshape x0 -> x3, local copies, waits for them, and re-layouts: none -> 9.78 us  [the longest x2 6.47 us: local(): more = line(factors_more).reshape((-1, 2, 2, 2, 2) + factors_half.shape[1:])]
    ppermute x24 -> x28, starting transfers between devices: 33.2 us -> 39.5 us  [hop(): return lax.ppermute(value, ('section', 'dp'), pairs)]
    convert_element_type x12 -> x15, other arithmetic: 9.3 us -> 3.71 us  [add_low(): return (left.astype(F32) + right.astype(F32)).astype(BF)]
    pallas_call x4 -> x5, Pallas kernels: 67.5 us -> 72.8 us  [the longest x1 25.9 us: train_call(): pl.pallas_call(train_kernel, in_specs=in_specs + [NEAR] * 4 + [FAR], out_...]
    concatenate x9, other arithmetic: 5.56 us -> 0.62 us  [join(): self.part = jnp.concatenate([self.part, self.coming], axis=0)]
    ppermute x16 -> x21, waiting for transfers between devices: 8.46 us -> 6.11 us  [swap(): return lax.ppermute(value, 'section', SWAP)]
  transfers between devices with their start and end apart: 41 -> 49, of which waited for: 15 -> 15; matrix products, arithmetic and copies ran while one was open for 10% -> 10% of each run, Pallas kernels for 27% -> 34%
where the time goes in v3:
time: 289 us; the launch traced here: 284 us
  Pallas kernels  128 us (44%)
  starting transfers between devices  60.1 us (21%)
  waiting for transfers between devices  55.7 us (19%)
  local copies, waits for them, and re-layouts  21.2 us (7%)
  other arithmetic  14.3 us (5%)
  between operations  3.97 us (1%)
    ppermute x28, waiting for transfers between devices, hop(): return lax.ppermute(value, ('section', 'dp'), pairs)  49.6 us
    ppermute x28, starting transfers between devices, hop(): return lax.ppermute(value, ('section', 'dp'), pairs)  39.5 us
    pallas_call x1, Pallas kernels, train_call(): pl.pallas_call(train_kernel, in_specs=in_specs + [NEAR] * 4 + [FAR], out_...  25.9 us
    ppermute x21, starting transfers between devices, swap(): return lax.ppermute(value, 'section', SWAP)  20.5 us
    pallas_call x1, Pallas kernels, attention_call(): pl.pallas_call(attention_kernel, in_specs=[SCALARS, FAR, FAR] + [NEAR] *...  16.6 us
    pallas_call x1, Pallas kernels, feed_call(): pl.pallas_call(feed_kernel, in_specs=[SCALARS, NEAR] + [FAR] * 4 + [NEAR]...  12.5 us
    pallas_call x1, Pallas kernels, head_back_call(): pl.pallas_call(head_back_kernel, in_specs=[SCALARS] + [NEAR] * len(args)...  11.1 us
    pallas_call x1, Pallas kernels, mixing_call(): pl.pallas_call(mixing_kernel, in_specs=[SCALARS] + [FAR] * 4 + [NEAR] * 2...  10.8 us
  transfers between devices with their start and end apart: 49, of which 15 were waited for; matrix products, arithmetic and copies ran while one was open for 10% of the time, Pallas kernels for 34%

profile of v3, /device:TPU:0, one launch (start us, length us, event | category | flops | bytes accessed | tf_op | source)
XLA Modules:
  0.0 283.6 jit_solution(2566604421328470053)
XLA Ops:
  5.7 8.8 %qkv.1 = (bf16[512,3072]{1,0:T(8,128)(2,1)S(1)}, bf16[512,3072]{1,0:T(8,128)(2,1)}, f32[16,768]{1,0:T(8,128)S(1)}) custom-call(s32[9]{0:T(128)S(1)} %stack.64.info_ref, bf16[2,512,768]{2,1,0:T(8,128)(2,1)} %bitcast.64, bf16[768,2304]{1,0:T(8,128)(2,1)} %bitcast.60, f32[1,768]{1,0:T(1,128)} %refs_0_.1, f32[1,768]{1,0:T(1,128)} %refs_1_.1, f32[1,768]{1,0:T(1,128)} %refs_2_.1, ...), custom_call_target="tpu_custom_call" | custom-call | flops 6600000000 | bytes 12000000 | tf_op jit(solution)/shard_map/qkv/pallas_call | solution.py:163
  14.6 3.0 %copy-done = bf16[512,3072]{1,0:T(8,128)(2,1)S(1)} copy-done((bf16[512,3072]{1,0:T(8,128)(2,1)S(1)}, bf16[512,3072]{1,0:T(8,128)(2,1)}, u32[]{:S(2)}) %copy-start) | copy-done | bytes 3145752
  17.5 7.1 %head_rows.1 = (bf16[16,768]{1,0:T(8,128)(2,1)S(1)}, f32[16,9728]{1,0:T(8,128)S(1)}) custom-call(s32[9]{0:T(128)S(1)} %stack.64.info_ref, bf16[512,3072]{1,0:T(8,128)(2,1)S(1)} %get-tuple-element.109.own_ref.xq_a, bf16[512,3072]{1,0:T(8,128)(2,1)S(1)} %copy-done, bf16[768,768]{1,0:T(8,128)(2,1)} %bitcast.65, bf16[768,3072]{1,0:T(8,128)(2,1)} %bitcast.50, ...), custom_call_target="tpu_custom_call" | custom-call | flops 7699999744 | bytes 14000000 | tf_op jit(solution)/shard_map/head_rows/pallas_call | solution.py:278
  27.3 2.7 collective-permute-done.1.wp_b
  33.2 25.9 %layer_train.1 = (bf16[512,768]{1,0:T(8,128)(2,1)S(1)}, bf16[768,768]{1,0:T(8,128)(2,1)S(1)}, bf16[768,3072]{1,0:T(8,128)(2,1)S(1)}, bf16[3072,768]{1,0:T(8,128)...) custom-call(s32[9]{0:T(128)S(1)} %stack.64.info_ref, ...), custom_call_target="tpu_custom_call" | custom-call | flops 28600000512 | bytes 52000000 | tf_op jit(solution)/shard_map/layer_train/pallas_call | solution.py:480
  59.2 9.7 %inner_grad.1 = (bf16[16,48,1536]{2,1,0:T(8,128)(2,1)S(1)}, bf16[16,48,1536]{2,1,0:T(8,128)(2,1)S(1)}, f32[512,768]{1,0:T(8,128)S(1)}, bf16[512,768]{1,0:T(8,128...) custom-call(s32[9]{0:T(128)S(1)} %stack.64.info_ref, bf16[512,768]{1,0:T(8,128)(2,1)S(1)} %get-tuple-element.114.gf_ref, ...), custom_call_target="tpu_custom_call" | custom-call | flops 11000000512 | bytes 20000000 | tf_op jit(solution)/shard_map/inner_grad/pallas_call | solution.py:570
  70.1 2.7 collective-permute-start.8
  72.9 16.6 %attention_grad.1 = (bf16[16,48,1536]{2,1,0:T(8,128)(2,1)S(1)}, bf16[16,48,1536]{2,1,0:T(8,128)(2,1)S(1)}, bf16[512,2304]{1,0:T(8,128)(2,1)S(1)}, f32[8,768]{1,0:T(8,128)S(1)}) custom-call(s32[9]{0:T(128)S(1)} %stack.64.info_ref, bf16[512,3072]{1,0:T(8,128)(2,1)} %copy-done.2, bf16[512,3072]{1,0:T(8,128)(2,1)} %copy-done.9, ...), custom_call_target="tpu_custom_call" | custom-call | flops 15399999488 | bytes 28000000 | tf_op jit(solution)/shard_map/attention_grad/pallas_call | solution.py:652
  90.6 4.6 %input_grad.1 = (f32[512,768]{1,0:T(8,128)S(1)}, f32[16,768]{1,0:T(8,128)S(1)}) custom-call(s32[9]{0:T(128)S(1)} %stack.64.info_ref, bf16[768,2304]{1,0:T(8,128)(2,1)} %bitcast.62, bf16[768,2304]{1,0:T(8,128)(2,1)} %copy-done.8, bf16[512,2304]{1,0:T(8,128)(2,1)S(1)} %get-tuple-element.146.g_ref, f32[512,768]{1,0:T(8,128)S(1)} %get-tuple-element.147.gh_ref, ...), custom_call_target="tpu_custom_call" | custom-call | flops 4400000000 | bytes 8000000 | tf_op jit(solution)/shard_map/input_grad/pallas_call | solution.py:682
  97.2 2.6 collective-permute-start.16
  102.7 11.1 %head_rows_grad.1 = (f32[2,512,768]{2,1,0:T(8,128)S(1)}, bf16[40,768]{1,0:T(8,128)(2,1)S(1)}, bf16[40,768]{1,0:T(8,128)(2,1)S(1)}, bf16[16,768]{1,0:T(8,128)(2,1)S(1)}) custom-call(s32[9]{0:T(128)S(1)} %stack.64.info_ref, f32[16,768]{1,0:T(8,128)S(1)} %get-tuple-element.151.small_a, f32[16,768]{1,0:T(8,128)S(1)} %collective-permute-done.11.small_b, ...), custom_call_target="tpu_custom_call" | custom-call | flops 13200000000 | bytes 24000000 | tf_op jit(solution)/shard_map/head_rows_grad/pallas_call | solution.py:792
  114.0 13.0 %collective-permute-done.16 = bf16[8,48,1536]{2,1,0:T(8,128)(2,1)S(1)} collective-permute-done((bf16[8,48,1536]{2,1,0:T(8,128)(2,1)S(1)}, bf16[8,48,1536]{2,1,0:T(8,128)(2,1)S(1)}, u32[]{:S(2)}, u32[]{:S(2)}) %collective-permute-start.16) | collective-permute-done | bytes 1179680 | tf_op jit(solution)/shard_map/ppermute | solution.py:959
  128.4 9.1 %collective-permute-done.13 = bf16[2,96,768]{2,1,0:T(8,128)(2,1)S(1)} collective-permute-done((bf16[2,96,768]{2,1,0:T(8,128)(2,1)S(1)}, bf16[2,96,768]{2,1,0:T(8,128)(2,1)S(1)}, u32[]{:S(2)}, u32[]{:S(2)}) %collective-permute-start.13) | collective-permute-done | bytes 294944 | tf_op jit(solution)/shard_map/ppermute | solution.py:959
  137.6 2.6 collective-permute-start.19
  144.5 5.6 %collective-permute-start.24 = (bf16[2,56,768]{2,0,1:T(2,128)(2,1)S(1)}, bf16[2,56,768]{2,0,1:T(2,128)(2,1)S(1)}, u32[]{:S(2)}, u32[]{:S(2)}) collective-permute-start(bf16[2,56,768]{2,0,1:T(2,128)(2,1)S(1)} %pad_maximum_fusion.12), channel_id=1, source_target_pairs={{0,4},{1,5},{2,6},{3,7},{4,0},{5,1},{6,2},{7,3},{8,12},{9,13},{10,... | collective-permute-start | bytes 516104 | tf_op jit(solution)/shard_map/ppermute | solution.py:959
  151.5 3.7 %collective-permute-done.24 = bf16[2,56,768]{2,0,1:T(2,128)(2,1)S(1)} collective-permute-done((bf16[2,56,768]{2,0,1:T(2,128)(2,1)S(1)}, bf16[2,56,768]{2,0,1:T(2,128)(2,1)S(1)}, u32[]{:S(2)}, u32[]{:S(2)}) %collective-permute-start.24) | collective-permute-done | bytes 172064 | tf_op jit(solution)/shard_map/ppermute | solution.py:959
  158.4 6.9 %collective-permute-done.22 = bf16[2,48,1536]{2,1,0:T(8,128)(2,1)S(1)} collective-permute-done((bf16[2,48,1536]{2,1,0:T(8,128)(2,1)S(1)}, bf16[2,48,1536]{2,1,0:T(8,128)(2,1)S(1)}, u32[]{:S(2)}, u32[]{:S(2)}) %collective-permute-start.22) | collective-permute-done | bytes 294944 | tf_op jit(solution)/shard_map/ppermute | solution.py:959
  169.1 2.5 collective-permute-start.27
  172.0 9.3 %collective-permute-done.28 = bf16[1,48,1536]{2,1,0:T(8,128)(2,1)S(1)} collective-permute-done((bf16[1,48,1536]{2,1,0:T(8,128)(2,1)S(1)}, bf16[1,48,1536]{2,1,0:T(8,128)(2,1)S(1)}, u32[]{:S(2)}, u32[]{:S(2)}) %collective-permute-start.28) | collective-permute-done | bytes 147488 | tf_op jit(solution)/shard_map/ppermute | solution.py:959
  183.7 2.8 collective-permute-start.39
  190.5 2.4 collective-permute-done.30
  193.7 10.8 %mixing.1.normed_ref = f32[512,768]{1,0:T(8,128)S(1)} custom-call(s32[9]{0:T(128)S(1)} %stack.64.info_ref, bf16[512,3072]{1,0:T(8,128)(2,1)} %copy-done.2, bf16[512,3072]{1,0:T(8,128)(2,1)} %copy-done.9, bf16[768,768]{1,0:T(8,128)(2,1)} %bitcast.68, bf16[768,768]{1,0:T(8,128)(2,1)} %copy-done.11, f32[16,768]{1,0:T(8,128)S(1)} %get-tuple-element.111.table.mine, ...), custom_call_target="tpu_custom_call" | custom-call | flops 11000000512 | bytes 20000000 | tf_op jit(solution)/shard_map/mixing/pallas_call | solution.py:359
  204.6 13.4 %collective-permute-start.44 = (bf16[8,96,768]{2,1,0:T(8,128)(2,1)S(1)}, bf16[8,96,768]{2,1,0:T(8,128)(2,1)}, u32[]{:S(2)}, u32[]{:S(2)}) collective-permute-start(bf16[8,96,768]{2,1,0:T(8,128)(2,1)S(1)} %pad_maximum_fusion.1.b_low), channel_id=1, source_target_pairs={{0,16},{16,0},{1,17},{17,1},{2,18},{18,2},{3,19},{19,3},{4,20},{20... | collective-permute-start | bytes 3538952 | tf_op jit(solution)/shard_map/ppermute | solution.py:945
  221.0 12.5 %layer_feed.1 = bf16[512,768]{1,0:T(8,128)(2,1)S(1)} custom-call(s32[9]{0:T(128)S(1)} %stack.64.info_ref, f32[512,768]{1,0:T(8,128)S(1)} %mixing.1.normed_ref, bf16[768,3072]{1,0:T(8,128)(2,1)} %bitcast.53, bf16[768,3072]{1,0:T(8,128)(2,1)} %collective-permute-done.4.wi_b, bf16[3072,768]{1,0:T(8,128)(2,1)} %bitcast.58, ...), custom_call_target="tpu_custom_call" | custom-call | flops 12099999744 | bytes 22000000 | tf_op jit(solution)/shard_map/layer_feed/pallas_call | solution.py:516
  239.3 3.4 %reshape.41 = bf16[1,2,2,2,2,40,768]{6,4,3,2,1,5,0:T(2,128)(2,1)} reshape(bf16[16,40,768]{2,0,1:T(8,128)(2,1)} %copy-done.6) | data formatting | bytes 1966080 | tf_op jit(solution)/shard_map/reshape | solution.py:1159
  242.7 3.1 %copy.37 = bf16[1,2,2,2,2,40,768]{6,3,4,1,2,5,0:T(2,128)(2,1)} copy(bf16[1,2,2,2,2,40,768]{6,4,3,2,1,5,0:T(2,128)(2,1)} %reshape.41) | data formatting | bytes 1966080 | tf_op jit(solution)/shard_map/reshape | solution.py:1159
  245.8 3.3 %reshape.42 = bf16[16,40,768]{2,0,1:T(8,128)(2,1)} reshape(bf16[1,2,2,2,2,40,768]{6,4,3,2,1,5,0:T(2,128)(2,1)} %bitcast.44) | data formatting | bytes 1966080 | tf_op jit(solution)/shard_map/reshape | solution.py:1160
  252.3 2.8 maximum_select_fusion.1
  255.1 7.3 %outer_final.1 = f32[3072,768]{1,0:T(8,128)} custom-call(s32[9]{0:T(128)S(1)} %stack.64.info_ref, bf16[8,96,768]{2,1,0:T(8,128)(2,1)} %collective-permute-done.44.a_low, bf16[8,96,768]{2,1,0:T(8,128)(2,1)} %collective-permute-done.45.a_high, bf16[8,96,768]{2,1,0:T(8,128)(2,1)S(1)} %pad_maximum_fusion.1.b_low, ...), custom_call_target="tpu_custom_call" | custom-call | flops 5500000256 | bytes 10000000 | tf_op jit(solution)/shard_map/outer_final/pallas_call | solution.py:835
  262.4 2.4 collective-permute-done.43.b_high
  269.5 6.9 %inner_final.1 = f32[768,3072]{1,0:T(8,128)} custom-call(s32[9]{0:T(128)S(1)} %stack.64.info_ref, bf16[8,48,1536]{2,1,0:T(8,128)(2,1)} %collective-permute-done.47.a_low, bf16[8,48,1536]{2,1,0:T(8,128)(2,1)S(1)} %collective-permute-done.48.a_high, bf16[8,48,1536]{2,1,0:T(8,128)(2,1)S(1)} %pad_maximum_fusion.2.b_low, ...), custom_call_target="tpu_custom_call" | custom-call | flops 5500000256 | bytes 10000000 | tf_op jit(solution)/shard_map/inner_final/pallas_call | solution.py:883
  276.4 7.0 %qkv_final.1 = (f32[768,2304]{1,0:T(8,128)}, f32[768,768]{1,0:T(8,128)}) custom-call(s32[9]{0:T(128)S(1)} %stack.64.info_ref, bf16[8,48,1536]{2,1,0:T(8,128)(2,1)S(1)} %collective-permute-done.41.a_low, bf16[8,48,1536]{2,1,0:T(8,128)(2,1)S(1)} %collective-permute-done.46.a_high, bf16[8,48,1536]{2,1,0:T(8,128)(2,1)S(1)} %pad_maximum_fusion.3.b_low, ...), custom_call_target="tpu_custom_call" | custom-call | flops 6600000000 | bytes 12000000 | tf_op jit(solution)/shard_map/qkv_final/pallas_call | solution.py:933
  (148 shorter events, 54.1 us)
Async XLA Ops:
  0.6 29.3 %collective-permute-start.4 = (bf16[768,3072]{1,0:T(8,128)(2,1)}, bf16[768,3072]{1,0:T(8,128)(2,1)}, u32[]{:S(2)}, u32[]{:S(2)}) collective-permute-start(bf16[768,3072]{1,0:T(8,128)(2,1)} %bitcast.49), channel_id=1, source_target_pairs={{0,16},{16,0},{1,17},{17,1},{2,18},{18,2},{3,19},{19,3},{4,20},{20... | collective-permute-start | bytes 14155784 | tf_op jit(solution)/shard_map/ppermute | solution.py:945
  1.2 28.8 %collective-permute-start.5 = (bf16[3072,768]{1,0:T(8,128)(2,1)}, bf16[3072,768]{1,0:T(8,128)(2,1)}, u32[]{:S(2)}, u32[]{:S(2)}) collective-permute-start(bf16[3072,768]{1,0:T(8,128)(2,1)} %bitcast.54), channel_id=1, source_target_pairs={{0,16},{16,0},{1,17},{17,1},{2,18},{18,2},{3,19},{19,3},{4,20},{20... | collective-permute-start | bytes 14155784 | tf_op jit(solution)/shard_map/ppermute | solution.py:945
  1.2 28.7 %collective-permute-start.3 = (bf16[768,2304]{1,0:T(8,128)(2,1)}, bf16[768,2304]{1,0:T(8,128)(2,1)S(1)}, u32[]{:S(2)}, u32[]{:S(2)}) collective-permute-start(bf16[768,2304]{1,0:T(8,128)(2,1)} %bitcast.59), channel_id=1, source_target_pairs={{0,16},{16,0},{1,17},{17,1},{2,18},{18,2},{3,19},{19,3},{4,20},{20... | collective-permute-start | bytes 10616840 | tf_op jit(solution)/shard_map/ppermute | solution.py:945
  14.5 15.5 %collective-permute-start = (bf16[512,3072]{1,0:T(8,128)(2,1)}, bf16[512,3072]{1,0:T(8,128)(2,1)S(1)}, u32[]{:S(2)}, u32[]{:S(2)}) collective-permute-start(bf16[512,3072]{1,0:T(8,128)(2,1)} %get-tuple-element.110.other_ref), channel_id=1, source_target_pairs={{0,16},{16,0},{1,17},{17,1},{2,18},{18,2},{3,19},{19,3},{4,20},{20... | collective-permute-start | bytes 9437192 | tf_op jit(solution)/shard_map/ppermute | solution.py:945
  69.0 20.5 %collective-permute-start.9 = (bf16[16,48,1536]{2,1,0:T(8,128)(2,1)S(1)}, bf16[16,48,1536]{2,1,0:T(8,128)(2,1)S(1)}, u32[]{:S(2)}, u32[]{:S(2)}) collective-permute-start(bf16[16,48,1536]{2,1,0:T(8,128)(2,1)S(1)} %get-tuple-element.140), channel_id=1, source_target_pairs={{0,16},{16,0},{1,17},{17,1},{2,18},{18,2},{3,19},{19,3},{4,20},{20... | collective-permute-start | bytes 7077896 | tf_op jit(solution)/shard_map/ppermute | solution.py:945
  70.1 19.4 %collective-permute-start.8 = (bf16[8,96,768]{2,1,0:T(8,128)(2,1)S(1)}, bf16[8,96,768]{2,1,0:T(8,128)(2,1)S(1)}, u32[]{:S(2)}, u32[]{:S(2)}) collective-permute-start(bf16[8,96,768]{2,1,0:T(8,128)(2,1)S(1)} %get-tuple-element.207), channel_id=1, source_target_pairs={{0,2},{1,3},{2,0},{3,1},{4,6},{5,7},{6,4},{7,5},{8,10},{9,11},{10,... | collective-permute-start | bytes 3538952 | tf_op jit(solution)/shard_map/ppermute | solution.py:959
  89.5 10.3 %collective-permute-start.12 = (bf16[16,48,1536]{2,1,0:T(8,128)(2,1)S(1)}, bf16[16,48,1536]{2,1,0:T(8,128)(2,1)S(1)}, u32[]{:S(2)}, u32[]{:S(2)}) collective-permute-start(bf16[16,48,1536]{2,1,0:T(8,128)(2,1)S(1)} %get-tuple-element.153), channel_id=1, source_target_pairs={{0,16},{16,0},{1,17},{17,1},{2,18},{18,2},{3,19},{19,3},{4,20},{20... | collective-permute-start | bytes 7077896 | tf_op jit(solution)/shard_map/ppermute | solution.py:945
  95.7 18.1 %collective-permute-start.10 = (bf16[4,96,768]{2,1,0:T(8,128)(2,1)S(1)}, bf16[4,96,768]{2,1,0:T(8,128)(2,1)S(1)}, u32[]{:S(2)}, u32[]{:S(2)}) collective-permute-start(bf16[4,96,768]{2,1,0:T(8,128)(2,1)S(1)} %get-tuple-element.213), channel_id=1, source_target_pairs={{0,1},{1,0},{2,3},{3,2},{4,5},{5,4},{6,7},{7,6},{8,9},{9,8},{10,11... | collective-permute-start | bytes 1769480 | tf_op jit(solution)/shard_map/ppermute | solution.py:959
  97.2 29.8 %collective-permute-start.16 = (bf16[8,48,1536]{2,1,0:T(8,128)(2,1)S(1)}, bf16[8,48,1536]{2,1,0:T(8,128)(2,1)S(1)}, u32[]{:S(2)}, u32[]{:S(2)}) collective-permute-start(bf16[8,48,1536]{2,1,0:T(8,128)(2,1)S(1)} %get-tuple-element.203), channel_id=1, source_target_pairs={{0,8},{1,9},{2,10},{3,11},{4,12},{5,13},{6,14},{7,15},{8,0},{9,1},... | collective-permute-start | bytes 3538952 | tf_op jit(solution)/shard_map/ppermute | solution.py:959
  100.5 27.4 %collective-permute-start.15 = (bf16[8,48,1536]{2,1,0:T(8,128)(2,1)S(1)}, bf16[8,48,1536]{2,1,0:T(8,128)(2,1)S(1)}, u32[]{:S(2)}, u32[]{:S(2)}) collective-permute-start(bf16[8,48,1536]{2,1,0:T(8,128)(2,1)S(1)} %get-tuple-element.205), channel_id=1, source_target_pairs={{0,1},{1,0},{2,3},{3,2},{4,5},{5,4},{6,7},{7,6},{8,9},{9,8},{10,11... | collective-permute-start | bytes 3538952 | tf_op jit(solution)/shard_map/ppermute | solution.py:959
  127.0 10.5 %collective-permute-start.13 = (bf16[2,96,768]{2,1,0:T(8,128)(2,1)S(1)}, bf16[2,96,768]{2,1,0:T(8,128)(2,1)S(1)}, u32[]{:S(2)}, u32[]{:S(2)}) collective-permute-start(bf16[2,96,768]{2,1,0:T(8,128)(2,1)S(1)} %get-tuple-element.221), channel_id=1, source_target_pairs={{0,8},{1,9},{2,10},{3,11},{4,12},{5,13},{6,14},{7,15},{8,0},{9,1},... | collective-permute-start | bytes 884744 | tf_op jit(solution)/shard_map/ppermute | solution.py:959
  142.1 14.0 %collective-permute-start.23 = (bf16[2,48,1536]{2,1,0:T(8,128)(2,1)S(1)}, bf16[2,48,1536]{2,1,0:T(8,128)(2,1)S(1)}, u32[]{:S(2)}, u32[]{:S(2)}) collective-permute-start(bf16[2,48,1536]{2,1,0:T(8,128)(2,1)S(1)} %get-tuple-element.217), channel_id=1, source_target_pairs={{0,2},{1,3},{2,0},{3,1},{4,6},{5,7},{6,4},{7,5},{8,10},{9,11},{10,... | collective-permute-start | bytes 884744 | tf_op jit(solution)/shard_map/ppermute | solution.py:959
  144.5 10.8 %collective-permute-start.24 = (bf16[2,56,768]{2,0,1:T(2,128)(2,1)S(1)}, bf16[2,56,768]{2,0,1:T(2,128)(2,1)S(1)}, u32[]{:S(2)}, u32[]{:S(2)}) collective-permute-start(bf16[2,56,768]{2,0,1:T(2,128)(2,1)S(1)} %pad_maximum_fusion.12), channel_id=1, source_target_pairs={{0,4},{1,5},{2,6},{3,7},{4,0},{5,1},{6,2},{7,3},{8,12},{9,13},{10,... | collective-permute-start | bytes 516104 | tf_op jit(solution)/shard_map/ppermute | solution.py:959
  150.3 15.1 %collective-permute-start.21 = (bf16[1,96,768]{2,1,0:T(8,128)(2,1)S(1)}, bf16[1,96,768]{2,1,0:T(8,128)(2,1)S(1)}, u32[]{:S(2)}, u32[]{:S(2)}) collective-permute-start(bf16[1,96,768]{2,1,0:T(8,128)(2,1)S(1)} %add_convert_fusion.24), channel_id=1, source_target_pairs={{0,4},{1,5},{2,6},{3,7},{4,0},{5,1},{6,2},{7,3},{8,12},{9,13},{10,... | collective-permute-start | bytes 442376 | tf_op jit(solution)/shard_map/ppermute | solution.py:959
  155.6 16.0 %collective-permute-start.29 = (bf16[4,56,768]{2,0,1:T(4,128)(2,1)S(1)}, bf16[4,56,768]{2,0,1:T(4,128)(2,1)S(1)}, u32[]{:S(2)}, u32[]{:S(2)}) collective-permute-start(bf16[4,56,768]{2,0,1:T(4,128)(2,1)S(1)} %pad_maximum_fusion.8), channel_id=1, source_target_pairs={{0,2},{1,3},{2,0},{3,1},{4,6},{5,7},{6,4},{7,5},{8,10},{9,11},{10,... | collective-permute-start | bytes 1032200 | tf_op jit(solution)/shard_map/ppermute | solution.py:959
  165.4 17.5 %collective-permute-start.25 = (bf16[2,96,768]{2,1,0:T(8,128)(2,1)S(1)}, bf16[2,96,768]{2,1,0:T(8,128)(2,1)S(1)}, u32[]{:S(2)}, u32[]{:S(2)}) collective-permute-start(bf16[2,96,768]{2,1,0:T(8,128)(2,1)S(1)} %pad_maximum_fusion.9), channel_id=1, source_target_pairs={{0,8},{1,9},{2,10},{3,11},{4,12},{5,13},{6,14},{7,15},{8,0},{9,1},... | collective-permute-start | bytes 884744 | tf_op jit(solution)/shard_map/ppermute | solution.py:959
  167.5 13.8 %collective-permute-start.28 = (bf16[1,48,1536]{2,1,0:T(8,128)(2,1)S(1)}, bf16[1,48,1536]{2,1,0:T(8,128)(2,1)S(1)}, u32[]{:S(2)}, u32[]{:S(2)}) collective-permute-start(bf16[1,48,1536]{2,1,0:T(8,128)(2,1)S(1)} %get-tuple-element.223), channel_id=1, source_target_pairs={{0,8},{1,9},{2,10},{3,11},{4,12},{5,13},{6,14},{7,15},{8,0},{9,1},... | collective-permute-start | bytes 442376 | tf_op jit(solution)/shard_map/ppermute | solution.py:959
  169.1 12.3 %collective-permute-start.27 = (bf16[1,48,1536]{2,1,0:T(8,128)(2,1)S(1)}, bf16[1,48,1536]{2,1,0:T(8,128)(2,1)S(1)}, u32[]{:S(2)}, u32[]{:S(2)}) collective-permute-start(bf16[1,48,1536]{2,1,0:T(8,128)(2,1)S(1)} %add_convert_fusion.20), channel_id=1, source_target_pairs={{0,4},{1,5},{2,6},{3,7},{4,0},{5,1},{6,2},{7,3},{8,12},{9,13},{10,... | collective-permute-start | bytes 442376 | tf_op jit(solution)/shard_map/ppermute | solution.py:959
  183.7 51.2 %collective-permute-start.39 = (f32[512,768]{1,0:T(8,128)S(1)}, f32[512,768]{1,0:T(8,128)S(1)}, u32[]{:S(2)}, u32[]{:S(2)}) collective-permute-start(f32[512,768]{1,0:T(8,128)S(1)} %get-tuple-element.154), channel_id=1, source_target_pairs={{0,16},{16,0},{1,17},{17,1},{2,18},{18,2},{3,19},{19,3},{4,20},{20... | collective-permute-start | bytes 4718600 | tf_op jit(solution)/shard_map/ppermute | solution.py:945
  186.5 32.4 %collective-permute-start.34 = (bf16[8,56,768]{2,0,1:T(8,128)(2,1)S(1)}, bf16[8,56,768]{2,0,1:T(8,128)(2,1)S(1)}, u32[]{:S(2)}, u32[]{:S(2)}) collective-permute-start(bf16[8,56,768]{2,0,1:T(8,128)(2,1)S(1)} %pad_maximum_fusion.4), channel_id=1, source_target_pairs={{0,1},{1,0},{2,3},{3,2},{4,5},{5,4},{6,7},{7,6},{8,9},{9,8},{10,11... | collective-permute-start | bytes 2064392 | tf_op jit(solution)/shard_map/ppermute | solution.py:959
  188.2 16.4 %collective-permute-start.36 = (bf16[2,48,1536]{2,1,0:T(8,128)(2,1)S(1)}, bf16[2,48,1536]{2,1,0:T(8,128)(2,1)S(1)}, u32[]{:S(2)}, u32[]{:S(2)}) collective-permute-start(bf16[2,48,1536]{2,1,0:T(8,128)(2,1)S(1)} %pad_maximum_fusion.11), channel_id=1, source_target_pairs={{0,4},{1,5},{2,6},{3,7},{4,0},{5,1},{6,2},{7,3},{8,12},{9,13},{10,... | collective-permute-start | bytes 884744 | tf_op jit(solution)/shard_map/ppermute | solution.py:959
  189.8 28.3 %collective-permute-start.35 = (bf16[4,48,1536]{2,1,0:T(8,128)(2,1)S(1)}, bf16[4,48,1536]{2,1,0:T(8,128)(2,1)S(1)}, u32[]{:S(2)}, u32[]{:S(2)}) collective-permute-start(bf16[4,48,1536]{2,1,0:T(8,128)(2,1)S(1)} %pad_maximum_fusion.6), channel_id=1, source_target_pairs={{0,1},{1,0},{2,3},{3,2},{4,5},{5,4},{6,7},{7,6},{8,9},{9,8},{10,11... | collective-permute-start | bytes 1769480 | tf_op jit(solution)/shard_map/ppermute | solution.py:959
  193.0 27.1 %collective-permute-start.33 = (bf16[8,96,768]{2,1,0:T(8,128)(2,1)S(1)}, bf16[8,96,768]{2,1,0:T(8,128)(2,1)}, u32[]{:S(2)}, u32[]{:S(2)}) collective-permute-start(bf16[8,96,768]{2,1,0:T(8,128)(2,1)S(1)} %pad_maximum_fusion.1.b_low), channel_id=1, source_target_pairs={{0,2},{1,3},{2,0},{3,1},{4,6},{5,7},{6,4},{7,5},{8,10},{9,11},{10,... | collective-permute-start | bytes 3538952 | tf_op jit(solution)/shard_map/ppermute | solution.py:959
  204.6 50.5 %collective-permute-start.44 = (bf16[8,96,768]{2,1,0:T(8,128)(2,1)S(1)}, bf16[8,96,768]{2,1,0:T(8,128)(2,1)}, u32[]{:S(2)}, u32[]{:S(2)}) collective-permute-start(bf16[8,96,768]{2,1,0:T(8,128)(2,1)S(1)} %pad_maximum_fusion.1.b_low), channel_id=1, source_target_pairs={{0,16},{16,0},{1,17},{17,1},{2,18},{18,2},{3,19},{19,3},{4,20},{20... | collective-permute-start | bytes 3538952 | tf_op jit(solution)/shard_map/ppermute | solution.py:945
  218.1 15.4 %collective-permute-start.40 = (bf16[4,48,1536]{2,1,0:T(8,128)(2,1)S(1)}, bf16[4,48,1536]{2,1,0:T(8,128)(2,1)S(1)}, u32[]{:S(2)}, u32[]{:S(2)}) collective-permute-start(bf16[4,48,1536]{2,1,0:T(8,128)(2,1)S(1)} %pad_maximum_fusion.7), channel_id=1, source_target_pairs={{0,2},{1,3},{2,0},{3,1},{4,6},{5,7},{6,4},{7,5},{8,10},{9,11},{10,... | collective-permute-start | bytes 1769480 | tf_op jit(solution)/shard_map/ppermute | solution.py:959
  219.1 19.2 %collective-permute-start.38 = (bf16[16,40,768]{2,0,1:T(8,128)(2,1)S(1)}, bf16[16,40,768]{2,0,1:T(8,128)(2,1)S(1)}, u32[]{:S(2)}, u32[]{:S(2)}) collective-permute-start(bf16[16,40,768]{2,0,1:T(8,128)(2,1)S(1)} %slice.264), channel_id=1, source_target_pairs={{0,16},{16,0},{1,17},{17,1},{2,18},{18,2},{3,19},{19,3},{4,20},{20... | collective-permute-start | bytes 2949128 | tf_op jit(solution)/shard_map/ppermute | solution.py:945
  220.1 35.0 %collective-permute-start.45 = (bf16[8,96,768]{2,1,0:T(8,128)(2,1)}, bf16[8,96,768]{2,1,0:T(8,128)(2,1)}, u32[]{:S(2)}, u32[]{:S(2)}) collective-permute-start(bf16[8,96,768]{2,1,0:T(8,128)(2,1)} %collective-permute-done.33.b_high), channel_id=1, source_target_pairs={{0,16},{16,0},{1,17},{17,1},{2,18},{18,2},{3,19},{19,3},{4,20},{20... | collective-permute-start | bytes 3538952 | tf_op jit(solution)/shard_map/ppermute | solution.py:945
  234.7 16.1 %collective-permute-start.37 = (bf16[512,768]{1,0:T(8,128)(2,1)}, bf16[512,768]{1,0:T(8,128)(2,1)}, u32[]{:S(2)}, u32[]{:S(2)}) collective-permute-start(bf16[512,768]{1,0:T(8,128)(2,1)} %get-tuple-element.216), channel_id=1, source_target_pairs={{0,16},{16,0},{1,17},{17,1},{2,18},{18,2},{3,19},{19,3},{4,20},{20... | collective-permute-start | bytes 2359304 | tf_op jit(solution)/shard_map/ppermute | solution.py:945
  234.9 29.9 %collective-permute-start.43 = (bf16[8,48,1536]{2,1,0:T(8,128)(2,1)S(1)}, bf16[8,48,1536]{2,1,0:T(8,128)(2,1)}, u32[]{:S(2)}, u32[]{:S(2)}) collective-permute-start(bf16[8,48,1536]{2,1,0:T(8,128)(2,1)S(1)} %pad_maximum_fusion.2.b_low), channel_id=1, source_target_pairs={{0,8},{1,9},{2,10},{3,11},{4,12},{5,13},{6,14},{7,15},{8,0},{9,1},... | collective-permute-start | bytes 3538952 | tf_op jit(solution)/shard_map/ppermute | solution.py:959
  239.3 29.1 %collective-permute-start.47 = (bf16[8,48,1536]{2,1,0:T(8,128)(2,1)S(1)}, bf16[8,48,1536]{2,1,0:T(8,128)(2,1)}, u32[]{:S(2)}, u32[]{:S(2)}) collective-permute-start(bf16[8,48,1536]{2,1,0:T(8,128)(2,1)S(1)} %pad_maximum_fusion.2.b_low), channel_id=1, source_target_pairs={{0,16},{16,0},{1,17},{17,1},{2,18},{18,2},{3,19},{19,3},{4,20},{20... | collective-permute-start | bytes 3538952 | tf_op jit(solution)/shard_map/ppermute | solution.py:945
  250.9 16.3 %collective-permute-start.42 = (bf16[8,48,1536]{2,1,0:T(8,128)(2,1)S(1)}, bf16[8,48,1536]{2,1,0:T(8,128)(2,1)S(1)}, u32[]{:S(2)}, u32[]{:S(2)}) collective-permute-start(bf16[8,48,1536]{2,1,0:T(8,128)(2,1)S(1)} %pad_maximum_fusion.3.b_low), channel_id=1, source_target_pairs={{0,1},{1,0},{2,3},{3,2},{4,5},{5,4},{6,7},{7,6},{8,9},{9,8},{10,11... | collective-permute-start | bytes 3538952 | tf_op jit(solution)/shard_map/ppermute | solution.py:959
  264.8 11.6 %collective-permute-start.41 = (bf16[8,48,1536]{2,1,0:T(8,128)(2,1)S(1)}, bf16[8,48,1536]{2,1,0:T(8,128)(2,1)S(1)}, u32[]{:S(2)}, u32[]{:S(2)}) collective-permute-start(bf16[8,48,1536]{2,1,0:T(8,128)(2,1)S(1)} %pad_maximum_fusion.3.b_low), channel_id=1, source_target_pairs={{0,16},{16,0},{1,17},{17,1},{2,18},{18,2},{3,19},{19,3},{4,20},{20... | collective-permute-start | bytes 3538952 | tf_op jit(solution)/shard_map/ppermute | solution.py:945
  (29 other events, 179.6 us)

commit v4 on v3

--- a/solution.py
+++ b/solution.py
@@ -18,10 +18,15 @@
 STRIP = 512
 GROUP = 16
 ROW_TILE = 16
-ORDERS = (((2, 1, 8, 4), (1, 4, 2, 8)), ((8, 1, 2, 4), (2, 4, 8, 1)), ((1, 2, 4, 8), (2, 1, 8, 4)))
+ORDERS = (
+    ((2, 1, 8, 4), (1, 4, 2, 8)),
+    ((8, 1, 2, 4), (2, 4, 8, 1)),
+    ((1, 2, 4, 8), (2, 1, 8, 4)),
+)
 SWAP = ((0, 1), (1, 0))
-KEY_SUMS, VALUE_SUMS, VECTORS, ACTS, INNERS, FACTORS = 0, 24, 48, 64, 72, 80
-V_OUTER, V_NORMED, V_CONTEXT, V_PROJ, V_INPUT, V_GQUERY, V_QUERY, V_GCONTEXT = range(8)
+KEY_SUMS, VALUE_SUMS, QUERIES, GCONTEXTS = 0, 24, 48, 50
+OUTERS, NORMEDS, CONTEXTS, PROJS, INPUTS, GQUERIES, ACTS, INNERS = 0, 2, 4, 6, 8, 10, 12, 20
+SUMS, FACTORS = 52, 64
 
 
 def params_of(mebibytes):
@@ -29,7 +34,7 @@
 
 
 def cost(micros):
-    return pl.CostEstimate(flops=int(micros * 1.1e9), bytes_accessed=int(micros * 2e6), transcendentals=0)
+    return pl.CostEstimate(flops=int(micros * 0.11e9), bytes_accessed=int(micros * 0.2e6), transcendentals=0)
 
 
 def nn(left, right):
@@ -180,7 +185,7 @@
             ],
         ),
         out_shape=[struct((length, wide), BF)] * 2 + [struct((ROW_TILE, width), F32)],
-        compiler_params=params_of(50),
+        compiler_params=params_of(20),
         cost_estimate=cost(6),
         name="qkv",
     )(info, *far(inputs, weight, *vectors))
@@ -693,7 +698,7 @@
 
 def head_back_kernel(
     info_ref, small_a, small_b, kept_ref, own_ref, other_ref,
-    wq_ref, wp_ref, wi_ref, wo_ref, table, x_ref, pay_ref, later_ref, sums_ref, wq, wp, wi, wo, sems,
+    wq_ref, wp_ref, wi_ref, wo_ref, table, x_ref, first_ref, second_ref, wq, wp, wi, wo, sems,
 ):
     copies = [
         pltpu.make_async_copy(ref, scr, sems.at[i])
@@ -727,8 +732,7 @@
     normed = (n1 * pick(ATTN_G) + pick(ATTN_B)).astype(BF)
     copies[3].wait()
     query_bias = value_bias = jnp.zeros((1, width), F32)
-    vectors = {}
-    sums_of = []
+    heads, rest = {}, {}
     for i, ref in enumerate((own_ref, other_ref)):
         mid = (1 - 2 * i) * info_ref[0] + i
         keys, values, inputs = ref[:, width : 2 * width], ref[:, 2 * width : 3 * width], ref[:, 3 * width :]
@@ -740,7 +744,9 @@
         gs = (probs * (gp - jnp.sum(probs * gp, axis=-1, keepdims=True))).astype(BF)
         low = probs.astype(BF)
         gq = (heads_of(nn(gs, keys)) * 0.125).astype(BF)
-        sums_of += [(KEY_SUMS + HEADS * i, nn(gs, inputs)), (VALUE_SUMS + HEADS * i, nn(low, inputs))]
+        for place, value in ((KEY_SUMS, nn(gs, inputs)), (VALUE_SUMS, nn(low, inputs))):
+            for h in range(HEADS):
+                heads[place + HEADS * i + h] = value[h : h + 1, :]
         key_back = nt(query_heads, wq[:, width : 2 * width]).astype(BF)
         value_back = nt(gc_heads, wq[:, 2 * width :]).astype(BF)
         gx = tn(gs, key_back) + tn(low, value_back)
@@ -750,39 +756,32 @@
         query_bias = query_bias + gq.astype(F32)
         mass = jnp.sum(low.astype(F32), axis=-1, keepdims=True)
         value_bias = value_bias + heads_of(gc_heads.astype(F32) * mass)
-        for key, piece in (
-            (V_OUTER, gf[i : i + 1, :]),
-            (V_NORMED, normed[i : i + 1, :]),
-            (V_CONTEXT, context[i : i + 1, :]),
-            (V_PROJ, ga[i : i + 1, :]),
-            (V_INPUT, ref[0:1, 3 * width :]),
-            (V_GQUERY, gq),
-            (V_QUERY, query),
-            (V_GCONTEXT, gc_row),
-        ):
-            vectors[2 * key + i] = piece
+        heads[QUERIES + i] = query
+        heads[GCONTEXTS + i] = gc_row
+        for place, value in ((OUTERS, gf), (NORMEDS, normed), (CONTEXTS, context), (PROJS, ga)):
+            rest[place + i] = value[i : i + 1, :]
+        rest[INPUTS + i] = ref[0:1, 3 * width :]
+        rest[GQUERIES + i] = gq
     gu_sum = col_sum(gu)
     act = kept("acts").astype(BF)
     own_small = [query_bias, value_bias, col_sum(ga), col_sum(gn * n1), col_sum(gn)]
     own_small += [gu_sum[:, width * k : width * (k + 1)] for k in range(ff // width)]
     own_small += [col_sum(gf), col_sum(grad * n2), col_sum(grad)]
 
-    def stack(pieces):
-        row = lax.broadcasted_iota(jnp.int32, (ROW_TILE, width), 0)
-        made = jnp.zeros((ROW_TILE, width), F32)
-        for k, piece in enumerate(pieces):
-            made = jnp.where(row == k, piece.astype(F32), made)
-        return made
-
-    wide = [value[i : i + 1, width * k : width * (k + 1)] for value in (act, gu) for i in range(2) for k in range(ff // width)]
-    rows = [value[h : h + 1, :] for place, value in sums_of for h in range(HEADS)]
-    rows = rows[0:HEADS] + rows[2 * HEADS : 3 * HEADS] + rows[HEADS : 2 * HEADS] + rows[3 * HEADS :]
-    rows += [vectors[k] for k in range(16)] + wide
-    half = FACTORS // 2
-    for ref, start in ((pay_ref, 0), (later_ref, half)):
-        for k in range(0, half, 8):
-            ref[k : k + 8, :] = stack(rows[start + k : start + k + 8])[0:8, :].astype(BF)
-    sums_ref[...] = jnp.where(info_ref[0] == 0, stack(own_small), small_a[...] + small_b[...]).astype(BF)
+    for k in range(ff // width):
+        for i in range(2):
+            rest[ACTS + 4 * i + k] = act[i : i + 1, width * k : width * (k + 1)]
+            rest[INNERS + 4 * i + k] = gu[i : i + 1, width * k : width * (k + 1)]
+    row = lax.broadcasted_iota(jnp.int32, (8, width), 0)
+    for ref, rows in ((first_ref, heads), (second_ref, rest)):
+        for k, piece in enumerate(own_small):
+            rows[SUMS + k] = jnp.where(info_ref[0] == 0, piece, small_a[k : k + 1, :] + small_b[k : k + 1, :])
+        for start in range(0, FACTORS, 8):
+            made = jnp.zeros((8, width), F32)
+            for k in range(8):
+                if start + k in rows:
+                    made = jnp.where(row == k, rows[start + k].astype(F32), made)
+            ref[start : start + 8, :] = made.astype(BF)
 
 
 def head_back_call(info, small_a, small_b, kept, own, other, wq, wp, wi, wo, table):
@@ -792,10 +791,8 @@
     return pl.pallas_call(
         head_back_kernel,
         in_specs=[SCALARS] + [NEAR] * len(args) + [FAR] * 4 + [NEAR],
-        out_specs=[NEAR] * 4,
-        out_shape=[struct((2, length, width), F32)]
-        + [struct((FACTORS // 2, width), BF)] * 2
-        + [struct((ROW_TILE, width), BF)],
+        out_specs=[NEAR] * 3,
+        out_shape=[struct((2, length, width), F32)] + [struct((FACTORS, width), BF)] * 2,
         scratch_shapes=[pltpu.VMEM(w.shape, BF) for w in (wq, wp, wi, wo)] + [pltpu.SemaphoreType.DMA((4,))],
         compiler_params=params_of(28),
         cost_estimate=cost(12),
@@ -803,142 +800,138 @@
     )(info, *args, *far(wq, wp, wi, wo), table)
 
 
-def outer_final_kernel(info_ref, a_low, a_high, b_low, b_high, gt_ref, o_ref):
-    step = pl.program_id(0)
-    rows = a_low.shape[1]
-    each = o_ref.shape[0] // rows
-    per_half = pl.num_programs(0) // 2
-
-    @pl.when(info_ref[0] == 1)
-    def _():
-        def fill(low, high, first, order):
-            for p in range(each):
-                piece = piece_at(low, high, jnp.bitwise_xor(first + p, order))
-                o_ref[p * rows : (p + 1) * rows, :] = piece.astype(F32)
-
-        pl.when(step < per_half)(lambda: fill(a_low, a_high, step * each, info_ref[4]))
-        pl.when(step >= per_half)(lambda: fill(b_low, b_high, (step - per_half) * each, info_ref[3]))
-
-    @pl.when(info_ref[0] == 0)
-    def _():
-        made = None
-        for j in range(2):
-            left = gt_ref[ACTS + 4 * j + step]
-            term = tn(left, gt_ref[VECTORS + 2 * V_OUTER + j])
-            made = term if made is None else made + term
-        o_ref[...] = made
-
-
-def outer_final_call(info, quarters, gt):
-    width = quarters[0].shape[2]
-    ff = 4 * quarters[0].shape[0] * quarters[0].shape[1]
-    return pl.pallas_call(
-        outer_final_kernel,
-        grid=(ff // width,),
-        in_specs=[SCALARS] + [full(a.shape) for a in quarters] + [full(gt.shape)],
-        out_specs=pl.BlockSpec((width, width), lambda i: (i, 0)),
-        out_shape=struct((ff, width), F32),
-        compiler_params=params_of(32),
-        cost_estimate=cost(5),
-        name="outer_final",
-    )(info, *quarters, gt)
-
-
 def piece_at(low, high, place, cols=slice(None)):
     half = low.shape[0]
     inside = lax.rem(place, half)
     return jnp.where(place < half, low[inside, :, cols], high[inside, :, cols])
 
 
-def unfold(halves, cols, order, target):
-    low, high = halves
-    rows = low.shape[1]
-    for p in range(GROUP):
-        target[p * rows : (p + 1) * rows, :] = piece_at(low, high, jnp.bitwise_xor(p, order), cols).astype(F32)
-
-
-def inner_final_kernel(info_ref, a_low, a_high, b_low, b_high, gt_ref, o_ref):
-    step = pl.program_id(0)
-    width = o_ref.shape[1]
-
-    @pl.when(info_ref[0] == 1)
-    def _():
-        for k in range(4):
-            ref, order = (((a_low, a_high), info_ref[6]), ((b_low, b_high), info_ref[5]))[k // 2]
-            cols = slice((k % 2) * width, (k % 2 + 1) * width)
-            pl.when(step == k)(lambda ref=ref, order=order, cols=cols: unfold(ref, cols, order, o_ref))
-
-    @pl.when(info_ref[0] == 0)
-    def _():
-        made = None
-        for j in range(2):
-            term = tn(gt_ref[VECTORS + 2 * V_NORMED + j], gt_ref[INNERS + 4 * j + step])
-            made = term if made is None else made + term
-        o_ref[...] = made
-
-
-def inner_final_call(info, quarters, gt):
-    width = gt.shape[2]
-    ff = 2 * quarters[0].shape[2]
+def feed_final_kernel(outer, info_ref, a_low, a_high, b_low, b_high, rest_ref, o_ref, buffers, sems):
+    width = buffers.shape[1]
+    rows = a_low.shape[1]
+    first = 4 if outer else 6
+    halves = ((a_low, a_high, info_ref[first]), (b_low, b_high, info_ref[first - 1]))
+
+    def products(left, right):
+        return sum(tn(rest_ref[left[0] + j * left[1]], rest_ref[right[0] + j * right[1]]) for j in range(2))
+
+    copies = []
+    for k in range(4):
+        slot = k % 2
+        if k >= 2:
+            copies[k - 2].wait()
+
+        @pl.when(info_ref[0] == 1)
+        def _():
+            low, high, order = halves[k // 2]
+            for p in range(width // rows):
+                if outer:
+                    piece = piece_at(low, high, jnp.bitwise_xor((k % 2) * (width // rows) + p, order))
+                else:
+                    cols = slice((k % 2) * width, (k % 2 + 1) * width)
+                    piece = piece_at(low, high, jnp.bitwise_xor(p, order), cols)
+                buffers[slot, p * rows : (p + 1) * rows, :] = piece.astype(F32)
+
+        @pl.when(info_ref[0] == 0)
+        def _():
+            left, right = ((ACTS + k, 4), (OUTERS, 1)) if outer else ((NORMEDS, 1), (INNERS + k, 4))
+            buffers[slot] = products(left, right)
+
+        block = slice(k * width, (k + 1) * width)
+        target = o_ref.at[block, :] if outer else o_ref.at[:, block]
+        copies.append(pltpu.make_async_copy(buffers.at[slot], target, sems.at[slot]))
+        copies[-1].start()
+    copies[-2].wait()
+    copies[-1].wait()
+
+
+def feed_final_call(outer, info, quarters, rest):
+    width = rest.shape[2]
+    ff = 4 * width
     return pl.pallas_call(
-        inner_final_kernel,
-        grid=(ff // width,),
-        in_specs=[SCALARS] + [full(a.shape) for a in quarters] + [full(gt.shape)],
-        out_specs=pl.BlockSpec((width, width), lambda i: (0, i)),
-        out_shape=struct((width, ff), F32),
-        compiler_params=params_of(32),
-        cost_estimate=cost(5),
-        name="inner_final",
-    )(info, *quarters, gt)
-
-
-def qkv_final_kernel(info_ref, a_low, a_high, b_low, b_high, gt_ref, o_ref, p_ref):
+        lambda *refs: feed_final_kernel(outer, *refs),
+        in_specs=[SCALARS] + [NEAR] * 5,
+        out_specs=FAR,
+        out_shape=struct((ff, width) if outer else (width, ff), F32),
+        scratch_shapes=[pltpu.VMEM((2, width, width), F32), pltpu.SemaphoreType.DMA((2,))],
+        compiler_params=params_of(10),
+        cost_estimate=cost(4),
+        name="outer_final" if outer else "inner_final",
+    )(info, *quarters, rest)
+
+
+def qkv_final_kernel(info_ref, a_low, a_high, b_low, b_high, heads_ref, rest_ref, o_ref, p_ref, made, made_p, sems):
     width = p_ref.shape[0]
     wide = 3 * width // 2
     half = width // 2
+    rows = a_low.shape[1]
 
     @pl.when(info_ref[0] == 1)
     def _():
-        for ref, order, k in (((a_low, a_high), info_ref[8], 0), ((b_low, b_high), info_ref[7], 1)):
-            unfold(ref, slice(0, wide), order, o_ref.at[:, k * wide : (k + 1) * wide])
-            unfold(ref, slice(wide, wide + half), order, p_ref.at[:, k * half : (k + 1) * half])
+        copies = []
+        for k, (low, high, order) in enumerate(((a_low, a_high, info_ref[8]), (b_low, b_high, info_ref[7]))):
+            for p in range(GROUP):
+                place = jnp.bitwise_xor(p, order)
+                at = slice(p * rows, (p + 1) * rows)
+                made[at, k * wide : (k + 1) * wide] = piece_at(low, high, place, slice(0, wide)).astype(F32)
+                piece = piece_at(low, high, place, slice(wide, wide + half))
+                made_p[at, k * half : (k + 1) * half] = piece.astype(F32)
+            cols = slice(k * wide, (k + 1) * wide)
+            copies.append(pltpu.make_async_copy(made.at[:, cols], o_ref.at[:, cols], sems.at[k]))
+            copies[-1].start()
+        copies.append(pltpu.make_async_copy(made_p, p_ref, sems.at[2]))
+        copies[-1].start()
+        for copy in copies:
+            copy.wait()
 
     @pl.when(info_ref[0] == 0)
     def _():
         def pairs(left, right):
-            return tn(gt_ref[VECTORS + 2 * left], gt_ref[VECTORS + 2 * right]) + tn(
-                gt_ref[VECTORS + 2 * left + 1], gt_ref[VECTORS + 2 * right + 1]
-            )
-
-        p_ref[...] = pairs(V_CONTEXT, V_PROJ)
-        o_ref[:, 0:width] = pairs(V_INPUT, V_GQUERY)
-        chips = gt_ref.shape[1]
+            return tn(rest_ref[left], rest_ref[right]) + tn(rest_ref[left + 1], rest_ref[right + 1])
+
+        made_p[...] = pairs(CONTEXTS, PROJS)
+        copies = [pltpu.make_async_copy(made_p, p_ref, sems.at[3])]
+        copies[-1].start()
+        chips = heads_ref.shape[1]
         lane = lax.broadcasted_iota(jnp.int32, (chips, width), 1)
-        for place, base, key in ((1, KEY_SUMS, V_QUERY), (2, VALUE_SUMS, V_GCONTEXT)):
-            made = None
-            for j in range(2):
-                left = gt_ref[base + HEADS * j : base + HEADS * j + HEADS].reshape(HEADS * chips, width)
-                row = gt_ref[VECTORS + 2 * key + j]
-                heads = [
-                    jnp.where((lane >= HEAD_DIM * h) & (lane < HEAD_DIM * (h + 1)), row, jnp.zeros_like(row))
-                    for h in range(HEADS)
-                ]
-                term = tn(left, jnp.concatenate(heads, axis=0))
-                made = term if made is None else made + term
-            o_ref[:, place * width : (place + 1) * width] = made
-
-
-def qkv_final_call(info, quarters, gt):
-    width = gt.shape[2]
+        for place, base, key in ((0, 0, 0), (1, KEY_SUMS, QUERIES), (2, VALUE_SUMS, GCONTEXTS)):
+            cols = slice(place * width, (place + 1) * width)
+            if place == 0:
+                made[:, cols] = pairs(INPUTS, GQUERIES)
+            else:
+                term = None
+                for j in range(2):
+                    left = heads_ref[base + HEADS * j : base + HEADS * j + HEADS].reshape(HEADS * chips, width)
+                    row = heads_ref[key + j]
+                    heads = [
+                        jnp.where((lane >= HEAD_DIM * h) & (lane < HEAD_DIM * (h + 1)), row, jnp.zeros_like(row))
+                        for h in range(HEADS)
+                    ]
+                    one = tn(left, jnp.concatenate(heads, axis=0))
+                    term = one if term is None else term + one
+                made[:, cols] = term
+            copies.append(pltpu.make_async_copy(made.at[:, cols], o_ref.at[:, cols], sems.at[4 + place]))
+            copies[-1].start()
+        for copy in copies:
+            copy.wait()
+
+
+def qkv_final_call(info, quarters, heads, rest):
+    width = rest.shape[2]
     return pl.pallas_call(
         qkv_final_kernel,
-        in_specs=[SCALARS] + [full(a.shape) for a in quarters] + [full(gt.shape)],
-        out_specs=[full((width, 3 * width)), full((width, width))],
+        in_specs=[SCALARS] + [NEAR] * 6,
+        out_specs=[FAR, FAR],
         out_shape=[struct((width, 3 * width), F32), struct((width, width), F32)],
-        compiler_params=params_of(32),
-        cost_estimate=cost(6),
+        scratch_shapes=[
+            pltpu.VMEM((width, 3 * width), F32),
+            pltpu.VMEM((width, width), F32),
+            pltpu.SemaphoreType.DMA((7,)),
+        ],
+        compiler_params=params_of(16),
+        cost_estimate=cost(4),
         name="qkv_final",
-    )(info, *quarters, gt)
+    )(info, *quarters, heads, rest)
 
 
 def swap(value):
@@ -997,8 +990,8 @@
     def join(self):
         self.part = jnp.concatenate([self.part, self.coming], axis=0)
 
-    def quarters(self):
-        return (swap(self.part), swap(self.coming), self.part, self.coming)
+    def quarters(self, line):
+        return (swap(line(self.part)), swap(line(self.coming)), self.part, self.coming)
 
 
 class Line:
@@ -1104,23 +1097,25 @@
     g2 = Sum(inner_keep, inner_send, 1)
 
     made = attention_call(info, xq_pair, fixed, after(gc, g1.part), ga, context, lse)
-    qkv_keep, qkv_send, g_qkv, small3 = beside(made, g1, g2)
-    g3 = Sum(qkv_keep, qkv_send, 2)
+    qkv_keep, qkv_send, g_qkv, small3 = beside(made, g1)
     line = Line()
     line.halve(g2, 0)
     line.halve(g1, 1)
+    g3 = Sum(qkv_keep, line(qkv_send), 2)
     gx, dsmall = line.run(input_call, info, line(g_qkv), gh, wq_pair, small1, small2, small3)
-    dsmall_other = swap(dsmall)
+    dsmall_other = swap(line(dsmall))
     line.halve(g3, 0)
-    encoder_gx, factors_a, factors_b, own_sums = line.run(
+    encoder_gx, heads, rest = line.run(
         head_back_call, info, dsmall, line(dsmall_other), head[1], own, other, wq, wp, wi, wo, own_table
     )
-    factors_b = swap(factors_b)
-    gx_other = swap(gx)
+    came = swap(line(rest))
+    gx_other = swap(line(gx))
     line.halve(g1, 2)
+    (normed,) = line.run(lambda *a: (mixing_call(*a),), info, xq_pair, wp_pair, (own_table, line(tables[1])))
     line.halve(g2, 1)
     line.halve(g3, 1)
-    factors = Gather(jnp.concatenate([jnp.where(first_section, factors_a, line(factors_b)), own_sums]))
+    shared = jnp.where(first_section, heads, jnp.concatenate([line(came)[:SUMS], heads[SUMS:]]))
+    factors = Gather(shared)
     factors.double(0)
     line.token = factors.part
     line.halve(g1, 3)
@@ -1140,36 +1135,32 @@
     line.join(g3, 2)
     line.join(g2, 1)
     line.join(g1, 0)
-    (normed,) = line.run(lambda *a: (mixing_call(*a),), info, xq_pair, wp_pair, (own_table, line(tables[1])))
+    (e_low,) = line.run(lambda *a: (feed_call(*a),), info, line(normed), wi_pair, wo_pair, tables)
     line.join(g3, 1)
     line.join(g2, 0)
     line.join(factors, None)
     factors.across()
-    factors_half = factors.part[:, : FACTORS // 2]
-    factors_more = swap(factors_half)
+    sums = jnp.sum(line(factors.part)[:, SUMS:].astype(F32), axis=0)
+    heads_all = jnp.transpose(factors.part, (1, 0, 2))
+    heads_all, sums = line.run(lambda *a: a, heads_all, sums)
+    line.join(g3, 0)
+    rest_all = swap(line(heads_all)[:SUMS])
+    z_other = swap(line(jnp.where(first_section, z, e_low)))
+    z_mine = jnp.where(first_section, e_low, z)
     line.take(g1)
-    outer_quarters = g1.quarters()
-    (e_low,) = line.run(lambda *a: (feed_call(*a),), info, line(normed), wi_pair, wo_pair, tables)
-    z_other = swap(jnp.where(first_section, z, e_low))
-    z_mine = jnp.where(first_section, e_low, z)
-    line.join(g3, 0)
+    outer_quarters = g1.quarters(line)
     decoder_gx = jnp.stack([line(gx_other), gx])
     later = jnp.arange(gx.shape[0])[None, :, None] > 0
     (embed_grads,) = line.run(lambda a: (jnp.where(first_section, encoder_gx, jnp.where(later, a, 0.0)),), decoder_gx)
-    more = line(factors_more).reshape((-1, 2, 2, 2, 2) + factors_half.shape[1:])
-    more = jnp.transpose(more, (0, 2, 1, 4, 3, 5, 6)).reshape(factors_half.shape)
-    gt = jnp.transpose(jnp.concatenate([factors_half, more], axis=1), (1, 0, 2))
-    sums = jnp.sum(factors.part[:, FACTORS // 2 :].astype(F32), axis=0)
-    gt, sums = line.run(lambda *a: a, gt, sums)
     outputs = jnp.where(first_section, jnp.stack([z_mine, line(z_other)]), jnp.stack([z_other, z_mine]))
     (outputs,) = line.run(lambda a: (a,), outputs)
-    (outer_grad,) = line.run(lambda *a: (outer_final_call(*a),), info, outer_quarters, line(gt))
+    (outer_grad,) = line.run(lambda *a: (feed_final_call(True, *a),), info, outer_quarters, line(rest_all))
     line.take(g2)
-    inner_quarters = g2.quarters()
+    inner_quarters = g2.quarters(line)
     line.take(g3)
-    qkv_quarters = g3.quarters()
-    (inner_grad,) = line.run(lambda *a: (inner_final_call(*a),), info, inner_quarters, line(gt))
-    qkv_grad, proj_grad = qkv_final_call(info, qkv_quarters, line(gt))
+    qkv_quarters = g3.quarters(line)
+    (inner_grad,) = line.run(lambda *a: (feed_final_call(False, *a),), info, inner_quarters, line(rest_all))
+    qkv_grad, proj_grad = line.run(qkv_final_call, info, qkv_quarters, heads_all, line(rest_all))
     results = (
         outputs,
         embed_grads,

time: 289 us -> 278 us (0.962)
  waiting for transfers between devices: 55.7 us -> 75 us
  local copies, waits for them, and re-layouts: 21.2 us -> 4.93 us
  starting transfers between devices: 60.1 us -> 55.1 us
  other arithmetic: 14.3 us -> 9.75 us
  Pallas kernels: 128 us -> 124 us
    ppermute x28, waiting for transfers between devices: 49.6 us -> 62.6 us  [hop(): return lax.ppermute(value, ('section', 'dp'), pairs)]
    reshape x3 -> x0, local copies, waits for them, and re-layouts: 9.78 us -> none  [the longest x2 6.47 us: local(): more = line(factors_more).reshape((-1, 2, 2, 2, 2) + factors_half.shape[1:])]
    unnamed x26 -> x12, local copies, waits for them, and re-layouts: 9.24 us -> 2.65 us
    ppermute x21, waiting for transfers between devices: 6.11 us -> 12.3 us  [swap(): return lax.ppermute(value, 'section', SWAP)]
    pallas_call x3, Pallas kernels: 21.2 us -> 16.9 us  [the longest x2 11.6 us: feed_final_call(): pl.pallas_call(lambda *refs: feed_final_kernel(outer, *refs), in_specs=[S...]
    ppermute x28, starting transfers between devices: 39.5 us -> 36.4 us  [hop(): return lax.ppermute(value, ('section', 'dp'), pairs)]
  transfers between devices with their start and end apart: 49 -> 49, of which waited for: 15 -> 20; matrix products, arithmetic and copies ran while one was open for 10% -> 4% of each run, Pallas kernels for 34% -> 34%
where the time goes in v4:
time: 278 us; the launch traced here: 273 us
  Pallas kernels  124 us (45%)
  waiting for transfers between devices  75 us (27%)
  starting transfers between devices  55.1 us (20%)
  other arithmetic  9.75 us (4%)
  local copies, waits for them, and re-layouts  4.93 us (2%)
  between operations  3.95 us (1%)
    ppermute x28, waiting for transfers between devices, hop(): return lax.ppermute(value, ('section', 'dp'), pairs)  62.6 us
    ppermute x28, starting transfers between devices, hop(): return lax.ppermute(value, ('section', 'dp'), pairs)  36.4 us
    pallas_call x1, Pallas kernels, train_call(): pl.pallas_call(train_kernel, in_specs=in_specs + [NEAR] * 4 + [FAR], out_...  26.2 us
    ppermute x21, starting transfers between devices, swap(): return lax.ppermute(value, 'section', SWAP)  18.7 us
    pallas_call x1, Pallas kernels, attention_call(): pl.pallas_call(attention_kernel, in_specs=[SCALARS, FAR, FAR] + [NEAR] *...  16.4 us
    pallas_call x1, Pallas kernels, feed_call(): pl.pallas_call(feed_kernel, in_specs=[SCALARS, NEAR] + [FAR] * 4 + [NEAR]...  12.7 us
    ppermute x21, waiting for transfers between devices, swap(): return lax.ppermute(value, 'section', SWAP)  12.3 us
    pallas_call x2, Pallas kernels, feed_final_call(): pl.pallas_call(lambda *refs: feed_final_kernel(outer, *refs), in_specs=[S...  11.6 us
  transfers between devices with their start and end apart: 49, of which 20 were waited for; matrix products, arithmetic and copies ran while one was open for 4% of the time, Pallas kernels for 34%

profile of v4, /device:TPU:0, one launch (start us, length us, event | category | flops | bytes accessed | tf_op | source)
XLA Modules:
  0.0 272.5 jit_solution(11601555550568583994)
XLA Ops:
  5.7 7.6 %qkv.1 = (bf16[512,3072]{1,0:T(8,128)(2,1)S(1)}, bf16[512,3072]{1,0:T(8,128)(2,1)S(1)}, f32[16,768]{1,0:T(8,128)S(1)}) custom-call(s32[9]{0:T(128)S(1)} %stack.64.info_ref.refs_0_, bf16[2,512,768]{2,1,0:T(8,128)(2,1)} %bitcast.64, bf16[768,2304]{1,0:T(8,128)(2,1)} %bitcast.49, f32[1,768]{1,0:T(1,128)} %refs_0_.1, f32[1,768]{1,0:T(1,128)} %refs_1_.1, ...), custom_call_target="tpu_custom_call" | custom-call | flops 660000000 | bytes 1200000 | tf_op jit(solution)/shard_map/qkv/pallas_call | solution.py:168
  13.4 7.1 %head_rows.1 = (bf16[16,768]{1,0:T(8,128)(2,1)S(1)}, f32[16,9728]{1,0:T(8,128)S(1)}) custom-call(s32[9]{0:T(128)S(1)} %stack.64.info_ref.refs_0_, bf16[512,3072]{1,0:T(8,128)(2,1)S(1)} %get-tuple-element.119.own_ref.xq_a, bf16[512,3072]{1,0:T(8,128)(2,1)S(1)} %get-tuple-element.120.other_ref, bf16[768,768]{1,0:T(8,128)(2,1)} %bitcast.53, ...), custom_call_target="tpu_custom_call" | custom-call | flops 770000000 | bytes 1400000 | tf_op jit(solution)/shard_map/head_rows/pallas_call | solution.py:283
  21.0 3.5 %collective-permute-done.6.arrived_ref = bf16[16,768]{1,0:T(8,128)(2,1)S(1)} collective-permute-done((bf16[16,768]{1,0:T(8,128)(2,1)S(1)}, bf16[16,768]{1,0:T(8,128)(2,1)S(1)}, u32[]{:S(2)}, u32[]{:S(2)}) %collective-permute-start.6) | collective-permute-done | bytes 24608 | tf_op jit(solution)/shard_map/ppermute | solution.py:938
  26.1 2.5 collective-permute-done.1.wp_b
  30.7 26.2 %layer_train.1 = (bf16[512,768]{1,0:T(8,128)(2,1)S(1)}, bf16[768,768]{1,0:T(8,128)(2,1)S(1)}, bf16[768,3072]{1,0:T(8,128)(2,1)S(1)}, bf16[3072,768]{1,0:T(8,128)...) custom-call(s32[9]{0:T(128)S(1)} %stack.64.info_ref.refs_0_, ...), custom_call_target="tpu_custom_call" | custom-call | flops 2860000000 | bytes 5200000 | tf_op jit(solution)/shard_map/layer_train/pallas_call | solution.py:485
  57.3 9.9 %inner_grad.1 = (bf16[16,48,1536]{2,1,0:T(8,128)(2,1)S(1)}, bf16[16,48,1536]{2,1,0:T(8,128)(2,1)S(1)}, f32[512,768]{1,0:T(8,128)S(1)}, bf16[512,768]{1,0:T(8,128...) custom-call(s32[9]{0:T(128)S(1)} %stack.64.info_ref.refs_0_, ...), custom_call_target="tpu_custom_call" | custom-call | flops 1100000000 | bytes 2000000 | tf_op jit(solution)/shard_map/inner_grad/pallas_call | solution.py:575
  68.2 2.9 %collective-permute-start.8 = (bf16[8,96,768]{2,1,0:T(8,128)(2,1)S(1)}, bf16[8,96,768]{2,1,0:T(8,128)(2,1)S(1)}, u32[]{:S(2)}, u32[]{:S(2)}) collective-permute-start(bf16[8,96,768]{2,1,0:T(8,128)(2,1)S(1)} %get-tuple-element.227), channel_id=1, source_target_pairs={{0,2},{1,3},{2,0},{3,1},{4,6},{5,7},{6,4},{7,5},{8,10},{9,11},{10,... | collective-permute-start | bytes 3538952 | tf_op jit(solution)/shard_map/ppermute | solution.py:952
  71.2 16.4 %attention_grad.1 = (bf16[16,48,1536]{2,1,0:T(8,128)(2,1)S(1)}, bf16[16,48,1536]{2,1,0:T(8,128)(2,1)S(1)}, bf16[512,2304]{1,0:T(8,128)(2,1)S(1)}, f32[8,768]{1,0:T(8,128)S(1)}) custom-call(s32[9]{0:T(128)S(1)} %stack.64.info_ref.refs_0_, bf16[512,3072]{1,0:T(8,128)(2,1)} %copy-done, bf16[512,3072]{1,0:T(8,128)(2,1)} %copy-done.2, ...), custom_call_target="tpu_custom_call" | custom-call | flops 1540000000 | bytes 2800000 | tf_op jit(solution)/shard_map/attention_grad/pallas_call | solution.py:657
  88.8 4.6 %input_grad.1 = (f32[512,768]{1,0:T(8,128)S(1)}, f32[16,768]{1,0:T(8,128)S(1)}) custom-call(s32[9]{0:T(128)S(1)} %stack.64.info_ref.refs_0_, bf16[768,2304]{1,0:T(8,128)(2,1)} %bitcast.51, bf16[768,2304]{1,0:T(8,128)(2,1)} %collective-permute-done.3.wq_b.w_b, bf16[512,2304]{1,0:T(8,128)(2,1)S(1)} %get-tuple-element.155.g_ref, ...), custom_call_target="tpu_custom_call" | custom-call | flops 440000000 | bytes 800000 | tf_op jit(solution)/shard_map/input_grad/pallas_call | solution.py:687
  94.9 2.6 collective-permute-start.16
  100.1 11.1 %head_rows_grad.1 = (f32[2,512,768]{2,1,0:T(8,128)S(1)}, bf16[64,768]{1,0:T(8,128)(2,1)S(1)}, bf16[64,768]{1,0:T(8,128)(2,1)S(1)}) custom-call(s32[9]{0:T(128)S(1)} %stack.64.info_ref.refs_0_, f32[16,768]{1,0:T(8,128)S(1)} %get-tuple-element.162.small_a, f32[16,768]{1,0:T(8,128)S(1)} %collective-permute-done.11.small_b, ...), custom_call_target="tpu_custom_call" | custom-call | flops 1320000000 | bytes 2400000 | tf_op jit(solution)/shard_map/head_rows_grad/pallas_call | solution.py:791
  111.4 11.3 %mixing.1.normed_ref = f32[512,768]{1,0:T(8,128)S(1)} custom-call(s32[9]{0:T(128)S(1)} %stack.64.info_ref.refs_0_, bf16[512,3072]{1,0:T(8,128)(2,1)} %copy-done, bf16[512,3072]{1,0:T(8,128)(2,1)} %copy-done.2, bf16[768,768]{1,0:T(8,128)(2,1)} %bitcast.56, bf16[768,768]{1,0:T(8,128)(2,1)} %copy-done.4, f32[16,768]{1,0:T(8,128)S(1)} %get-tuple-element.121.table.mine, ...), custom_call_target="tpu_custom_call" | custom-call | flops 1100000000 | bytes 2000000 | tf_op jit(solution)/shard_map/mixing/pallas_call | solution.py:364
  122.7 2.0 collective-permute-done.16
  126.6 8.7 %collective-permute-done.13 = bf16[2,96,768]{2,1,0:T(8,128)(2,1)S(1)} collective-permute-done((bf16[2,96,768]{2,1,0:T(8,128)(2,1)S(1)}, bf16[2,96,768]{2,1,0:T(8,128)(2,1)S(1)}, u32[]{:S(2)}, u32[]{:S(2)}) %collective-permute-start.13) | collective-permute-done | bytes 294944 | tf_op jit(solution)/shard_map/ppermute | solution.py:952
  135.4 2.6 collective-permute-start.19
  142.8 5.6 %collective-permute-start.24 = (bf16[2,64,768]{2,0,1:T(2,128)(2,1)S(1)}, bf16[2,64,768]{2,0,1:T(2,128)(2,1)S(1)}, u32[]{:S(2)}, u32[]{:S(2)}) collective-permute-start(bf16[2,64,768]{2,0,1:T(2,128)(2,1)S(1)} %pad_maximum_fusion.12), channel_id=1, source_target_pairs={{0,4},{1,5},{2,6},{3,7},{4,0},{5,1},{6,2},{7,3},{8,12},{9,13},{10,... | collective-permute-start | bytes 589832 | tf_op jit(solution)/shard_map/ppermute | solution.py:952
  149.3 4.8 %collective-permute-done.24 = bf16[2,64,768]{2,0,1:T(2,128)(2,1)S(1)} collective-permute-done((bf16[2,64,768]{2,0,1:T(2,128)(2,1)S(1)}, bf16[2,64,768]{2,0,1:T(2,128)(2,1)S(1)}, u32[]{:S(2)}, u32[]{:S(2)}) %collective-permute-start.24) | collective-permute-done | bytes 196640 | tf_op jit(solution)/shard_map/ppermute | solution.py:952
  155.0 2.1 collective-permute-start.22
  157.3 6.8 %collective-permute-done.22 = bf16[2,48,1536]{2,1,0:T(8,128)(2,1)S(1)} collective-permute-done((bf16[2,48,1536]{2,1,0:T(8,128)(2,1)S(1)}, bf16[2,48,1536]{2,1,0:T(8,128)(2,1)S(1)}, u32[]{:S(2)}, u32[]{:S(2)}) %collective-permute-start.22) | collective-permute-done | bytes 294944 | tf_op jit(solution)/shard_map/ppermute | solution.py:952
  167.9 2.5 collective-permute-start.27
  170.9 9.2 %collective-permute-done.28 = bf16[1,48,1536]{2,1,0:T(8,128)(2,1)S(1)} collective-permute-done((bf16[1,48,1536]{2,1,0:T(8,128)(2,1)S(1)}, bf16[1,48,1536]{2,1,0:T(8,128)(2,1)S(1)}, u32[]{:S(2)}, u32[]{:S(2)}) %collective-permute-start.28) | collective-permute-done | bytes 147488 | tf_op jit(solution)/shard_map/ppermute | solution.py:952
  182.3 2.9 %collective-permute-start.38 = (f32[512,768]{1,0:T(8,128)S(1)}, f32[512,768]{1,0:T(8,128)S(1)}, u32[]{:S(2)}, u32[]{:S(2)}) collective-permute-start(f32[512,768]{1,0:T(8,128)S(1)} %get-tuple-element.204), channel_id=1, source_target_pairs={{0,16},{16,0},{1,17},{17,1},{2,18},{18,2},{3,19},{19,3},{4,20},{20... | collective-permute-start | bytes 4718600 | tf_op jit(solution)/shard_map/ppermute | solution.py:938
  187.7 1.7 collective-permute-done.31
  191.9 12.7 %layer_feed.1 = bf16[512,768]{1,0:T(8,128)(2,1)S(1)} custom-call(s32[9]{0:T(128)S(1)} %stack.64.info_ref.refs_0_, f32[512,768]{1,0:T(8,128)S(1)} %mixing.1.normed_ref, bf16[768,3072]{1,0:T(8,128)(2,1)} %bitcast.42, bf16[768,3072]{1,0:T(8,128)(2,1)} %collective-permute-done.4.wi_b, bf16[3072,768]{1,0:T(8,128)(2,1)} %bitcast.47, ...), custom_call_target="tpu_custom_call" | custom-call | flops 1210000000 | bytes 2200000 | tf_op jit(solution)/shard_map/layer_feed/pallas_call | solution.py:521
  205.8 10.3 %collective-permute-done.34 = bf16[4,48,1536]{2,1,0:T(8,128)(2,1)S(1)} collective-permute-done((bf16[4,48,1536]{2,1,0:T(8,128)(2,1)S(1)}, bf16[4,48,1536]{2,1,0:T(8,128)(2,1)S(1)}, u32[]{:S(2)}, u32[]{:S(2)}) %collective-permute-start.34) | collective-permute-done | bytes 589856 | tf_op jit(solution)/shard_map/ppermute | solution.py:952
  216.2 11.0 %collective-permute-start.37 = (bf16[512,768]{1,0:T(8,128)(2,1)S(1)}, bf16[512,768]{1,0:T(8,128)(2,1)S(1)}, u32[]{:S(2)}, u32[]{:S(2)}) collective-permute-start(bf16[512,768]{1,0:T(8,128)(2,1)S(1)} %get-tuple-element.203), channel_id=1, source_target_pairs={{0,16},{16,0},{1,17},{17,1},{2,18},{18,2},{3,19},{19,3},{4,20},{20... | collective-permute-start | bytes 2359304 | tf_op jit(solution)/shard_map/ppermute | solution.py:938
  230.0 2.1 fusion
  234.3 5.8 %outer_final.1 = f32[3072,768]{1,0:T(8,128)} custom-call(s32[9]{0:T(128)S(1)} %stack.64.info_ref.refs_0_, bf16[8,96,768]{2,1,0:T(8,128)(2,1)S(1)} %collective-permute-done.42.refs_1_, bf16[8,96,768]{2,1,0:T(8,128)(2,1)S(1)} %collective-permute-done.43.refs_2_, bf16[8,96,768]{2,1,0:T(8,128)(2,1)S(1)} %pad_maximum_fusion.1.refs_3_, ...), custom_call_target="tpu_custom_call" | custom-call | flops 440000000 | bytes 800000 | tf_op jit(solution)/shard_map/outer_final/pallas_call | solution.py:851
  240.1 16.6 %collective-permute-done.41.refs_4_ = bf16[8,48,1536]{2,1,0:T(8,128)(2,1)S(1)} collective-permute-done((bf16[8,48,1536]{2,1,0:T(8,128)(2,1)S(1)}, bf16[8,48,1536]{2,1,0:T(8,128)(2,1)S(1)}, u32[]{:S(2)}, u32[]{:S(2)}) %collective-permute-start.41) | collective-permute-done | bytes 1179680 | tf_op jit(solution)/shard_map/ppermute | solution.py:952
  259.5 1.7 collective-permute-done.48.refs_2_
  261.2 5.8 %inner_final.1 = f32[768,3072]{1,0:T(8,128)} custom-call(s32[9]{0:T(128)S(1)} %stack.64.info_ref.refs_0_, bf16[8,48,1536]{2,1,0:T(8,128)(2,1)S(1)} %collective-permute-done.47.refs_1_, bf16[8,48,1536]{2,1,0:T(8,128)(2,1)S(1)} %collective-permute-done.48.refs_2_, bf16[8,48,1536]{2,1,0:T(8,128)(2,1)S(1)} %pad_maximum_fusion.2.refs_3_, ...), custom_call_target="tpu_custom_call" | custom-call | flops 440000000 | bytes 800000 | tf_op jit(solution)/shard_map/inner_final/pallas_call | solution.py:851
  267.0 5.3 %qkv_final.1 = (f32[768,2304]{1,0:T(8,128)}, f32[768,768]{1,0:T(8,128)}) custom-call(s32[9]{0:T(128)S(1)} %stack.64.info_ref.refs_0_, bf16[8,48,1536]{2,1,0:T(8,128)(2,1)S(1)} %collective-permute-done.45.a_low, bf16[8,48,1536]{2,1,0:T(8,128)(2,1)S(1)} %collective-permute-done.46.a_high, bf16[8,48,1536]{2,1,0:T(8,128)(2,1)S(1)} %pad_maximum_fusion.3.b_low, ...), custom_call_target="tpu_custom_call" | custom-call | flops 440000000 | bytes 800000 | tf_op jit(solution)/shard_map/qkv_final/pallas_call | solution.py:921
  (131 shorter events, 42.6 us)
Async XLA Ops:
  0.6 28.0 %collective-permute-start.4 = (bf16[768,3072]{1,0:T(8,128)(2,1)}, bf16[768,3072]{1,0:T(8,128)(2,1)}, u32[]{:S(2)}, u32[]{:S(2)}) collective-permute-start(bf16[768,3072]{1,0:T(8,128)(2,1)} %bitcast.38), channel_id=1, source_target_pairs={{0,16},{16,0},{1,17},{17,1},{2,18},{18,2},{3,19},{19,3},{4,20},{20... | collective-permute-start | bytes 14155784 | tf_op jit(solution)/shard_map/ppermute | solution.py:938
  1.2 27.5 %collective-permute-start.5 = (bf16[3072,768]{1,0:T(8,128)(2,1)}, bf16[3072,768]{1,0:T(8,128)(2,1)}, u32[]{:S(2)}, u32[]{:S(2)}) collective-permute-start(bf16[3072,768]{1,0:T(8,128)(2,1)} %bitcast.43), channel_id=1, source_target_pairs={{0,16},{16,0},{1,17},{17,1},{2,18},{18,2},{3,19},{19,3},{4,20},{20... | collective-permute-start | bytes 14155784 | tf_op jit(solution)/shard_map/ppermute | solution.py:938
  1.2 27.4 %collective-permute-start.3 = (bf16[768,2304]{1,0:T(8,128)(2,1)}, bf16[768,2304]{1,0:T(8,128)(2,1)}, u32[]{:S(2)}, u32[]{:S(2)}) collective-permute-start(bf16[768,2304]{1,0:T(8,128)(2,1)} %bitcast.48), channel_id=1, source_target_pairs={{0,16},{16,0},{1,17},{17,1},{2,18},{18,2},{3,19},{19,3},{4,20},{20... | collective-permute-start | bytes 10616840 | tf_op jit(solution)/shard_map/ppermute | solution.py:938
  13.3 15.3 %collective-permute-start = (bf16[512,3072]{1,0:T(8,128)(2,1)S(1)}, bf16[512,3072]{1,0:T(8,128)(2,1)S(1)}, u32[]{:S(2)}, u32[]{:S(2)}) collective-permute-start(bf16[512,3072]{1,0:T(8,128)(2,1)S(1)} %get-tuple-element.120.other_ref), channel_id=1, source_target_pairs={{0,16},{16,0},{1,17},{17,1},{2,18},{18,2},{3,19},{19,3},{4,20},{20... | collective-permute-start | bytes 9437192 | tf_op jit(solution)/shard_map/ppermute | solution.py:938
  56.9 10.3 %collective-permute-start.7 = (bf16[16,96,768]{2,1,0:T(8,128)(2,1)S(1)}, bf16[16,96,768]{2,1,0:T(8,128)(2,1)S(1)}, u32[]{:S(2)}, u32[]{:S(2)}) collective-permute-start(bf16[16,96,768]{2,1,0:T(8,128)(2,1)S(1)} %get-tuple-element.138), channel_id=1, source_target_pairs={{0,16},{16,0},{1,17},{17,1},{2,18},{18,2},{3,19},{19,3},{4,20},{20... | collective-permute-start | bytes 7077896 | tf_op jit(solution)/shard_map/ppermute | solution.py:938
  67.3 20.3 %collective-permute-start.9 = (bf16[16,48,1536]{2,1,0:T(8,128)(2,1)S(1)}, bf16[16,48,1536]{2,1,0:T(8,128)(2,1)S(1)}, u32[]{:S(2)}, u32[]{:S(2)}) collective-permute-start(bf16[16,48,1536]{2,1,0:T(8,128)(2,1)S(1)} %get-tuple-element.152), channel_id=1, source_target_pairs={{0,16},{16,0},{1,17},{17,1},{2,18},{18,2},{3,19},{19,3},{4,20},{20... | collective-permute-start | bytes 7077896 | tf_op jit(solution)/shard_map/ppermute | solution.py:938
  68.2 19.3 %collective-permute-start.8 = (bf16[8,96,768]{2,1,0:T(8,128)(2,1)S(1)}, bf16[8,96,768]{2,1,0:T(8,128)(2,1)S(1)}, u32[]{:S(2)}, u32[]{:S(2)}) collective-permute-start(bf16[8,96,768]{2,1,0:T(8,128)(2,1)S(1)} %get-tuple-element.227), channel_id=1, source_target_pairs={{0,2},{1,3},{2,0},{3,1},{4,6},{5,7},{6,4},{7,5},{8,10},{9,11},{10,... | collective-permute-start | bytes 3538952 | tf_op jit(solution)/shard_map/ppermute | solution.py:952
  93.4 17.9 %collective-permute-start.10 = (bf16[4,96,768]{2,1,0:T(8,128)(2,1)S(1)}, bf16[4,96,768]{2,1,0:T(8,128)(2,1)S(1)}, u32[]{:S(2)}, u32[]{:S(2)}) collective-permute-start(bf16[4,96,768]{2,1,0:T(8,128)(2,1)S(1)} %get-tuple-element.233), channel_id=1, source_target_pairs={{0,1},{1,0},{2,3},{3,2},{4,5},{5,4},{6,7},{7,6},{8,9},{9,8},{10,11... | collective-permute-start | bytes 1769480 | tf_op jit(solution)/shard_map/ppermute | solution.py:952
  94.9 29.8 %collective-permute-start.16 = (bf16[8,48,1536]{2,1,0:T(8,128)(2,1)S(1)}, bf16[8,48,1536]{2,1,0:T(8,128)(2,1)S(1)}, u32[]{:S(2)}, u32[]{:S(2)}) collective-permute-start(bf16[8,48,1536]{2,1,0:T(8,128)(2,1)S(1)} %get-tuple-element.223), channel_id=1, source_target_pairs={{0,8},{1,9},{2,10},{3,11},{4,12},{5,13},{6,14},{7,15},{8,0},{9,1},... | collective-permute-start | bytes 3538952 | tf_op jit(solution)/shard_map/ppermute | solution.py:952
  98.2 27.7 %collective-permute-start.15 = (bf16[8,48,1536]{2,1,0:T(8,128)(2,1)S(1)}, bf16[8,48,1536]{2,1,0:T(8,128)(2,1)S(1)}, u32[]{:S(2)}, u32[]{:S(2)}) collective-permute-start(bf16[8,48,1536]{2,1,0:T(8,128)(2,1)S(1)} %get-tuple-element.225), channel_id=1, source_target_pairs={{0,1},{1,0},{2,3},{3,2},{4,5},{5,4},{6,7},{7,6},{8,9},{9,8},{10,11... | collective-permute-start | bytes 3538952 | tf_op jit(solution)/shard_map/ppermute | solution.py:952
  124.7 10.6 %collective-permute-start.13 = (bf16[2,96,768]{2,1,0:T(8,128)(2,1)S(1)}, bf16[2,96,768]{2,1,0:T(8,128)(2,1)S(1)}, u32[]{:S(2)}, u32[]{:S(2)}) collective-permute-start(bf16[2,96,768]{2,1,0:T(8,128)(2,1)S(1)} %get-tuple-element.241), channel_id=1, source_target_pairs={{0,8},{1,9},{2,10},{3,11},{4,12},{5,13},{6,14},{7,15},{8,0},{9,1},... | collective-permute-start | bytes 884744 | tf_op jit(solution)/shard_map/ppermute | solution.py:952
  125.1 10.2 %collective-permute-start.20 = (bf16[4,48,1536]{2,1,0:T(8,128)(2,1)S(1)}, bf16[4,48,1536]{2,1,0:T(8,128)(2,1)S(1)}, u32[]{:S(2)}, u32[]{:S(2)}) collective-permute-start(bf16[4,48,1536]{2,1,0:T(8,128)(2,1)S(1)} %get-tuple-element.229), channel_id=1, source_target_pairs={{0,1},{1,0},{2,3},{3,2},{4,5},{5,4},{6,7},{7,6},{8,9},{9,8},{10,11... | collective-permute-start | bytes 1769480 | tf_op jit(solution)/shard_map/ppermute | solution.py:952
  138.0 10.5 %collective-permute-start.18 = (bf16[4,48,1536]{2,1,0:T(8,128)(2,1)S(1)}, bf16[4,48,1536]{2,1,0:T(8,128)(2,1)S(1)}, u32[]{:S(2)}, u32[]{:S(2)}) collective-permute-start(bf16[4,48,1536]{2,1,0:T(8,128)(2,1)S(1)} %get-tuple-element.231), channel_id=1, source_target_pairs={{0,2},{1,3},{2,0},{3,1},{4,6},{5,7},{6,4},{7,5},{8,10},{9,11},{10,... | collective-permute-start | bytes 1769480 | tf_op jit(solution)/shard_map/ppermute | solution.py:952
  138.6 10.0 %collective-permute-start.17 = (bf16[1,96,768]{2,1,0:T(8,128)(2,1)S(1)}, bf16[1,96,768]{2,1,0:T(8,128)(2,1)S(1)}, u32[]{:S(2)}, u32[]{:S(2)}) collective-permute-start(bf16[1,96,768]{2,1,0:T(8,128)(2,1)S(1)} %get-tuple-element.248), channel_id=1, source_target_pairs={{0,4},{1,5},{2,6},{3,7},{4,0},{5,1},{6,2},{7,3},{8,12},{9,13},{10,... | collective-permute-start | bytes 442376 | tf_op jit(solution)/shard_map/ppermute | solution.py:952
  139.9 15.2 %collective-permute-start.23 = (bf16[2,48,1536]{2,1,0:T(8,128)(2,1)S(1)}, bf16[2,48,1536]{2,1,0:T(8,128)(2,1)S(1)}, u32[]{:S(2)}, u32[]{:S(2)}) collective-permute-start(bf16[2,48,1536]{2,1,0:T(8,128)(2,1)S(1)} %get-tuple-element.237), channel_id=1, source_target_pairs={{0,2},{1,3},{2,0},{3,1},{4,6},{5,7},{6,4},{7,5},{8,10},{9,11},{10,... | collective-permute-start | bytes 884744 | tf_op jit(solution)/shard_map/ppermute | solution.py:952
  142.8 11.3 %collective-permute-start.24 = (bf16[2,64,768]{2,0,1:T(2,128)(2,1)S(1)}, bf16[2,64,768]{2,0,1:T(2,128)(2,1)S(1)}, u32[]{:S(2)}, u32[]{:S(2)}) collective-permute-start(bf16[2,64,768]{2,0,1:T(2,128)(2,1)S(1)} %pad_maximum_fusion.12), channel_id=1, source_target_pairs={{0,4},{1,5},{2,6},{3,7},{4,0},{5,1},{6,2},{7,3},{8,12},{9,13},{10,... | collective-permute-start | bytes 589832 | tf_op jit(solution)/shard_map/ppermute | solution.py:952
  148.6 15.5 %collective-permute-start.21 = (bf16[1,96,768]{2,1,0:T(8,128)(2,1)S(1)}, bf16[1,96,768]{2,1,0:T(8,128)(2,1)S(1)}, u32[]{:S(2)}, u32[]{:S(2)}) collective-permute-start(bf16[1,96,768]{2,1,0:T(8,128)(2,1)S(1)} %add_convert_fusion.24), channel_id=1, source_target_pairs={{0,4},{1,5},{2,6},{3,7},{4,0},{5,1},{6,2},{7,3},{8,12},{9,13},{10,... | collective-permute-start | bytes 442376 | tf_op jit(solution)/shard_map/ppermute | solution.py:952
  154.6 15.9 %collective-permute-start.29 = (bf16[4,64,768]{2,0,1:T(4,128)(2,1)S(1)}, bf16[4,64,768]{2,0,1:T(4,128)(2,1)S(1)}, u32[]{:S(2)}, u32[]{:S(2)}) collective-permute-start(bf16[4,64,768]{2,0,1:T(4,128)(2,1)S(1)} %pad_maximum_fusion.8), channel_id=1, source_target_pairs={{0,2},{1,3},{2,0},{3,1},{4,6},{5,7},{6,4},{7,5},{8,10},{9,11},{10,... | collective-permute-start | bytes 1179656 | tf_op jit(solution)/shard_map/ppermute | solution.py:952
  164.2 16.0 %collective-permute-start.25 = (bf16[2,96,768]{2,1,0:T(8,128)(2,1)S(1)}, bf16[2,96,768]{2,1,0:T(8,128)(2,1)S(1)}, u32[]{:S(2)}, u32[]{:S(2)}) collective-permute-start(bf16[2,96,768]{2,1,0:T(8,128)(2,1)S(1)} %pad_maximum_fusion.9), channel_id=1, source_target_pairs={{0,8},{1,9},{2,10},{3,11},{4,12},{5,13},{6,14},{7,15},{8,0},{9,1},... | collective-permute-start | bytes 884744 | tf_op jit(solution)/shard_map/ppermute | solution.py:952
  166.3 13.7 %collective-permute-start.28 = (bf16[1,48,1536]{2,1,0:T(8,128)(2,1)S(1)}, bf16[1,48,1536]{2,1,0:T(8,128)(2,1)S(1)}, u32[]{:S(2)}, u32[]{:S(2)}) collective-permute-start(bf16[1,48,1536]{2,1,0:T(8,128)(2,1)S(1)} %get-tuple-element.243), channel_id=1, source_target_pairs={{0,8},{1,9},{2,10},{3,11},{4,12},{5,13},{6,14},{7,15},{8,0},{9,1},... | collective-permute-start | bytes 442376 | tf_op jit(solution)/shard_map/ppermute | solution.py:952
  167.9 12.3 %collective-permute-start.27 = (bf16[1,48,1536]{2,1,0:T(8,128)(2,1)S(1)}, bf16[1,48,1536]{2,1,0:T(8,128)(2,1)S(1)}, u32[]{:S(2)}, u32[]{:S(2)}) collective-permute-start(bf16[1,48,1536]{2,1,0:T(8,128)(2,1)S(1)} %add_convert_fusion.20), channel_id=1, source_target_pairs={{0,4},{1,5},{2,6},{3,7},{4,0},{5,1},{6,2},{7,3},{8,12},{9,13},{10,... | collective-permute-start | bytes 442376 | tf_op jit(solution)/shard_map/ppermute | solution.py:952
  180.3 9.9 %collective-permute-start.30 = (bf16[4,96,768]{2,1,0:T(8,128)(2,1)S(1)}, bf16[4,96,768]{2,1,0:T(8,128)(2,1)S(1)}, u32[]{:S(2)}, u32[]{:S(2)}) collective-permute-start(bf16[4,96,768]{2,1,0:T(8,128)(2,1)S(1)} %pad_maximum_fusion.5), channel_id=1, source_target_pairs={{0,1},{1,0},{2,3},{3,2},{4,5},{5,4},{6,7},{7,6},{8,9},{9,8},{10,11... | collective-permute-start | bytes 1769480 | tf_op jit(solution)/shard_map/ppermute | solution.py:952
  182.3 45.6 %collective-permute-start.38 = (f32[512,768]{1,0:T(8,128)S(1)}, f32[512,768]{1,0:T(8,128)S(1)}, u32[]{:S(2)}, u32[]{:S(2)}) collective-permute-start(f32[512,768]{1,0:T(8,128)S(1)} %get-tuple-element.204), channel_id=1, source_target_pairs={{0,16},{16,0},{1,17},{17,1},{2,18},{18,2},{3,19},{19,3},{4,20},{20... | collective-permute-start | bytes 4718600 | tf_op jit(solution)/shard_map/ppermute | solution.py:938
  185.2 20.3 %collective-permute-start.35 = (bf16[8,64,768]{2,0,1:T(8,128)(2,1)S(1)}, bf16[8,64,768]{2,0,1:T(8,128)(2,1)S(1)}, u32[]{:S(2)}, u32[]{:S(2)}) collective-permute-start(bf16[8,64,768]{2,0,1:T(8,128)(2,1)S(1)} %pad_maximum_fusion.4), channel_id=1, source_target_pairs={{0,1},{1,0},{2,3},{3,2},{4,5},{5,4},{6,7},{7,6},{8,9},{9,8},{10,11... | collective-permute-start | bytes 2359304 | tf_op jit(solution)/shard_map/ppermute | solution.py:952
  187.0 17.5 %collective-permute-start.33 = (bf16[2,48,1536]{2,1,0:T(8,128)(2,1)S(1)}, bf16[2,48,1536]{2,1,0:T(8,128)(2,1)S(1)}, u32[]{:S(2)}, u32[]{:S(2)}) collective-permute-start(bf16[2,48,1536]{2,1,0:T(8,128)(2,1)S(1)} %pad_maximum_fusion.11), channel_id=1, source_target_pairs={{0,4},{1,5},{2,6},{3,7},{4,0},{5,1},{6,2},{7,3},{8,12},{9,13},{10,... | collective-permute-start | bytes 884744 | tf_op jit(solution)/shard_map/ppermute | solution.py:952
  189.5 15.9 %collective-permute-start.36 = (bf16[4,48,1536]{2,1,0:T(8,128)(2,1)S(1)}, bf16[4,48,1536]{2,1,0:T(8,128)(2,1)S(1)}, u32[]{:S(2)}, u32[]{:S(2)}) collective-permute-start(bf16[4,48,1536]{2,1,0:T(8,128)(2,1)S(1)} %pad_maximum_fusion.6), channel_id=1, source_target_pairs={{0,1},{1,0},{2,3},{3,2},{4,5},{5,4},{6,7},{7,6},{8,9},{9,8},{10,11... | collective-permute-start | bytes 1769480 | tf_op jit(solution)/shard_map/ppermute | solution.py:952
  190.4 37.0 %collective-permute-start.39 = (bf16[8,96,768]{2,1,0:T(8,128)(2,1)S(1)}, bf16[8,96,768]{2,1,0:T(8,128)(2,1)S(1)}, u32[]{:S(2)}, u32[]{:S(2)}) collective-permute-start(bf16[8,96,768]{2,1,0:T(8,128)(2,1)S(1)} %pad_maximum_fusion.1.refs_3_), channel_id=1, source_target_pairs={{0,2},{1,3},{2,0},{3,1},{4,6},{5,7},{6,4},{7,5},{8,10},{9,11},{10,... | collective-permute-start | bytes 3538952 | tf_op jit(solution)/shard_map/ppermute | solution.py:952
  204.6 11.4 %collective-permute-start.34 = (bf16[4,48,1536]{2,1,0:T(8,128)(2,1)S(1)}, bf16[4,48,1536]{2,1,0:T(8,128)(2,1)S(1)}, u32[]{:S(2)}, u32[]{:S(2)}) collective-permute-start(bf16[4,48,1536]{2,1,0:T(8,128)(2,1)S(1)} %pad_maximum_fusion.7), channel_id=1, source_target_pairs={{0,2},{1,3},{2,0},{3,1},{4,6},{5,7},{6,4},{7,5},{8,10},{9,11},{10,... | collective-permute-start | bytes 1769480 | tf_op jit(solution)/shard_map/ppermute | solution.py:952
  216.2 12.9 %collective-permute-start.37 = (bf16[512,768]{1,0:T(8,128)(2,1)S(1)}, bf16[512,768]{1,0:T(8,128)(2,1)S(1)}, u32[]{:S(2)}, u32[]{:S(2)}) collective-permute-start(bf16[512,768]{1,0:T(8,128)(2,1)S(1)} %get-tuple-element.203), channel_id=1, source_target_pairs={{0,16},{16,0},{1,17},{17,1},{2,18},{18,2},{3,19},{19,3},{4,20},{20... | collective-permute-start | bytes 2359304 | tf_op jit(solution)/shard_map/ppermute | solution.py:938
  227.9 28.7 %collective-permute-start.41 = (bf16[8,48,1536]{2,1,0:T(8,128)(2,1)S(1)}, bf16[8,48,1536]{2,1,0:T(8,128)(2,1)S(1)}, u32[]{:S(2)}, u32[]{:S(2)}) collective-permute-start(bf16[8,48,1536]{2,1,0:T(8,128)(2,1)S(1)} %pad_maximum_fusion.2.refs_3_), channel_id=1, source_target_pairs={{0,8},{1,9},{2,10},{3,11},{4,12},{5,13},{6,14},{7,15},{8,0},{9,1},... | collective-permute-start | bytes 3538952 | tf_op jit(solution)/shard_map/ppermute | solution.py:952
  229.1 28.1 %collective-permute-start.40 = (bf16[8,48,1536]{2,1,0:T(8,128)(2,1)S(1)}, bf16[8,48,1536]{2,1,0:T(8,128)(2,1)S(1)}, u32[]{:S(2)}, u32[]{:S(2)}) collective-permute-start(bf16[8,48,1536]{2,1,0:T(8,128)(2,1)S(1)} %pad_maximum_fusion.3.b_low), channel_id=1, source_target_pairs={{0,1},{1,0},{2,3},{3,2},{4,5},{5,4},{6,7},{7,6},{8,9},{9,8},{10,11... | collective-permute-start | bytes 3538952 | tf_op jit(solution)/shard_map/ppermute | solution.py:952
  257.2 9.8 %collective-permute-start.46 = (bf16[8,48,1536]{2,1,0:T(8,128)(2,1)S(1)}, bf16[8,48,1536]{2,1,0:T(8,128)(2,1)S(1)}, u32[]{:S(2)}, u32[]{:S(2)}) collective-permute-start(bf16[8,48,1536]{2,1,0:T(8,128)(2,1)S(1)} %collective-permute-done.40.b_high), channel_id=1, source_target_pairs={{0,16},{16,0},{1,17},{17,1},{2,18},{18,2},{3,19},{19,3},{4,20},{20... | collective-permute-start | bytes 3538952 | tf_op jit(solution)/shard_map/ppermute | solution.py:938
  (22 other events, 120.6 us)

commit v5 on v4

--- a/solution.py
+++ b/solution.py
@@ -15,7 +15,6 @@
 BF = jnp.bfloat16
 F32 = jnp.float32
 CHUNK = 768
-STRIP = 512
 GROUP = 16
 ROW_TILE = 16
 ORDERS = (
@@ -272,14 +271,15 @@
     n2, r2 = row_norm(normed + (nn(acts[...], wo[...]) + pick(OUTER_B)))
     put("n2", n2)
     put("r2", r2)
-    e_ref[...] = (n2 * pick(FFN_G) + pick(FFN_B)).astype(BF)
+    e_ref[0:ROW_TILE, :] = table[...]
+    e_ref[ROW_TILE:, :] = (n2 * pick(FFN_G) + pick(FFN_B)).astype(BF).astype(F32)
 
 
 def head_call(info, own, other, wp, wi, wo, table):
     length = own.shape[0]
     width, ff = wi.shape
     kept = max(place + size for place, size in kept_places(width, ff, length).values())
-    shapes = [struct((ROW_TILE, width), BF), struct((ROW_TILE, kept), F32)]
+    shapes = [struct((2 * ROW_TILE, width), F32), struct((ROW_TILE, kept), F32)]
     return pl.pallas_call(
         head_kernel,
         in_specs=[SCALARS, NEAR, NEAR, FAR, FAR, FAR, NEAR],
@@ -379,7 +379,7 @@
 
 
 def train_kernel(
-    info_ref, xq_a, xq_b, wq_a, wq_b, wp_a, wp_b, wi_a, wi_b, wo_a, wo_b, mine, table, head_ref, arrived_ref, cot_ref,
+    info_ref, xq_a, xq_b, wq_a, wq_b, wp_a, wp_b, wi_a, wi_b, wo_a, wo_b, mine, table, cot_ref,
     z_ref, wp, wi, wo, ctx, lse_ref, fixed_ref, n1_ref, r1_ref, slope_ref, gf_ref, sg_ref, small_ref, keep_ref, send_ref,
     xq, lse_scr, sems,
 ):
@@ -397,7 +397,8 @@
     lane = lax.broadcasted_iota(jnp.int32, (length, PAIR), 1)
     row = lax.broadcasted_iota(jnp.int32, (length, PAIR), 0)
     bias_col = jnp.where(row < info_ref[1], 0.0, BIG_NEG).astype(BF)
-    many = jnp.broadcast_to(jnp.where(section == 0, head_ref[0:1, :], arrived_ref[1:2, :]), (ROW_TILE, width))
+    first = jnp.where(section == 0, mine[ROW_TILE : ROW_TILE + 1, :], table[ROW_TILE + 1 : ROW_TILE + 2, :])
+    many = jnp.broadcast_to(first.astype(BF), (ROW_TILE, width))
     fixed = []
     for k, shift in enumerate((pick(QUERY_B), None, pick(VALUE_B))):
         cols, place = thirds[k]
@@ -455,7 +456,7 @@
                 ref[jnp.bitwise_xor(c * each + p, order)] = made[p * rows : (p + 1) * rows, :]
 
 
-def train_call(info, pairs, tables, head, arrived, cot):
+def train_call(info, pairs, tables, cot):
     xq, wq, wp, wi, wo = (piece[0] for piece in pairs)
     length = xq.shape[0]
     width, ff = wi.shape
@@ -464,7 +465,7 @@
     for pair in pairs:
         args += far(*pair)
         in_specs += [FAR, FAR]
-    args += [*tables, head, arrived, *far(cot)]
+    args += [*tables, *far(cot)]
     shapes = [
         struct((length, width), BF),
         near(wp.shape, BF),
@@ -484,7 +485,7 @@
     ]
     return pl.pallas_call(
         train_kernel,
-        in_specs=in_specs + [NEAR] * 4 + [FAR],
+        in_specs=in_specs + [NEAR] * 2 + [FAR],
         out_specs=[NEAR] * len(shapes),
         out_shape=shapes,
         scratch_shapes=[
@@ -608,7 +609,7 @@
         kt = turned(k)
         gc = gc_ref[:, pl.ds(base, PAIR)]
         zero = jnp.zeros_like(gc)
-        strips = [slice(s * STRIP, (s + 1) * STRIP) for s in range(length // STRIP)]
+        strips = [slice(0, length)]
         gk = [None] * len(strips)
         gv = [None] * len(strips)
         gqt = []
@@ -1076,17 +1077,16 @@
     info = jnp.stack(scalars).astype(jnp.int32)
     vectors = [weights[k] for k in (1, 2, 4, 5, 6, 8, 10, 11, 12)]
     own, other, own_table = qkv_call(info, inputs, wq, vectors)
-    tables = (own_table, swap(own_table))
     wq_pair = (wq, swap(wq))
     wp_pair = (wp, swap(wp))
     xq_pair = (own, swap(other))
     wi_pair = (wi, swap(wi))
     wo_pair = (wo, swap(wo))
     head = head_call(info, own, other, wp, wi, wo, own_table)
-    arrived = swap(head[0])
+    tables = (head[0], swap(head[0]))
     pairs = (xq_pair, wq_pair, wp_pair, wi_pair, wo_pair)
     (z, wp_d, wi_d, wo_d, context, lse, fixed, n1, r1, slope, gf, sg, small1, outer_keep, outer_send) = train_call(
-        info, pairs, tables, head[0], arrived, cotangent
+        info, pairs, tables, cotangent
     )
     g1 = Sum(outer_keep, outer_send, 0)
 
@@ -1111,7 +1111,7 @@
     came = swap(line(rest))
     gx_other = swap(line(gx))
     line.halve(g1, 2)
-    (normed,) = line.run(lambda *a: (mixing_call(*a),), info, xq_pair, wp_pair, (own_table, line(tables[1])))
+    (normed,) = line.run(lambda *a: (mixing_call(*a),), info, xq_pair, wp_pair, (tables[0], line(tables[1])))
     line.halve(g2, 1)
     line.halve(g3, 1)
     shared = jnp.where(first_section, heads, jnp.concatenate([line(came)[:SUMS], heads[SUMS:]]))
@@ -1135,28 +1135,28 @@
     line.join(g3, 2)
     line.join(g2, 1)
     line.join(g1, 0)
-    (e_low,) = line.run(lambda *a: (feed_call(*a),), info, line(normed), wi_pair, wo_pair, tables)
     line.join(g3, 1)
     line.join(g2, 0)
     line.join(factors, None)
+    line.join(g3, 0)
     factors.across()
     sums = jnp.sum(line(factors.part)[:, SUMS:].astype(F32), axis=0)
     heads_all = jnp.transpose(factors.part, (1, 0, 2))
     heads_all, sums = line.run(lambda *a: a, heads_all, sums)
-    line.join(g3, 0)
+    (e_low,) = line.run(lambda *a: (feed_call(*a),), info, line(normed), wi_pair, wo_pair, tables)
+    decoder_gx = jnp.stack([line(gx_other), gx])
+    later = jnp.arange(gx.shape[0])[None, :, None] > 0
+    (embed_grads,) = line.run(lambda a: (jnp.where(first_section, encoder_gx, jnp.where(later, a, 0.0)),), decoder_gx)
+    line.take(g1)
+    line.take(g2)
     rest_all = swap(line(heads_all)[:SUMS])
     z_other = swap(line(jnp.where(first_section, z, e_low)))
     z_mine = jnp.where(first_section, e_low, z)
-    line.take(g1)
     outer_quarters = g1.quarters(line)
-    decoder_gx = jnp.stack([line(gx_other), gx])
-    later = jnp.arange(gx.shape[0])[None, :, None] > 0
-    (embed_grads,) = line.run(lambda a: (jnp.where(first_section, encoder_gx, jnp.where(later, a, 0.0)),), decoder_gx)
+    inner_quarters = g2.quarters(line)
     outputs = jnp.where(first_section, jnp.stack([z_mine, line(z_other)]), jnp.stack([z_other, z_mine]))
     (outputs,) = line.run(lambda a: (a,), outputs)
     (outer_grad,) = line.run(lambda *a: (feed_final_call(True, *a),), info, outer_quarters, line(rest_all))
-    line.take(g2)
-    inner_quarters = g2.quarters(line)
     line.take(g3)
     qkv_quarters = g3.quarters(line)
     (inner_grad,) = line.run(lambda *a: (feed_final_call(False, *a),), info, inner_quarters, line(rest_all))

time: 278 us -> 272 us (0.978)
  starting transfers between devices: 55.1 us -> 52 us
  waiting for transfers between devices: 75 us -> 72.1 us
    ppermute x21 -> x20, starting transfers between devices: 18.7 us -> 8.61 us  [swap(): return lax.ppermute(value, 'section', SWAP)]
    ppermute x28, starting transfers between devices: 36.4 us -> 43.4 us  [hop(): return lax.ppermute(value, ('section', 'dp'), pairs)]
    ppermute x28, waiting for transfers between devices: 62.6 us -> 59.6 us  [hop(): return lax.ppermute(value, ('section', 'dp'), pairs)]
    ppermute x21 -> x20, waiting for transfers between devices: 12.3 us -> 12.4 us  [swap(): return lax.ppermute(value, 'section', SWAP)]
  transfers between devices with their start and end apart: 49 -> 48, of which waited for: 20 -> 16; matrix products, arithmetic and copies ran while one was open for 4% -> 4% of each run, Pallas kernels for 34% -> 35%
where the time goes in v5:
time: 272 us; the launch traced here: 266 us
  Pallas kernels  124 us (46%)
  waiting for transfers between devices  72.1 us (27%)
  starting transfers between devices  52 us (19%)
  other arithmetic  9.64 us (4%)
  local copies, waits for them, and re-layouts  4.93 us (2%)
  between operations  3.93 us (1%)
    ppermute x28, waiting for transfers between devices, hop(): return lax.ppermute(value, ('section', 'dp'), pairs)  59.6 us
    ppermute x28, starting transfers between devices, hop(): return lax.ppermute(value, ('section', 'dp'), pairs)  43.4 us
    pallas_call x1, Pallas kernels, train_call(): pl.pallas_call(train_kernel, in_specs=in_specs + [NEAR] * 2 + [FAR], out_...  26.3 us
    pallas_call x1, Pallas kernels, attention_call(): pl.pallas_call(attention_kernel, in_specs=[SCALARS, FAR, FAR] + [NEAR] *...  16.4 us
    pallas_call x1, Pallas kernels, feed_call(): pl.pallas_call(feed_kernel, in_specs=[SCALARS, NEAR] + [FAR] * 4 + [NEAR]...  12.7 us
    ppermute x20, waiting for transfers between devices, swap(): return lax.ppermute(value, 'section', SWAP)  12.4 us
    pallas_call x2, Pallas kernels, feed_final_call(): pl.pallas_call(lambda *refs: feed_final_kernel(outer, *refs), in_specs=[S...  11.6 us
    pallas_call x1, Pallas kernels, mixing_call(): pl.pallas_call(mixing_kernel, in_specs=[SCALARS] + [FAR] * 4 + [NEAR] * 2...  11.3 us
  transfers between devices with their start and end apart: 48, of which 16 were waited for; matrix products, arithmetic and copies ran while one was open for 4% of the time, Pallas kernels for 35%

profile of v5, /device:TPU:0, one launch (start us, length us, event | category | flops | bytes accessed | tf_op | source)
XLA Modules:
  0.0 266.5 jit_solution(8758169371106290572)
XLA Ops:
  5.7 7.6 %qkv.1 = (bf16[512,3072]{1,0:T(8,128)(2,1)S(1)}, bf16[512,3072]{1,0:T(8,128)(2,1)S(1)}, f32[16,768]{1,0:T(8,128)S(1)}) custom-call(s32[9]{0:T(128)S(1)} %stack.64.info_ref.refs_0_, bf16[2,512,768]{2,1,0:T(8,128)(2,1)} %bitcast.64, bf16[768,2304]{1,0:T(8,128)(2,1)} %bitcast.49, f32[1,768]{1,0:T(1,128)} %refs_0_.1, f32[1,768]{1,0:T(1,128)} %refs_1_.1, ...), custom_call_target="tpu_custom_call" | custom-call | flops 660000000 | bytes 1200000 | tf_op jit(solution)/shard_map/qkv/pallas_call | solution.py:167
  13.4 7.1 %head_rows.1 = (f32[32,768]{1,0:T(8,128)S(1)}, f32[16,9728]{1,0:T(8,128)S(1)}) custom-call(s32[9]{0:T(128)S(1)} %stack.64.info_ref.refs_0_, bf16[512,3072]{1,0:T(8,128)(2,1)S(1)} %get-tuple-element.119.own_ref.xq_a, bf16[512,3072]{1,0:T(8,128)(2,1)S(1)} %get-tuple-element.120.other_ref, bf16[768,768]{1,0:T(8,128)(2,1)} %bitcast.53, ...), custom_call_target="tpu_custom_call" | custom-call | flops 770000000 | bytes 1400000 | tf_op jit(solution)/shard_map/head_rows/pallas_call | solution.py:283
  21.0 3.7 %collective-permute-done.2.table.other = f32[32,768]{1,0:T(8,128)S(1)} collective-permute-done((f32[32,768]{1,0:T(8,128)S(1)}, f32[32,768]{1,0:T(8,128)S(1)}, u32[]{:S(2)}, u32[]{:S(2)}) %collective-permute-start.2) | collective-permute-done | bytes 98336 | tf_op jit(solution)/shard_map/ppermute | solution.py:939
  25.1 2.5 collective-permute-done.1.wp_b
  29.6 26.3 %layer_train.1 = (bf16[512,768]{1,0:T(8,128)(2,1)S(1)}, bf16[768,768]{1,0:T(8,128)(2,1)S(1)}, bf16[768,3072]{1,0:T(8,128)(2,1)S(1)}, bf16[3072,768]{1,0:T(8,128)...) custom-call(s32[9]{0:T(128)S(1)} %stack.64.info_ref.refs_0_, ...), custom_call_target="tpu_custom_call" | custom-call | flops 2860000000 | bytes 5200000 | tf_op jit(solution)/shard_map/layer_train/pallas_call | solution.py:486
  56.3 9.9 %inner_grad.1 = (bf16[16,48,1536]{2,1,0:T(8,128)(2,1)S(1)}, bf16[16,48,1536]{2,1,0:T(8,128)(2,1)S(1)}, f32[512,768]{1,0:T(8,128)S(1)}, bf16[512,768]{1,0:T(8,128...) custom-call(s32[9]{0:T(128)S(1)} %stack.64.info_ref.refs_0_, ...), custom_call_target="tpu_custom_call" | custom-call | flops 1100000000 | bytes 2000000 | tf_op jit(solution)/shard_map/inner_grad/pallas_call | solution.py:576
  67.2 3.0 %collective-permute-start.7 = (bf16[8,96,768]{2,1,0:T(8,128)(2,1)S(1)}, bf16[8,96,768]{2,1,0:T(8,128)(2,1)S(1)}, u32[]{:S(2)}, u32[]{:S(2)}) collective-permute-start(bf16[8,96,768]{2,1,0:T(8,128)(2,1)S(1)} %get-tuple-element.227), channel_id=1, source_target_pairs={{0,2},{1,3},{2,0},{3,1},{4,6},{5,7},{6,4},{7,5},{8,10},{9,11},{10,... | collective-permute-start | bytes 3538952 | tf_op jit(solution)/shard_map/ppermute | solution.py:953
  70.2 16.4 %attention_grad.1 = (bf16[16,48,1536]{2,1,0:T(8,128)(2,1)S(1)}, bf16[16,48,1536]{2,1,0:T(8,128)(2,1)S(1)}, bf16[512,2304]{1,0:T(8,128)(2,1)S(1)}, f32[8,768]{1,0:T(8,128)S(1)}) custom-call(s32[9]{0:T(128)S(1)} %stack.64.info_ref.refs_0_, bf16[512,3072]{1,0:T(8,128)(2,1)} %copy-done, bf16[512,3072]{1,0:T(8,128)(2,1)} %copy-done.2, ...), custom_call_target="tpu_custom_call" | custom-call | flops 1540000000 | bytes 2800000 | tf_op jit(solution)/shard_map/attention_grad/pallas_call | solution.py:658
  87.8 4.6 %input_grad.1 = (f32[512,768]{1,0:T(8,128)S(1)}, f32[16,768]{1,0:T(8,128)S(1)}) custom-call(s32[9]{0:T(128)S(1)} %stack.64.info_ref.refs_0_, bf16[768,2304]{1,0:T(8,128)(2,1)} %bitcast.51, bf16[768,2304]{1,0:T(8,128)(2,1)} %collective-permute-done.3.wq_b.w_b, bf16[512,2304]{1,0:T(8,128)(2,1)S(1)} %get-tuple-element.155.g_ref, ...), custom_call_target="tpu_custom_call" | custom-call | flops 440000000 | bytes 800000 | tf_op jit(solution)/shard_map/input_grad/pallas_call | solution.py:688
  93.9 2.6 collective-permute-start.14
  99.1 11.1 %head_rows_grad.1 = (f32[2,512,768]{2,1,0:T(8,128)S(1)}, bf16[64,768]{1,0:T(8,128)(2,1)S(1)}, bf16[64,768]{1,0:T(8,128)(2,1)S(1)}) custom-call(s32[9]{0:T(128)S(1)} %stack.64.info_ref.refs_0_, f32[16,768]{1,0:T(8,128)S(1)} %get-tuple-element.162.small_a, f32[16,768]{1,0:T(8,128)S(1)} %collective-permute-done.10.small_b, ...), custom_call_target="tpu_custom_call" | custom-call | flops 1320000000 | bytes 2400000 | tf_op jit(solution)/shard_map/head_rows_grad/pallas_call | solution.py:792
  110.4 11.3 %mixing.1.normed_ref = f32[512,768]{1,0:T(8,128)S(1)} custom-call(s32[9]{0:T(128)S(1)} %stack.64.info_ref.refs_0_, bf16[512,3072]{1,0:T(8,128)(2,1)} %copy-done, bf16[512,3072]{1,0:T(8,128)(2,1)} %copy-done.2, bf16[768,768]{1,0:T(8,128)(2,1)} %bitcast.56, bf16[768,768]{1,0:T(8,128)(2,1)} %copy-done.4, f32[32,768]{1,0:T(8,128)S(1)} %get-tuple-element.122.mine, ...), custom_call_target="tpu_custom_call" | custom-call | flops 1100000000 | bytes 2000000 | tf_op jit(solution)/shard_map/mixing/pallas_call | solution.py:364
  125.6 8.8 %collective-permute-done.17 = bf16[2,96,768]{2,1,0:T(8,128)(2,1)S(1)} collective-permute-done((bf16[2,96,768]{2,1,0:T(8,128)(2,1)S(1)}, bf16[2,96,768]{2,1,0:T(8,128)(2,1)S(1)}, u32[]{:S(2)}, u32[]{:S(2)}) %collective-permute-start.17) | collective-permute-done | bytes 294944 | tf_op jit(solution)/shard_map/ppermute | solution.py:953
  134.4 2.6 collective-permute-start.15
  141.9 5.5 %collective-permute-start.18 = (bf16[2,64,768]{2,0,1:T(2,128)(2,1)S(1)}, bf16[2,64,768]{2,0,1:T(2,128)(2,1)S(1)}, u32[]{:S(2)}, u32[]{:S(2)}) collective-permute-start(bf16[2,64,768]{2,0,1:T(2,128)(2,1)S(1)} %pad_maximum_fusion.12), channel_id=1, source_target_pairs={{0,4},{1,5},{2,6},{3,7},{4,0},{5,1},{6,2},{7,3},{8,12},{9,13},{10,... | collective-permute-start | bytes 589832 | tf_op jit(solution)/shard_map/ppermute | solution.py:953
  148.3 4.9 %collective-permute-done.18 = bf16[2,64,768]{2,0,1:T(2,128)(2,1)S(1)} collective-permute-done((bf16[2,64,768]{2,0,1:T(2,128)(2,1)S(1)}, bf16[2,64,768]{2,0,1:T(2,128)(2,1)S(1)}, u32[]{:S(2)}, u32[]{:S(2)}) %collective-permute-start.18) | collective-permute-done | bytes 196640 | tf_op jit(solution)/shard_map/ppermute | solution.py:953
  156.4 6.7 %collective-permute-done.25 = bf16[2,48,1536]{2,1,0:T(8,128)(2,1)S(1)} collective-permute-done((bf16[2,48,1536]{2,1,0:T(8,128)(2,1)S(1)}, bf16[2,48,1536]{2,1,0:T(8,128)(2,1)S(1)}, u32[]{:S(2)}, u32[]{:S(2)}) %collective-permute-start.25) | collective-permute-done | bytes 294944 | tf_op jit(solution)/shard_map/ppermute | solution.py:953
  167.0 2.5 collective-permute-start.27
  169.9 9.1 %collective-permute-done.28 = bf16[1,48,1536]{2,1,0:T(8,128)(2,1)S(1)} collective-permute-done((bf16[1,48,1536]{2,1,0:T(8,128)(2,1)S(1)}, bf16[1,48,1536]{2,1,0:T(8,128)(2,1)S(1)}, u32[]{:S(2)}, u32[]{:S(2)}) %collective-permute-start.28) | collective-permute-done | bytes 147488 | tf_op jit(solution)/shard_map/ppermute | solution.py:953
  181.5 4.5 %collective-permute-done.30 = bf16[1,48,1536]{2,1,0:T(8,128)(2,1)S(1)} collective-permute-done((bf16[1,48,1536]{2,1,0:T(8,128)(2,1)S(1)}, bf16[1,48,1536]{2,1,0:T(8,128)(2,1)S(1)}, u32[]{:S(2)}, u32[]{:S(2)}) %collective-permute-start.30) | collective-permute-done | bytes 147488 | tf_op jit(solution)/shard_map/ppermute | solution.py:953
  186.1 2.1 collective-permute-start.32
  188.3 2.3 collective-permute-start.33
  190.5 3.6 %collective-permute-start.38 = (f32[512,768]{1,0:T(8,128)S(1)}, f32[512,768]{1,0:T(8,128)S(1)}, u32[]{:S(2)}, u32[]{:S(2)}) collective-permute-start(f32[512,768]{1,0:T(8,128)S(1)} %get-tuple-element.203), channel_id=1, source_target_pairs={{0,16},{16,0},{1,17},{17,1},{2,18},{18,2},{3,19},{19,3},{4,20},{20... | collective-permute-start | bytes 4718600 | tf_op jit(solution)/shard_map/ppermute | solution.py:939
  195.8 6.1 %collective-permute-done.33 = bf16[2,48,1536]{2,1,0:T(8,128)(2,1)S(1)} collective-permute-done((bf16[2,48,1536]{2,1,0:T(8,128)(2,1)S(1)}, bf16[2,48,1536]{2,1,0:T(8,128)(2,1)S(1)}, u32[]{:S(2)}, u32[]{:S(2)}) %collective-permute-start.33) | collective-permute-done | bytes 294944 | tf_op jit(solution)/shard_map/ppermute | solution.py:953
  204.2 2.9 %collective-permute-start.36 = (bf16[8,48,1536]{2,1,0:T(8,128)(2,1)S(1)}, bf16[8,48,1536]{2,1,0:T(8,128)(2,1)S(1)}, u32[]{:S(2)}, u32[]{:S(2)}) collective-permute-start(bf16[8,48,1536]{2,1,0:T(8,128)(2,1)S(1)} %pad_maximum_fusion.2.refs_3_), channel_id=1, source_target_pairs={{0,8},{1,9},{2,10},{3,11},{4,12},{5,13},{6,14},{7,15},{8,0},{9,1},... | collective-permute-start | bytes 3538952 | tf_op jit(solution)/shard_map/ppermute | solution.py:953
  207.2 4.7 %collective-permute-done.35 = bf16[4,48,1536]{2,1,0:T(8,128)(2,1)S(1)} collective-permute-done((bf16[4,48,1536]{2,1,0:T(8,128)(2,1)S(1)}, bf16[4,48,1536]{2,1,0:T(8,128)(2,1)S(1)}, u32[]{:S(2)}, u32[]{:S(2)}) %collective-permute-start.35) | collective-permute-done | bytes 589856 | tf_op jit(solution)/shard_map/ppermute | solution.py:953
  212.1 12.7 %layer_feed.1 = bf16[512,768]{1,0:T(8,128)(2,1)S(1)} custom-call(s32[9]{0:T(128)S(1)} %stack.64.info_ref.refs_0_, f32[512,768]{1,0:T(8,128)S(1)} %mixing.1.normed_ref, bf16[768,3072]{1,0:T(8,128)(2,1)} %bitcast.42, bf16[768,3072]{1,0:T(8,128)(2,1)} %collective-permute-done.4.wi_b, bf16[3072,768]{1,0:T(8,128)(2,1)} %bitcast.47, ...), custom_call_target="tpu_custom_call" | custom-call | flops 1210000000 | bytes 2200000 | tf_op jit(solution)/shard_map/layer_feed/pallas_call | solution.py:522
  226.9 9.6 %collective-permute-done.37.refs_4_ = bf16[8,96,768]{2,1,0:T(8,128)(2,1)S(1)} collective-permute-done((bf16[8,96,768]{2,1,0:T(8,128)(2,1)S(1)}, bf16[8,96,768]{2,1,0:T(8,128)(2,1)S(1)}, u32[]{:S(2)}, u32[]{:S(2)}) %collective-permute-start.37) | collective-permute-done | bytes 1179680 | tf_op jit(solution)/shard_map/ppermute | solution.py:953
  239.3 5.0 %collective-permute-done.39 = bf16[512,768]{1,0:T(8,128)(2,1)S(1)} collective-permute-done((bf16[512,768]{1,0:T(8,128)(2,1)S(1)}, bf16[512,768]{1,0:T(8,128)(2,1)S(1)}, u32[]{:S(2)}, u32[]{:S(2)}) %collective-permute-start.39) | collective-permute-done | bytes 786464 | tf_op jit(solution)/shard_map/ppermute | solution.py:939
  246.2 5.8 %outer_final.1 = f32[3072,768]{1,0:T(8,128)} custom-call(s32[9]{0:T(128)S(1)} %stack.64.info_ref.refs_0_, bf16[8,96,768]{2,1,0:T(8,128)(2,1)S(1)} %collective-permute-done.41.refs_1_, bf16[8,96,768]{2,1,0:T(8,128)(2,1)S(1)} %collective-permute-done.42.refs_2_, bf16[8,96,768]{2,1,0:T(8,128)(2,1)S(1)} %pad_maximum_fusion.1.refs_3_, ...), custom_call_target="tpu_custom_call" | custom-call | flops 440000000 | bytes 800000 | tf_op jit(solution)/shard_map/outer_final/pallas_call | solution.py:852
  255.1 5.8 %inner_final.1 = f32[768,3072]{1,0:T(8,128)} custom-call(s32[9]{0:T(128)S(1)} %stack.64.info_ref.refs_0_, bf16[8,48,1536]{2,1,0:T(8,128)(2,1)S(1)} %collective-permute-done.46.refs_1_, bf16[8,48,1536]{2,1,0:T(8,128)(2,1)S(1)} %collective-permute-done.47.refs_2_, bf16[8,48,1536]{2,1,0:T(8,128)(2,1)S(1)} %pad_maximum_fusion.2.refs_3_, ...), custom_call_target="tpu_custom_call" | custom-call | flops 440000000 | bytes 800000 | tf_op jit(solution)/shard_map/inner_final/pallas_call | solution.py:852
  260.9 5.3 %qkv_final.1 = (f32[768,2304]{1,0:T(8,128)}, f32[768,768]{1,0:T(8,128)}) custom-call(s32[9]{0:T(128)S(1)} %stack.64.info_ref.refs_0_, bf16[8,48,1536]{2,1,0:T(8,128)(2,1)S(1)} %collective-permute-done.44.a_low, bf16[8,48,1536]{2,1,0:T(8,128)(2,1)S(1)} %collective-permute-done.45.a_high, bf16[8,48,1536]{2,1,0:T(8,128)(2,1)S(1)} %pad_maximum_fusion.3.b_low, ...), custom_call_target="tpu_custom_call" | custom-call | flops 440000000 | bytes 800000 | tf_op jit(solution)/shard_map/qkv_final/pallas_call | solution.py:922
  (129 shorter events, 46.0 us)
Async XLA Ops:
  0.6 26.9 %collective-permute-start.4 = (bf16[768,3072]{1,0:T(8,128)(2,1)}, bf16[768,3072]{1,0:T(8,128)(2,1)}, u32[]{:S(2)}, u32[]{:S(2)}) collective-permute-start(bf16[768,3072]{1,0:T(8,128)(2,1)} %bitcast.38), channel_id=1, source_target_pairs={{0,16},{16,0},{1,17},{17,1},{2,18},{18,2},{3,19},{19,3},{4,20},{20... | collective-permute-start | bytes 14155784 | tf_op jit(solution)/shard_map/ppermute | solution.py:939
  1.2 26.4 %collective-permute-start.5 = (bf16[3072,768]{1,0:T(8,128)(2,1)}, bf16[3072,768]{1,0:T(8,128)(2,1)}, u32[]{:S(2)}, u32[]{:S(2)}) collective-permute-start(bf16[3072,768]{1,0:T(8,128)(2,1)} %bitcast.43), channel_id=1, source_target_pairs={{0,16},{16,0},{1,17},{17,1},{2,18},{18,2},{3,19},{19,3},{4,20},{20... | collective-permute-start | bytes 14155784 | tf_op jit(solution)/shard_map/ppermute | solution.py:939
  1.2 26.3 %collective-permute-start.3 = (bf16[768,2304]{1,0:T(8,128)(2,1)}, bf16[768,2304]{1,0:T(8,128)(2,1)}, u32[]{:S(2)}, u32[]{:S(2)}) collective-permute-start(bf16[768,2304]{1,0:T(8,128)(2,1)} %bitcast.48), channel_id=1, source_target_pairs={{0,16},{16,0},{1,17},{17,1},{2,18},{18,2},{3,19},{19,3},{4,20},{20... | collective-permute-start | bytes 10616840 | tf_op jit(solution)/shard_map/ppermute | solution.py:939
  13.3 14.3 %collective-permute-start = (bf16[512,3072]{1,0:T(8,128)(2,1)S(1)}, bf16[512,3072]{1,0:T(8,128)(2,1)S(1)}, u32[]{:S(2)}, u32[]{:S(2)}) collective-permute-start(bf16[512,3072]{1,0:T(8,128)(2,1)S(1)} %get-tuple-element.120.other_ref), channel_id=1, source_target_pairs={{0,16},{16,0},{1,17},{17,1},{2,18},{18,2},{3,19},{19,3},{4,20},{20... | collective-permute-start | bytes 9437192 | tf_op jit(solution)/shard_map/ppermute | solution.py:939
  55.9 10.4 %collective-permute-start.6 = (bf16[16,96,768]{2,1,0:T(8,128)(2,1)S(1)}, bf16[16,96,768]{2,1,0:T(8,128)(2,1)S(1)}, u32[]{:S(2)}, u32[]{:S(2)}) collective-permute-start(bf16[16,96,768]{2,1,0:T(8,128)(2,1)S(1)} %get-tuple-element.138), channel_id=1, source_target_pairs={{0,16},{16,0},{1,17},{17,1},{2,18},{18,2},{3,19},{19,3},{4,20},{20... | collective-permute-start | bytes 7077896 | tf_op jit(solution)/shard_map/ppermute | solution.py:939
  66.3 20.3 %collective-permute-start.8 = (bf16[16,48,1536]{2,1,0:T(8,128)(2,1)S(1)}, bf16[16,48,1536]{2,1,0:T(8,128)(2,1)S(1)}, u32[]{:S(2)}, u32[]{:S(2)}) collective-permute-start(bf16[16,48,1536]{2,1,0:T(8,128)(2,1)S(1)} %get-tuple-element.152), channel_id=1, source_target_pairs={{0,16},{16,0},{1,17},{17,1},{2,18},{18,2},{3,19},{19,3},{4,20},{20... | collective-permute-start | bytes 7077896 | tf_op jit(solution)/shard_map/ppermute | solution.py:939
  67.2 19.4 %collective-permute-start.7 = (bf16[8,96,768]{2,1,0:T(8,128)(2,1)S(1)}, bf16[8,96,768]{2,1,0:T(8,128)(2,1)S(1)}, u32[]{:S(2)}, u32[]{:S(2)}) collective-permute-start(bf16[8,96,768]{2,1,0:T(8,128)(2,1)S(1)} %get-tuple-element.227), channel_id=1, source_target_pairs={{0,2},{1,3},{2,0},{3,1},{4,6},{5,7},{6,4},{7,5},{8,10},{9,11},{10,... | collective-permute-start | bytes 3538952 | tf_op jit(solution)/shard_map/ppermute | solution.py:953
  92.4 17.9 %collective-permute-start.9 = (bf16[4,96,768]{2,1,0:T(8,128)(2,1)S(1)}, bf16[4,96,768]{2,1,0:T(8,128)(2,1)S(1)}, u32[]{:S(2)}, u32[]{:S(2)}) collective-permute-start(bf16[4,96,768]{2,1,0:T(8,128)(2,1)S(1)} %get-tuple-element.233), channel_id=1, source_target_pairs={{0,1},{1,0},{2,3},{3,2},{4,5},{5,4},{6,7},{7,6},{8,9},{9,8},{10,11... | collective-permute-start | bytes 1769480 | tf_op jit(solution)/shard_map/ppermute | solution.py:953
  93.9 29.8 %collective-permute-start.14 = (bf16[8,48,1536]{2,1,0:T(8,128)(2,1)S(1)}, bf16[8,48,1536]{2,1,0:T(8,128)(2,1)S(1)}, u32[]{:S(2)}, u32[]{:S(2)}) collective-permute-start(bf16[8,48,1536]{2,1,0:T(8,128)(2,1)S(1)} %get-tuple-element.223), channel_id=1, source_target_pairs={{0,8},{1,9},{2,10},{3,11},{4,12},{5,13},{6,14},{7,15},{8,0},{9,1},... | collective-permute-start | bytes 3538952 | tf_op jit(solution)/shard_map/ppermute | solution.py:953
  97.3 27.7 %collective-permute-start.13 = (bf16[8,48,1536]{2,1,0:T(8,128)(2,1)S(1)}, bf16[8,48,1536]{2,1,0:T(8,128)(2,1)S(1)}, u32[]{:S(2)}, u32[]{:S(2)}) collective-permute-start(bf16[8,48,1536]{2,1,0:T(8,128)(2,1)S(1)} %get-tuple-element.225), channel_id=1, source_target_pairs={{0,1},{1,0},{2,3},{3,2},{4,5},{5,4},{6,7},{7,6},{8,9},{9,8},{10,11... | collective-permute-start | bytes 3538952 | tf_op jit(solution)/shard_map/ppermute | solution.py:953
  123.7 10.6 %collective-permute-start.17 = (bf16[2,96,768]{2,1,0:T(8,128)(2,1)S(1)}, bf16[2,96,768]{2,1,0:T(8,128)(2,1)S(1)}, u32[]{:S(2)}, u32[]{:S(2)}) collective-permute-start(bf16[2,96,768]{2,1,0:T(8,128)(2,1)S(1)} %get-tuple-element.241), channel_id=1, source_target_pairs={{0,8},{1,9},{2,10},{3,11},{4,12},{5,13},{6,14},{7,15},{8,0},{9,1},... | collective-permute-start | bytes 884744 | tf_op jit(solution)/shard_map/ppermute | solution.py:953
  124.1 10.3 %collective-permute-start.16 = (bf16[4,48,1536]{2,1,0:T(8,128)(2,1)S(1)}, bf16[4,48,1536]{2,1,0:T(8,128)(2,1)S(1)}, u32[]{:S(2)}, u32[]{:S(2)}) collective-permute-start(bf16[4,48,1536]{2,1,0:T(8,128)(2,1)S(1)} %get-tuple-element.231), channel_id=1, source_target_pairs={{0,1},{1,0},{2,3},{3,2},{4,5},{5,4},{6,7},{7,6},{8,9},{9,8},{10,11... | collective-permute-start | bytes 1769480 | tf_op jit(solution)/shard_map/ppermute | solution.py:953
  137.0 10.4 %collective-permute-start.20 = (bf16[4,48,1536]{2,1,0:T(8,128)(2,1)S(1)}, bf16[4,48,1536]{2,1,0:T(8,128)(2,1)S(1)}, u32[]{:S(2)}, u32[]{:S(2)}) collective-permute-start(bf16[4,48,1536]{2,1,0:T(8,128)(2,1)S(1)} %get-tuple-element.229), channel_id=1, source_target_pairs={{0,2},{1,3},{2,0},{3,1},{4,6},{5,7},{6,4},{7,5},{8,10},{9,11},{10,... | collective-permute-start | bytes 1769480 | tf_op jit(solution)/shard_map/ppermute | solution.py:953
  137.7 9.9 %collective-permute-start.19 = (bf16[1,96,768]{2,1,0:T(8,128)(2,1)S(1)}, bf16[1,96,768]{2,1,0:T(8,128)(2,1)S(1)}, u32[]{:S(2)}, u32[]{:S(2)}) collective-permute-start(bf16[1,96,768]{2,1,0:T(8,128)(2,1)S(1)} %get-tuple-element.247), channel_id=1, source_target_pairs={{0,4},{1,5},{2,6},{3,7},{4,0},{5,1},{6,2},{7,3},{8,12},{9,13},{10,... | collective-permute-start | bytes 442376 | tf_op jit(solution)/shard_map/ppermute | solution.py:953
  138.9 15.2 %collective-permute-start.22 = (bf16[2,48,1536]{2,1,0:T(8,128)(2,1)S(1)}, bf16[2,48,1536]{2,1,0:T(8,128)(2,1)S(1)}, u32[]{:S(2)}, u32[]{:S(2)}) collective-permute-start(bf16[2,48,1536]{2,1,0:T(8,128)(2,1)S(1)} %get-tuple-element.239), channel_id=1, source_target_pairs={{0,2},{1,3},{2,0},{3,1},{4,6},{5,7},{6,4},{7,5},{8,10},{9,11},{10,... | collective-permute-start | bytes 884744 | tf_op jit(solution)/shard_map/ppermute | solution.py:953
  141.9 11.3 %collective-permute-start.18 = (bf16[2,64,768]{2,0,1:T(2,128)(2,1)S(1)}, bf16[2,64,768]{2,0,1:T(2,128)(2,1)S(1)}, u32[]{:S(2)}, u32[]{:S(2)}) collective-permute-start(bf16[2,64,768]{2,0,1:T(2,128)(2,1)S(1)} %pad_maximum_fusion.12), channel_id=1, source_target_pairs={{0,4},{1,5},{2,6},{3,7},{4,0},{5,1},{6,2},{7,3},{8,12},{9,13},{10,... | collective-permute-start | bytes 589832 | tf_op jit(solution)/shard_map/ppermute | solution.py:953
  147.6 15.5 %collective-permute-start.24 = (bf16[1,96,768]{2,1,0:T(8,128)(2,1)S(1)}, bf16[1,96,768]{2,1,0:T(8,128)(2,1)S(1)}, u32[]{:S(2)}, u32[]{:S(2)}) collective-permute-start(bf16[1,96,768]{2,1,0:T(8,128)(2,1)S(1)} %add_convert_fusion.24), channel_id=1, source_target_pairs={{0,4},{1,5},{2,6},{3,7},{4,0},{5,1},{6,2},{7,3},{8,12},{9,13},{10,... | collective-permute-start | bytes 442376 | tf_op jit(solution)/shard_map/ppermute | solution.py:953
  153.6 15.9 %collective-permute-start.21 = (bf16[4,64,768]{2,0,1:T(4,128)(2,1)S(1)}, bf16[4,64,768]{2,0,1:T(4,128)(2,1)S(1)}, u32[]{:S(2)}, u32[]{:S(2)}) collective-permute-start(bf16[4,64,768]{2,0,1:T(4,128)(2,1)S(1)} %pad_maximum_fusion.8), channel_id=1, source_target_pairs={{0,2},{1,3},{2,0},{3,1},{4,6},{5,7},{6,4},{7,5},{8,10},{9,11},{10,... | collective-permute-start | bytes 1179656 | tf_op jit(solution)/shard_map/ppermute | solution.py:953
  163.2 17.5 %collective-permute-start.31 = (bf16[2,96,768]{2,1,0:T(8,128)(2,1)S(1)}, bf16[2,96,768]{2,1,0:T(8,128)(2,1)S(1)}, u32[]{:S(2)}, u32[]{:S(2)}) collective-permute-start(bf16[2,96,768]{2,1,0:T(8,128)(2,1)S(1)} %pad_maximum_fusion.9), channel_id=1, source_target_pairs={{0,8},{1,9},{2,10},{3,11},{4,12},{5,13},{6,14},{7,15},{8,0},{9,1},... | collective-permute-start | bytes 884744 | tf_op jit(solution)/shard_map/ppermute | solution.py:953
  165.4 13.7 %collective-permute-start.28 = (bf16[1,48,1536]{2,1,0:T(8,128)(2,1)S(1)}, bf16[1,48,1536]{2,1,0:T(8,128)(2,1)S(1)}, u32[]{:S(2)}, u32[]{:S(2)}) collective-permute-start(bf16[1,48,1536]{2,1,0:T(8,128)(2,1)S(1)} %get-tuple-element.243), channel_id=1, source_target_pairs={{0,8},{1,9},{2,10},{3,11},{4,12},{5,13},{6,14},{7,15},{8,0},{9,1},... | collective-permute-start | bytes 442376 | tf_op jit(solution)/shard_map/ppermute | solution.py:953
  167.0 12.2 %collective-permute-start.27 = (bf16[1,48,1536]{2,1,0:T(8,128)(2,1)S(1)}, bf16[1,48,1536]{2,1,0:T(8,128)(2,1)S(1)}, u32[]{:S(2)}, u32[]{:S(2)}) collective-permute-start(bf16[1,48,1536]{2,1,0:T(8,128)(2,1)S(1)} %add_convert_fusion.20), channel_id=1, source_target_pairs={{0,4},{1,5},{2,6},{3,7},{4,0},{5,1},{6,2},{7,3},{8,12},{9,13},{10,... | collective-permute-start | bytes 442376 | tf_op jit(solution)/shard_map/ppermute | solution.py:953
  180.8 14.9 %collective-permute-start.34 = (bf16[4,96,768]{2,1,0:T(8,128)(2,1)S(1)}, bf16[4,96,768]{2,1,0:T(8,128)(2,1)S(1)}, u32[]{:S(2)}, u32[]{:S(2)}) collective-permute-start(bf16[4,96,768]{2,1,0:T(8,128)(2,1)S(1)} %pad_maximum_fusion.5), channel_id=1, source_target_pairs={{0,1},{1,0},{2,3},{3,2},{4,5},{5,4},{6,7},{7,6},{8,9},{9,8},{10,11... | collective-permute-start | bytes 1769480 | tf_op jit(solution)/shard_map/ppermute | solution.py:953
  186.1 17.9 %collective-permute-start.32 = (bf16[4,48,1536]{2,1,0:T(8,128)(2,1)S(1)}, bf16[4,48,1536]{2,1,0:T(8,128)(2,1)S(1)}, u32[]{:S(2)}, u32[]{:S(2)}) collective-permute-start(bf16[4,48,1536]{2,1,0:T(8,128)(2,1)S(1)} %pad_maximum_fusion.6), channel_id=1, source_target_pairs={{0,1},{1,0},{2,3},{3,2},{4,5},{5,4},{6,7},{7,6},{8,9},{9,8},{10,11... | collective-permute-start | bytes 1769480 | tf_op jit(solution)/shard_map/ppermute | solution.py:953
  188.3 13.6 %collective-permute-start.33 = (bf16[2,48,1536]{2,1,0:T(8,128)(2,1)S(1)}, bf16[2,48,1536]{2,1,0:T(8,128)(2,1)S(1)}, u32[]{:S(2)}, u32[]{:S(2)}) collective-permute-start(bf16[2,48,1536]{2,1,0:T(8,128)(2,1)S(1)} %pad_maximum_fusion.11), channel_id=1, source_target_pairs={{0,4},{1,5},{2,6},{3,7},{4,0},{5,1},{6,2},{7,3},{8,12},{9,13},{10,... | collective-permute-start | bytes 884744 | tf_op jit(solution)/shard_map/ppermute | solution.py:953
  190.5 34.3 %collective-permute-start.38 = (f32[512,768]{1,0:T(8,128)S(1)}, f32[512,768]{1,0:T(8,128)S(1)}, u32[]{:S(2)}, u32[]{:S(2)}) collective-permute-start(f32[512,768]{1,0:T(8,128)S(1)} %get-tuple-element.203), channel_id=1, source_target_pairs={{0,16},{16,0},{1,17},{17,1},{2,18},{18,2},{3,19},{19,3},{4,20},{20... | collective-permute-start | bytes 4718600 | tf_op jit(solution)/shard_map/ppermute | solution.py:939
  194.1 13.0 %collective-permute-start.26 = (bf16[8,64,768]{2,0,1:T(8,128)(2,1)S(1)}, bf16[8,64,768]{2,0,1:T(8,128)(2,1)S(1)}, u32[]{:S(2)}, u32[]{:S(2)}) collective-permute-start(bf16[8,64,768]{2,0,1:T(8,128)(2,1)S(1)} %pad_maximum_fusion.4), channel_id=1, source_target_pairs={{0,1},{1,0},{2,3},{3,2},{4,5},{5,4},{6,7},{7,6},{8,9},{9,8},{10,11... | collective-permute-start | bytes 2359304 | tf_op jit(solution)/shard_map/ppermute | solution.py:953
  202.0 9.9 %collective-permute-start.35 = (bf16[4,48,1536]{2,1,0:T(8,128)(2,1)S(1)}, bf16[4,48,1536]{2,1,0:T(8,128)(2,1)S(1)}, u32[]{:S(2)}, u32[]{:S(2)}) collective-permute-start(bf16[4,48,1536]{2,1,0:T(8,128)(2,1)S(1)} %pad_maximum_fusion.7), channel_id=1, source_target_pairs={{0,2},{1,3},{2,0},{3,1},{4,6},{5,7},{6,4},{7,5},{8,10},{9,11},{10,... | collective-permute-start | bytes 1769480 | tf_op jit(solution)/shard_map/ppermute | solution.py:953
  203.5 33.0 %collective-permute-start.37 = (bf16[8,96,768]{2,1,0:T(8,128)(2,1)S(1)}, bf16[8,96,768]{2,1,0:T(8,128)(2,1)S(1)}, u32[]{:S(2)}, u32[]{:S(2)}) collective-permute-start(bf16[8,96,768]{2,1,0:T(8,128)(2,1)S(1)} %pad_maximum_fusion.1.refs_3_), channel_id=1, source_target_pairs={{0,2},{1,3},{2,0},{3,1},{4,6},{5,7},{6,4},{7,5},{8,10},{9,11},{10,... | collective-permute-start | bytes 3538952 | tf_op jit(solution)/shard_map/ppermute | solution.py:953
  204.2 32.3 %collective-permute-start.36 = (bf16[8,48,1536]{2,1,0:T(8,128)(2,1)S(1)}, bf16[8,48,1536]{2,1,0:T(8,128)(2,1)S(1)}, u32[]{:S(2)}, u32[]{:S(2)}) collective-permute-start(bf16[8,48,1536]{2,1,0:T(8,128)(2,1)S(1)} %pad_maximum_fusion.2.refs_3_), channel_id=1, source_target_pairs={{0,8},{1,9},{2,10},{3,11},{4,12},{5,13},{6,14},{7,15},{8,0},{9,1},... | collective-permute-start | bytes 3538952 | tf_op jit(solution)/shard_map/ppermute | solution.py:953
  236.5 9.5 %collective-permute-start.43 = (bf16[52,16,768]{2,1,0:T(8,128)(2,1)S(1)}, bf16[52,16,768]{2,1,0:T(8,128)(2,1)S(1)}, u32[]{:S(2)}, u32[]{:S(2)}) collective-permute-start(bf16[52,16,768]{2,1,0:T(8,128)(2,1)S(1)} %slice.244), channel_id=1, source_target_pairs={{0,16},{16,0},{1,17},{17,1},{2,18},{18,2},{3,19},{19,3},{4,20},{20... | collective-permute-start | bytes 3833864 | tf_op jit(solution)/shard_map/ppermute | solution.py:939
  237.2 16.2 %collective-permute-start.40 = (bf16[8,48,1536]{2,1,0:T(8,128)(2,1)S(1)}, bf16[8,48,1536]{2,1,0:T(8,128)(2,1)S(1)}, u32[]{:S(2)}, u32[]{:S(2)}) collective-permute-start(bf16[8,48,1536]{2,1,0:T(8,128)(2,1)S(1)} %pad_maximum_fusion.3.b_low), channel_id=1, source_target_pairs={{0,1},{1,0},{2,3},{3,2},{4,5},{5,4},{6,7},{7,6},{8,9},{9,8},{10,11... | collective-permute-start | bytes 3538952 | tf_op jit(solution)/shard_map/ppermute | solution.py:953
  244.3 10.8 %collective-permute-start.46 = (bf16[8,48,1536]{2,1,0:T(8,128)(2,1)S(1)}, bf16[8,48,1536]{2,1,0:T(8,128)(2,1)S(1)}, u32[]{:S(2)}, u32[]{:S(2)}) collective-permute-start(bf16[8,48,1536]{2,1,0:T(8,128)(2,1)S(1)} %pad_maximum_fusion.2.refs_3_), channel_id=1, source_target_pairs={{0,16},{16,0},{1,17},{17,1},{2,18},{18,2},{3,19},{19,3},{4,20},{20... | collective-permute-start | bytes 3538952 | tf_op jit(solution)/shard_map/ppermute | solution.py:939
  (21 other events, 126.1 us)

commit v6 on v5

--- a/solution.py
+++ b/solution.py
@@ -49,7 +49,7 @@
 
 
 def turned(value):
-    return jnp.transpose(value.astype(F32)).astype(BF)
+    return jnp.transpose(value.astype(BF))
 
 
 def col_sum(value):
@@ -538,7 +538,7 @@
     section = info_ref[0]
     pick = layer_vectors(mine, table, section == 1)
     gain = pick(ATTN_G)
-    low = jnp.transpose(n1_ref[...] * gain + pick(ATTN_B)).astype(BF)
+    low = turned(n1_ref[...] * gain + pick(ATTN_B))
     ff = wi_ref.shape[1]
     half_chunks = ff // CHUNK // 2
     gf = gf_ref[...]

time: 272 us -> 272 us (level)
  no operation moved by 1% of the time
where the time goes in v6:
time: 272 us; the launch traced here: 266 us
  Pallas kernels  124 us (46%)
  waiting for transfers between devices  71 us (26%)
  starting transfers between devices  53.2 us (20%)
  other arithmetic  9.64 us (4%)
  local copies, waits for them, and re-layouts  4.93 us (2%)
  between operations  3.93 us (1%)
    ppermute x28, waiting for transfers between devices, hop(): return lax.ppermute(value, ('section', 'dp'), pairs)  58.6 us
    ppermute x28, starting transfers between devices, hop(): return lax.ppermute(value, ('section', 'dp'), pairs)  43.4 us
    pallas_call x1, Pallas kernels, train_call(): pl.pallas_call(train_kernel, in_specs=in_specs + [NEAR] * 2 + [FAR], out_...  26.3 us
    pallas_call x1, Pallas kernels, attention_call(): pl.pallas_call(attention_kernel, in_specs=[SCALARS, FAR, FAR] + [NEAR] *...  16.4 us
    pallas_call x1, Pallas kernels, feed_call(): pl.pallas_call(feed_kernel, in_specs=[SCALARS, NEAR] + [FAR] * 4 + [NEAR]...  12.7 us
    ppermute x20, waiting for transfers between devices, swap(): return lax.ppermute(value, 'section', SWAP)  12.4 us
    pallas_call x2, Pallas kernels, feed_final_call(): pl.pallas_call(lambda *refs: feed_final_kernel(outer, *refs), in_specs=[S...  11.6 us
    pallas_call x1, Pallas kernels, mixing_call(): pl.pallas_call(mixing_kernel, in_specs=[SCALARS] + [FAR] * 4 + [NEAR] * 2...  11.3 us
  transfers between devices with their start and end apart: 48, of which 16 were waited for; matrix products, arithmetic and copies ran while one was open for 4% of the time, Pallas kernels for 35%

profile of v6, /device:TPU:0, one launch (start us, length us, event | category | flops | bytes accessed | tf_op | source)
XLA Modules:
  0.0 266.4 jit_solution(7323287556495652524)
XLA Ops:
  5.7 7.6 %qkv.1 = (bf16[512,3072]{1,0:T(8,128)(2,1)S(1)}, bf16[512,3072]{1,0:T(8,128)(2,1)S(1)}, f32[16,768]{1,0:T(8,128)S(1)}) custom-call(s32[9]{0:T(128)S(1)} %stack.64.info_ref.refs_0_, bf16[2,512,768]{2,1,0:T(8,128)(2,1)} %bitcast.64, bf16[768,2304]{1,0:T(8,128)(2,1)} %bitcast.49, f32[1,768]{1,0:T(1,128)} %refs_0_.1, f32[1,768]{1,0:T(1,128)} %refs_1_.1, ...), custom_call_target="tpu_custom_call" | custom-call | flops 660000000 | bytes 1200000 | tf_op jit(solution)/shard_map/qkv/pallas_call | solution.py:167
  13.4 7.1 %head_rows.1 = (f32[32,768]{1,0:T(8,128)S(1)}, f32[16,9728]{1,0:T(8,128)S(1)}) custom-call(s32[9]{0:T(128)S(1)} %stack.64.info_ref.refs_0_, bf16[512,3072]{1,0:T(8,128)(2,1)S(1)} %get-tuple-element.119.own_ref.xq_a, bf16[512,3072]{1,0:T(8,128)(2,1)S(1)} %get-tuple-element.120.other_ref, bf16[768,768]{1,0:T(8,128)(2,1)} %bitcast.53, ...), custom_call_target="tpu_custom_call" | custom-call | flops 770000000 | bytes 1400000 | tf_op jit(solution)/shard_map/head_rows/pallas_call | solution.py:283
  21.0 3.7 %collective-permute-done.2.table.other = f32[32,768]{1,0:T(8,128)S(1)} collective-permute-done((f32[32,768]{1,0:T(8,128)S(1)}, f32[32,768]{1,0:T(8,128)S(1)}, u32[]{:S(2)}, u32[]{:S(2)}) %collective-permute-start.2) | collective-permute-done | bytes 98336 | tf_op jit(solution)/shard_map/ppermute | solution.py:939
  25.1 2.5 collective-permute-done.1.wp_b
  29.6 26.3 %layer_train.1 = (bf16[512,768]{1,0:T(8,128)(2,1)S(1)}, bf16[768,768]{1,0:T(8,128)(2,1)S(1)}, bf16[768,3072]{1,0:T(8,128)(2,1)S(1)}, bf16[3072,768]{1,0:T(8,128)...) custom-call(s32[9]{0:T(128)S(1)} %stack.64.info_ref.refs_0_, ...), custom_call_target="tpu_custom_call" | custom-call | flops 2860000000 | bytes 5200000 | tf_op jit(solution)/shard_map/layer_train/pallas_call | solution.py:486
  56.3 9.9 %inner_grad.1 = (bf16[16,48,1536]{2,1,0:T(8,128)(2,1)S(1)}, bf16[16,48,1536]{2,1,0:T(8,128)(2,1)S(1)}, f32[512,768]{1,0:T(8,128)S(1)}, bf16[512,768]{1,0:T(8,128...) custom-call(s32[9]{0:T(128)S(1)} %stack.64.info_ref.refs_0_, ...), custom_call_target="tpu_custom_call" | custom-call | flops 1100000000 | bytes 2000000 | tf_op jit(solution)/shard_map/inner_grad/pallas_call | solution.py:576
  67.2 3.0 %collective-permute-start.7 = (bf16[8,96,768]{2,1,0:T(8,128)(2,1)S(1)}, bf16[8,96,768]{2,1,0:T(8,128)(2,1)S(1)}, u32[]{:S(2)}, u32[]{:S(2)}) collective-permute-start(bf16[8,96,768]{2,1,0:T(8,128)(2,1)S(1)} %get-tuple-element.227), channel_id=1, source_target_pairs={{0,2},{1,3},{2,0},{3,1},{4,6},{5,7},{6,4},{7,5},{8,10},{9,11},{10,... | collective-permute-start | bytes 3538952 | tf_op jit(solution)/shard_map/ppermute | solution.py:953
  70.2 16.4 %attention_grad.1 = (bf16[16,48,1536]{2,1,0:T(8,128)(2,1)S(1)}, bf16[16,48,1536]{2,1,0:T(8,128)(2,1)S(1)}, bf16[512,2304]{1,0:T(8,128)(2,1)S(1)}, f32[8,768]{1,0:T(8,128)S(1)}) custom-call(s32[9]{0:T(128)S(1)} %stack.64.info_ref.refs_0_, bf16[512,3072]{1,0:T(8,128)(2,1)} %copy-done, bf16[512,3072]{1,0:T(8,128)(2,1)} %copy-done.2, ...), custom_call_target="tpu_custom_call" | custom-call | flops 1540000000 | bytes 2800000 | tf_op jit(solution)/shard_map/attention_grad/pallas_call | solution.py:658
  87.7 4.6 %input_grad.1 = (f32[512,768]{1,0:T(8,128)S(1)}, f32[16,768]{1,0:T(8,128)S(1)}) custom-call(s32[9]{0:T(128)S(1)} %stack.64.info_ref.refs_0_, bf16[768,2304]{1,0:T(8,128)(2,1)} %bitcast.51, bf16[768,2304]{1,0:T(8,128)(2,1)} %collective-permute-done.3.wq_b.w_b, bf16[512,2304]{1,0:T(8,128)(2,1)S(1)} %get-tuple-element.155.g_ref, ...), custom_call_target="tpu_custom_call" | custom-call | flops 440000000 | bytes 800000 | tf_op jit(solution)/shard_map/input_grad/pallas_call | solution.py:688
  93.9 2.6 collective-permute-start.14
  99.1 11.1 %head_rows_grad.1 = (f32[2,512,768]{2,1,0:T(8,128)S(1)}, bf16[64,768]{1,0:T(8,128)(2,1)S(1)}, bf16[64,768]{1,0:T(8,128)(2,1)S(1)}) custom-call(s32[9]{0:T(128)S(1)} %stack.64.info_ref.refs_0_, f32[16,768]{1,0:T(8,128)S(1)} %get-tuple-element.162.small_a, f32[16,768]{1,0:T(8,128)S(1)} %collective-permute-done.10.small_b, ...), custom_call_target="tpu_custom_call" | custom-call | flops 1320000000 | bytes 2400000 | tf_op jit(solution)/shard_map/head_rows_grad/pallas_call | solution.py:792
  110.4 11.3 %mixing.1.normed_ref = f32[512,768]{1,0:T(8,128)S(1)} custom-call(s32[9]{0:T(128)S(1)} %stack.64.info_ref.refs_0_, bf16[512,3072]{1,0:T(8,128)(2,1)} %copy-done, bf16[512,3072]{1,0:T(8,128)(2,1)} %copy-done.2, bf16[768,768]{1,0:T(8,128)(2,1)} %bitcast.56, bf16[768,768]{1,0:T(8,128)(2,1)} %copy-done.4, f32[32,768]{1,0:T(8,128)S(1)} %get-tuple-element.122.mine, ...), custom_call_target="tpu_custom_call" | custom-call | flops 1100000000 | bytes 2000000 | tf_op jit(solution)/shard_map/mixing/pallas_call | solution.py:364
  125.5 8.8 %collective-permute-done.17 = bf16[2,96,768]{2,1,0:T(8,128)(2,1)S(1)} collective-permute-done((bf16[2,96,768]{2,1,0:T(8,128)(2,1)S(1)}, bf16[2,96,768]{2,1,0:T(8,128)(2,1)S(1)}, u32[]{:S(2)}, u32[]{:S(2)}) %collective-permute-start.17) | collective-permute-done | bytes 294944 | tf_op jit(solution)/shard_map/ppermute | solution.py:953
  134.4 2.6 collective-permute-start.15
  141.8 5.5 %collective-permute-start.18 = (bf16[2,64,768]{2,0,1:T(2,128)(2,1)S(1)}, bf16[2,64,768]{2,0,1:T(2,128)(2,1)S(1)}, u32[]{:S(2)}, u32[]{:S(2)}) collective-permute-start(bf16[2,64,768]{2,0,1:T(2,128)(2,1)S(1)} %pad_maximum_fusion.12), channel_id=1, source_target_pairs={{0,4},{1,5},{2,6},{3,7},{4,0},{5,1},{6,2},{7,3},{8,12},{9,13},{10,... | collective-permute-start | bytes 589832 | tf_op jit(solution)/shard_map/ppermute | solution.py:953
  148.3 4.9 %collective-permute-done.18 = bf16[2,64,768]{2,0,1:T(2,128)(2,1)S(1)} collective-permute-done((bf16[2,64,768]{2,0,1:T(2,128)(2,1)S(1)}, bf16[2,64,768]{2,0,1:T(2,128)(2,1)S(1)}, u32[]{:S(2)}, u32[]{:S(2)}) %collective-permute-start.18) | collective-permute-done | bytes 196640 | tf_op jit(solution)/shard_map/ppermute | solution.py:953
  154.0 2.1 collective-permute-start.25
  156.3 6.7 %collective-permute-done.25 = bf16[2,48,1536]{2,1,0:T(8,128)(2,1)S(1)} collective-permute-done((bf16[2,48,1536]{2,1,0:T(8,128)(2,1)S(1)}, bf16[2,48,1536]{2,1,0:T(8,128)(2,1)S(1)}, u32[]{:S(2)}, u32[]{:S(2)}) %collective-permute-start.25) | collective-permute-done | bytes 294944 | tf_op jit(solution)/shard_map/ppermute | solution.py:953
  166.9 2.5 collective-permute-start.27
  169.9 9.1 %collective-permute-done.28 = bf16[1,48,1536]{2,1,0:T(8,128)(2,1)S(1)} collective-permute-done((bf16[1,48,1536]{2,1,0:T(8,128)(2,1)S(1)}, bf16[1,48,1536]{2,1,0:T(8,128)(2,1)S(1)}, u32[]{:S(2)}, u32[]{:S(2)}) %collective-permute-start.28) | collective-permute-done | bytes 147488 | tf_op jit(solution)/shard_map/ppermute | solution.py:953
  181.4 4.6 %collective-permute-done.30 = bf16[1,48,1536]{2,1,0:T(8,128)(2,1)S(1)} collective-permute-done((bf16[1,48,1536]{2,1,0:T(8,128)(2,1)S(1)}, bf16[1,48,1536]{2,1,0:T(8,128)(2,1)S(1)}, u32[]{:S(2)}, u32[]{:S(2)}) %collective-permute-start.30) | collective-permute-done | bytes 147488 | tf_op jit(solution)/shard_map/ppermute | solution.py:953
  188.2 2.3 collective-permute-start.33
  190.4 3.7 %collective-permute-start.38 = (f32[512,768]{1,0:T(8,128)S(1)}, f32[512,768]{1,0:T(8,128)S(1)}, u32[]{:S(2)}, u32[]{:S(2)}) collective-permute-start(f32[512,768]{1,0:T(8,128)S(1)} %get-tuple-element.203), channel_id=1, source_target_pairs={{0,16},{16,0},{1,17},{17,1},{2,18},{18,2},{3,19},{19,3},{4,20},{20... | collective-permute-start | bytes 4718600 | tf_op jit(solution)/shard_map/ppermute | solution.py:939
  195.8 6.1 %collective-permute-done.33 = bf16[2,48,1536]{2,1,0:T(8,128)(2,1)S(1)} collective-permute-done((bf16[2,48,1536]{2,1,0:T(8,128)(2,1)S(1)}, bf16[2,48,1536]{2,1,0:T(8,128)(2,1)S(1)}, u32[]{:S(2)}, u32[]{:S(2)}) %collective-permute-start.33) | collective-permute-done | bytes 294944 | tf_op jit(solution)/shard_map/ppermute | solution.py:953
  204.1 2.9 %collective-permute-start.36 = (bf16[8,48,1536]{2,1,0:T(8,128)(2,1)S(1)}, bf16[8,48,1536]{2,1,0:T(8,128)(2,1)S(1)}, u32[]{:S(2)}, u32[]{:S(2)}) collective-permute-start(bf16[8,48,1536]{2,1,0:T(8,128)(2,1)S(1)} %pad_maximum_fusion.2.refs_3_), channel_id=1, source_target_pairs={{0,8},{1,9},{2,10},{3,11},{4,12},{5,13},{6,14},{7,15},{8,0},{9,1},... | collective-permute-start | bytes 3538952 | tf_op jit(solution)/shard_map/ppermute | solution.py:953
  207.2 4.7 %collective-permute-done.35 = bf16[4,48,1536]{2,1,0:T(8,128)(2,1)S(1)} collective-permute-done((bf16[4,48,1536]{2,1,0:T(8,128)(2,1)S(1)}, bf16[4,48,1536]{2,1,0:T(8,128)(2,1)S(1)}, u32[]{:S(2)}, u32[]{:S(2)}) %collective-permute-start.35) | collective-permute-done | bytes 589856 | tf_op jit(solution)/shard_map/ppermute | solution.py:953
  212.1 12.7 %layer_feed.1 = bf16[512,768]{1,0:T(8,128)(2,1)S(1)} custom-call(s32[9]{0:T(128)S(1)} %stack.64.info_ref.refs_0_, f32[512,768]{1,0:T(8,128)S(1)} %mixing.1.normed_ref, bf16[768,3072]{1,0:T(8,128)(2,1)} %bitcast.42, bf16[768,3072]{1,0:T(8,128)(2,1)} %collective-permute-done.4.wi_b, bf16[3072,768]{1,0:T(8,128)(2,1)} %bitcast.47, ...), custom_call_target="tpu_custom_call" | custom-call | flops 1210000000 | bytes 2200000 | tf_op jit(solution)/shard_map/layer_feed/pallas_call | solution.py:522
  226.8 8.4 %collective-permute-done.37.refs_4_ = bf16[8,96,768]{2,1,0:T(8,128)(2,1)S(1)} collective-permute-done((bf16[8,96,768]{2,1,0:T(8,128)(2,1)S(1)}, bf16[8,96,768]{2,1,0:T(8,128)(2,1)S(1)}, u32[]{:S(2)}, u32[]{:S(2)}) %collective-permute-start.37) | collective-permute-done | bytes 1179680 | tf_op jit(solution)/shard_map/ppermute | solution.py:953
  239.3 5.0 %collective-permute-done.39 = bf16[512,768]{1,0:T(8,128)(2,1)S(1)} collective-permute-done((bf16[512,768]{1,0:T(8,128)(2,1)S(1)}, bf16[512,768]{1,0:T(8,128)(2,1)S(1)}, u32[]{:S(2)}, u32[]{:S(2)}) %collective-permute-start.39) | collective-permute-done | bytes 786464 | tf_op jit(solution)/shard_map/ppermute | solution.py:939
  246.1 5.8 %outer_final.1 = f32[3072,768]{1,0:T(8,128)} custom-call(s32[9]{0:T(128)S(1)} %stack.64.info_ref.refs_0_, bf16[8,96,768]{2,1,0:T(8,128)(2,1)S(1)} %collective-permute-done.41.refs_1_, bf16[8,96,768]{2,1,0:T(8,128)(2,1)S(1)} %collective-permute-done.42.refs_2_, bf16[8,96,768]{2,1,0:T(8,128)(2,1)S(1)} %pad_maximum_fusion.1.refs_3_, ...), custom_call_target="tpu_custom_call" | custom-call | flops 440000000 | bytes 800000 | tf_op jit(solution)/shard_map/outer_final/pallas_call | solution.py:852
  255.1 5.8 %inner_final.1 = f32[768,3072]{1,0:T(8,128)} custom-call(s32[9]{0:T(128)S(1)} %stack.64.info_ref.refs_0_, bf16[8,48,1536]{2,1,0:T(8,128)(2,1)S(1)} %collective-permute-done.46.refs_1_, bf16[8,48,1536]{2,1,0:T(8,128)(2,1)S(1)} %collective-permute-done.47.refs_2_, bf16[8,48,1536]{2,1,0:T(8,128)(2,1)S(1)} %pad_maximum_fusion.2.refs_3_, ...), custom_call_target="tpu_custom_call" | custom-call | flops 440000000 | bytes 800000 | tf_op jit(solution)/shard_map/inner_final/pallas_call | solution.py:852
  260.9 5.3 %qkv_final.1 = (f32[768,2304]{1,0:T(8,128)}, f32[768,768]{1,0:T(8,128)}) custom-call(s32[9]{0:T(128)S(1)} %stack.64.info_ref.refs_0_, bf16[8,48,1536]{2,1,0:T(8,128)(2,1)S(1)} %collective-permute-done.44.a_low, bf16[8,48,1536]{2,1,0:T(8,128)(2,1)S(1)} %collective-permute-done.45.a_high, bf16[8,48,1536]{2,1,0:T(8,128)(2,1)S(1)} %pad_maximum_fusion.3.b_low, ...), custom_call_target="tpu_custom_call" | custom-call | flops 440000000 | bytes 800000 | tf_op jit(solution)/shard_map/qkv_final/pallas_call | solution.py:922
  (129 shorter events, 47.1 us)
Async XLA Ops:
  0.6 26.9 %collective-permute-start.4 = (bf16[768,3072]{1,0:T(8,128)(2,1)}, bf16[768,3072]{1,0:T(8,128)(2,1)}, u32[]{:S(2)}, u32[]{:S(2)}) collective-permute-start(bf16[768,3072]{1,0:T(8,128)(2,1)} %bitcast.38), channel_id=1, source_target_pairs={{0,16},{16,0},{1,17},{17,1},{2,18},{18,2},{3,19},{19,3},{4,20},{20... | collective-permute-start | bytes 14155784 | tf_op jit(solution)/shard_map/ppermute | solution.py:939
  1.2 26.4 %collective-permute-start.5 = (bf16[3072,768]{1,0:T(8,128)(2,1)}, bf16[3072,768]{1,0:T(8,128)(2,1)}, u32[]{:S(2)}, u32[]{:S(2)}) collective-permute-start(bf16[3072,768]{1,0:T(8,128)(2,1)} %bitcast.43), channel_id=1, source_target_pairs={{0,16},{16,0},{1,17},{17,1},{2,18},{18,2},{3,19},{19,3},{4,20},{20... | collective-permute-start | bytes 14155784 | tf_op jit(solution)/shard_map/ppermute | solution.py:939
  1.2 26.3 %collective-permute-start.3 = (bf16[768,2304]{1,0:T(8,128)(2,1)}, bf16[768,2304]{1,0:T(8,128)(2,1)}, u32[]{:S(2)}, u32[]{:S(2)}) collective-permute-start(bf16[768,2304]{1,0:T(8,128)(2,1)} %bitcast.48), channel_id=1, source_target_pairs={{0,16},{16,0},{1,17},{17,1},{2,18},{18,2},{3,19},{19,3},{4,20},{20... | collective-permute-start | bytes 10616840 | tf_op jit(solution)/shard_map/ppermute | solution.py:939
  13.3 14.3 %collective-permute-start = (bf16[512,3072]{1,0:T(8,128)(2,1)S(1)}, bf16[512,3072]{1,0:T(8,128)(2,1)S(1)}, u32[]{:S(2)}, u32[]{:S(2)}) collective-permute-start(bf16[512,3072]{1,0:T(8,128)(2,1)S(1)} %get-tuple-element.120.other_ref), channel_id=1, source_target_pairs={{0,16},{16,0},{1,17},{17,1},{2,18},{18,2},{3,19},{19,3},{4,20},{20... | collective-permute-start | bytes 9437192 | tf_op jit(solution)/shard_map/ppermute | solution.py:939
  55.9 10.3 %collective-permute-start.6 = (bf16[16,96,768]{2,1,0:T(8,128)(2,1)S(1)}, bf16[16,96,768]{2,1,0:T(8,128)(2,1)S(1)}, u32[]{:S(2)}, u32[]{:S(2)}) collective-permute-start(bf16[16,96,768]{2,1,0:T(8,128)(2,1)S(1)} %get-tuple-element.138), channel_id=1, source_target_pairs={{0,16},{16,0},{1,17},{17,1},{2,18},{18,2},{3,19},{19,3},{4,20},{20... | collective-permute-start | bytes 7077896 | tf_op jit(solution)/shard_map/ppermute | solution.py:939
  66.2 20.3 %collective-permute-start.8 = (bf16[16,48,1536]{2,1,0:T(8,128)(2,1)S(1)}, bf16[16,48,1536]{2,1,0:T(8,128)(2,1)S(1)}, u32[]{:S(2)}, u32[]{:S(2)}) collective-permute-start(bf16[16,48,1536]{2,1,0:T(8,128)(2,1)S(1)} %get-tuple-element.152), channel_id=1, source_target_pairs={{0,16},{16,0},{1,17},{17,1},{2,18},{18,2},{3,19},{19,3},{4,20},{20... | collective-permute-start | bytes 7077896 | tf_op jit(solution)/shard_map/ppermute | solution.py:939
  67.2 19.3 %collective-permute-start.7 = (bf16[8,96,768]{2,1,0:T(8,128)(2,1)S(1)}, bf16[8,96,768]{2,1,0:T(8,128)(2,1)S(1)}, u32[]{:S(2)}, u32[]{:S(2)}) collective-permute-start(bf16[8,96,768]{2,1,0:T(8,128)(2,1)S(1)} %get-tuple-element.227), channel_id=1, source_target_pairs={{0,2},{1,3},{2,0},{3,1},{4,6},{5,7},{6,4},{7,5},{8,10},{9,11},{10,... | collective-permute-start | bytes 3538952 | tf_op jit(solution)/shard_map/ppermute | solution.py:953
  92.3 17.9 %collective-permute-start.9 = (bf16[4,96,768]{2,1,0:T(8,128)(2,1)S(1)}, bf16[4,96,768]{2,1,0:T(8,128)(2,1)S(1)}, u32[]{:S(2)}, u32[]{:S(2)}) collective-permute-start(bf16[4,96,768]{2,1,0:T(8,128)(2,1)S(1)} %get-tuple-element.233), channel_id=1, source_target_pairs={{0,1},{1,0},{2,3},{3,2},{4,5},{5,4},{6,7},{7,6},{8,9},{9,8},{10,11... | collective-permute-start | bytes 1769480 | tf_op jit(solution)/shard_map/ppermute | solution.py:953
  93.9 29.8 %collective-permute-start.14 = (bf16[8,48,1536]{2,1,0:T(8,128)(2,1)S(1)}, bf16[8,48,1536]{2,1,0:T(8,128)(2,1)S(1)}, u32[]{:S(2)}, u32[]{:S(2)}) collective-permute-start(bf16[8,48,1536]{2,1,0:T(8,128)(2,1)S(1)} %get-tuple-element.223), channel_id=1, source_target_pairs={{0,8},{1,9},{2,10},{3,11},{4,12},{5,13},{6,14},{7,15},{8,0},{9,1},... | collective-permute-start | bytes 3538952 | tf_op jit(solution)/shard_map/ppermute | solution.py:953
  97.2 27.7 %collective-permute-start.13 = (bf16[8,48,1536]{2,1,0:T(8,128)(2,1)S(1)}, bf16[8,48,1536]{2,1,0:T(8,128)(2,1)S(1)}, u32[]{:S(2)}, u32[]{:S(2)}) collective-permute-start(bf16[8,48,1536]{2,1,0:T(8,128)(2,1)S(1)} %get-tuple-element.225), channel_id=1, source_target_pairs={{0,1},{1,0},{2,3},{3,2},{4,5},{5,4},{6,7},{7,6},{8,9},{9,8},{10,11... | collective-permute-start | bytes 3538952 | tf_op jit(solution)/shard_map/ppermute | solution.py:953
  123.7 10.6 %collective-permute-start.17 = (bf16[2,96,768]{2,1,0:T(8,128)(2,1)S(1)}, bf16[2,96,768]{2,1,0:T(8,128)(2,1)S(1)}, u32[]{:S(2)}, u32[]{:S(2)}) collective-permute-start(bf16[2,96,768]{2,1,0:T(8,128)(2,1)S(1)} %get-tuple-element.241), channel_id=1, source_target_pairs={{0,8},{1,9},{2,10},{3,11},{4,12},{5,13},{6,14},{7,15},{8,0},{9,1},... | collective-permute-start | bytes 884744 | tf_op jit(solution)/shard_map/ppermute | solution.py:953
  124.1 10.3 %collective-permute-start.16 = (bf16[4,48,1536]{2,1,0:T(8,128)(2,1)S(1)}, bf16[4,48,1536]{2,1,0:T(8,128)(2,1)S(1)}, u32[]{:S(2)}, u32[]{:S(2)}) collective-permute-start(bf16[4,48,1536]{2,1,0:T(8,128)(2,1)S(1)} %get-tuple-element.231), channel_id=1, source_target_pairs={{0,1},{1,0},{2,3},{3,2},{4,5},{5,4},{6,7},{7,6},{8,9},{9,8},{10,11... | collective-permute-start | bytes 1769480 | tf_op jit(solution)/shard_map/ppermute | solution.py:953
  137.0 10.4 %collective-permute-start.20 = (bf16[4,48,1536]{2,1,0:T(8,128)(2,1)S(1)}, bf16[4,48,1536]{2,1,0:T(8,128)(2,1)S(1)}, u32[]{:S(2)}, u32[]{:S(2)}) collective-permute-start(bf16[4,48,1536]{2,1,0:T(8,128)(2,1)S(1)} %get-tuple-element.229), channel_id=1, source_target_pairs={{0,2},{1,3},{2,0},{3,1},{4,6},{5,7},{6,4},{7,5},{8,10},{9,11},{10,... | collective-permute-start | bytes 1769480 | tf_op jit(solution)/shard_map/ppermute | solution.py:953
  137.6 9.9 %collective-permute-start.19 = (bf16[1,96,768]{2,1,0:T(8,128)(2,1)S(1)}, bf16[1,96,768]{2,1,0:T(8,128)(2,1)S(1)}, u32[]{:S(2)}, u32[]{:S(2)}) collective-permute-start(bf16[1,96,768]{2,1,0:T(8,128)(2,1)S(1)} %get-tuple-element.247), channel_id=1, source_target_pairs={{0,4},{1,5},{2,6},{3,7},{4,0},{5,1},{6,2},{7,3},{8,12},{9,13},{10,... | collective-permute-start | bytes 442376 | tf_op jit(solution)/shard_map/ppermute | solution.py:953
  138.9 15.2 %collective-permute-start.22 = (bf16[2,48,1536]{2,1,0:T(8,128)(2,1)S(1)}, bf16[2,48,1536]{2,1,0:T(8,128)(2,1)S(1)}, u32[]{:S(2)}, u32[]{:S(2)}) collective-permute-start(bf16[2,48,1536]{2,1,0:T(8,128)(2,1)S(1)} %get-tuple-element.239), channel_id=1, source_target_pairs={{0,2},{1,3},{2,0},{3,1},{4,6},{5,7},{6,4},{7,5},{8,10},{9,11},{10,... | collective-permute-start | bytes 884744 | tf_op jit(solution)/shard_map/ppermute | solution.py:953
  141.8 11.3 %collective-permute-start.18 = (bf16[2,64,768]{2,0,1:T(2,128)(2,1)S(1)}, bf16[2,64,768]{2,0,1:T(2,128)(2,1)S(1)}, u32[]{:S(2)}, u32[]{:S(2)}) collective-permute-start(bf16[2,64,768]{2,0,1:T(2,128)(2,1)S(1)} %pad_maximum_fusion.12), channel_id=1, source_target_pairs={{0,4},{1,5},{2,6},{3,7},{4,0},{5,1},{6,2},{7,3},{8,12},{9,13},{10,... | collective-permute-start | bytes 589832 | tf_op jit(solution)/shard_map/ppermute | solution.py:953
  147.6 15.5 %collective-permute-start.24 = (bf16[1,96,768]{2,1,0:T(8,128)(2,1)S(1)}, bf16[1,96,768]{2,1,0:T(8,128)(2,1)S(1)}, u32[]{:S(2)}, u32[]{:S(2)}) collective-permute-start(bf16[1,96,768]{2,1,0:T(8,128)(2,1)S(1)} %add_convert_fusion.24), channel_id=1, source_target_pairs={{0,4},{1,5},{2,6},{3,7},{4,0},{5,1},{6,2},{7,3},{8,12},{9,13},{10,... | collective-permute-start | bytes 442376 | tf_op jit(solution)/shard_map/ppermute | solution.py:953
  153.6 15.9 %collective-permute-start.21 = (bf16[4,64,768]{2,0,1:T(4,128)(2,1)S(1)}, bf16[4,64,768]{2,0,1:T(4,128)(2,1)S(1)}, u32[]{:S(2)}, u32[]{:S(2)}) collective-permute-start(bf16[4,64,768]{2,0,1:T(4,128)(2,1)S(1)} %pad_maximum_fusion.8), channel_id=1, source_target_pairs={{0,2},{1,3},{2,0},{3,1},{4,6},{5,7},{6,4},{7,5},{8,10},{9,11},{10,... | collective-permute-start | bytes 1179656 | tf_op jit(solution)/shard_map/ppermute | solution.py:953
  163.2 17.5 %collective-permute-start.31 = (bf16[2,96,768]{2,1,0:T(8,128)(2,1)S(1)}, bf16[2,96,768]{2,1,0:T(8,128)(2,1)S(1)}, u32[]{:S(2)}, u32[]{:S(2)}) collective-permute-start(bf16[2,96,768]{2,1,0:T(8,128)(2,1)S(1)} %pad_maximum_fusion.9), channel_id=1, source_target_pairs={{0,8},{1,9},{2,10},{3,11},{4,12},{5,13},{6,14},{7,15},{8,0},{9,1},... | collective-permute-start | bytes 884744 | tf_op jit(solution)/shard_map/ppermute | solution.py:953
  165.3 13.7 %collective-permute-start.28 = (bf16[1,48,1536]{2,1,0:T(8,128)(2,1)S(1)}, bf16[1,48,1536]{2,1,0:T(8,128)(2,1)S(1)}, u32[]{:S(2)}, u32[]{:S(2)}) collective-permute-start(bf16[1,48,1536]{2,1,0:T(8,128)(2,1)S(1)} %get-tuple-element.243), channel_id=1, source_target_pairs={{0,8},{1,9},{2,10},{3,11},{4,12},{5,13},{6,14},{7,15},{8,0},{9,1},... | collective-permute-start | bytes 442376 | tf_op jit(solution)/shard_map/ppermute | solution.py:953
  166.9 12.2 %collective-permute-start.27 = (bf16[1,48,1536]{2,1,0:T(8,128)(2,1)S(1)}, bf16[1,48,1536]{2,1,0:T(8,128)(2,1)S(1)}, u32[]{:S(2)}, u32[]{:S(2)}) collective-permute-start(bf16[1,48,1536]{2,1,0:T(8,128)(2,1)S(1)} %add_convert_fusion.20), channel_id=1, source_target_pairs={{0,4},{1,5},{2,6},{3,7},{4,0},{5,1},{6,2},{7,3},{8,12},{9,13},{10,... | collective-permute-start | bytes 442376 | tf_op jit(solution)/shard_map/ppermute | solution.py:953
  180.7 15.0 %collective-permute-start.34 = (bf16[4,96,768]{2,1,0:T(8,128)(2,1)S(1)}, bf16[4,96,768]{2,1,0:T(8,128)(2,1)S(1)}, u32[]{:S(2)}, u32[]{:S(2)}) collective-permute-start(bf16[4,96,768]{2,1,0:T(8,128)(2,1)S(1)} %pad_maximum_fusion.5), channel_id=1, source_target_pairs={{0,1},{1,0},{2,3},{3,2},{4,5},{5,4},{6,7},{7,6},{8,9},{9,8},{10,11... | collective-permute-start | bytes 1769480 | tf_op jit(solution)/shard_map/ppermute | solution.py:953
  186.1 17.9 %collective-permute-start.32 = (bf16[4,48,1536]{2,1,0:T(8,128)(2,1)S(1)}, bf16[4,48,1536]{2,1,0:T(8,128)(2,1)S(1)}, u32[]{:S(2)}, u32[]{:S(2)}) collective-permute-start(bf16[4,48,1536]{2,1,0:T(8,128)(2,1)S(1)} %pad_maximum_fusion.6), channel_id=1, source_target_pairs={{0,1},{1,0},{2,3},{3,2},{4,5},{5,4},{6,7},{7,6},{8,9},{9,8},{10,11... | collective-permute-start | bytes 1769480 | tf_op jit(solution)/shard_map/ppermute | solution.py:953
  188.2 13.7 %collective-permute-start.33 = (bf16[2,48,1536]{2,1,0:T(8,128)(2,1)S(1)}, bf16[2,48,1536]{2,1,0:T(8,128)(2,1)S(1)}, u32[]{:S(2)}, u32[]{:S(2)}) collective-permute-start(bf16[2,48,1536]{2,1,0:T(8,128)(2,1)S(1)} %pad_maximum_fusion.11), channel_id=1, source_target_pairs={{0,4},{1,5},{2,6},{3,7},{4,0},{5,1},{6,2},{7,3},{8,12},{9,13},{10,... | collective-permute-start | bytes 884744 | tf_op jit(solution)/shard_map/ppermute | solution.py:953
  190.4 34.4 %collective-permute-start.38 = (f32[512,768]{1,0:T(8,128)S(1)}, f32[512,768]{1,0:T(8,128)S(1)}, u32[]{:S(2)}, u32[]{:S(2)}) collective-permute-start(f32[512,768]{1,0:T(8,128)S(1)} %get-tuple-element.203), channel_id=1, source_target_pairs={{0,16},{16,0},{1,17},{17,1},{2,18},{18,2},{3,19},{19,3},{4,20},{20... | collective-permute-start | bytes 4718600 | tf_op jit(solution)/shard_map/ppermute | solution.py:939
  194.1 12.9 %collective-permute-start.26 = (bf16[8,64,768]{2,0,1:T(8,128)(2,1)S(1)}, bf16[8,64,768]{2,0,1:T(8,128)(2,1)S(1)}, u32[]{:S(2)}, u32[]{:S(2)}) collective-permute-start(bf16[8,64,768]{2,0,1:T(8,128)(2,1)S(1)} %pad_maximum_fusion.4), channel_id=1, source_target_pairs={{0,1},{1,0},{2,3},{3,2},{4,5},{5,4},{6,7},{7,6},{8,9},{9,8},{10,11... | collective-permute-start | bytes 2359304 | tf_op jit(solution)/shard_map/ppermute | solution.py:953
  201.9 9.9 %collective-permute-start.35 = (bf16[4,48,1536]{2,1,0:T(8,128)(2,1)S(1)}, bf16[4,48,1536]{2,1,0:T(8,128)(2,1)S(1)}, u32[]{:S(2)}, u32[]{:S(2)}) collective-permute-start(bf16[4,48,1536]{2,1,0:T(8,128)(2,1)S(1)} %pad_maximum_fusion.7), channel_id=1, source_target_pairs={{0,2},{1,3},{2,0},{3,1},{4,6},{5,7},{6,4},{7,5},{8,10},{9,11},{10,... | collective-permute-start | bytes 1769480 | tf_op jit(solution)/shard_map/ppermute | solution.py:953
  203.3 31.9 %collective-permute-start.37 = (bf16[8,96,768]{2,1,0:T(8,128)(2,1)S(1)}, bf16[8,96,768]{2,1,0:T(8,128)(2,1)S(1)}, u32[]{:S(2)}, u32[]{:S(2)}) collective-permute-start(bf16[8,96,768]{2,1,0:T(8,128)(2,1)S(1)} %pad_maximum_fusion.1.refs_3_), channel_id=1, source_target_pairs={{0,2},{1,3},{2,0},{3,1},{4,6},{5,7},{6,4},{7,5},{8,10},{9,11},{10,... | collective-permute-start | bytes 3538952 | tf_op jit(solution)/shard_map/ppermute | solution.py:953
  204.1 31.2 %collective-permute-start.36 = (bf16[8,48,1536]{2,1,0:T(8,128)(2,1)S(1)}, bf16[8,48,1536]{2,1,0:T(8,128)(2,1)S(1)}, u32[]{:S(2)}, u32[]{:S(2)}) collective-permute-start(bf16[8,48,1536]{2,1,0:T(8,128)(2,1)S(1)} %pad_maximum_fusion.2.refs_3_), channel_id=1, source_target_pairs={{0,8},{1,9},{2,10},{3,11},{4,12},{5,13},{6,14},{7,15},{8,0},{9,1},... | collective-permute-start | bytes 3538952 | tf_op jit(solution)/shard_map/ppermute | solution.py:953
  235.4 10.6 %collective-permute-start.43 = (bf16[52,16,768]{2,1,0:T(8,128)(2,1)S(1)}, bf16[52,16,768]{2,1,0:T(8,128)(2,1)S(1)}, u32[]{:S(2)}, u32[]{:S(2)}) collective-permute-start(bf16[52,16,768]{2,1,0:T(8,128)(2,1)S(1)} %slice.244), channel_id=1, source_target_pairs={{0,16},{16,0},{1,17},{17,1},{2,18},{18,2},{3,19},{19,3},{4,20},{20... | collective-permute-start | bytes 3833864 | tf_op jit(solution)/shard_map/ppermute | solution.py:939
  237.1 16.2 %collective-permute-start.40 = (bf16[8,48,1536]{2,1,0:T(8,128)(2,1)S(1)}, bf16[8,48,1536]{2,1,0:T(8,128)(2,1)S(1)}, u32[]{:S(2)}, u32[]{:S(2)}) collective-permute-start(bf16[8,48,1536]{2,1,0:T(8,128)(2,1)S(1)} %pad_maximum_fusion.3.b_low), channel_id=1, source_target_pairs={{0,1},{1,0},{2,3},{3,2},{4,5},{5,4},{6,7},{7,6},{8,9},{9,8},{10,11... | collective-permute-start | bytes 3538952 | tf_op jit(solution)/shard_map/ppermute | solution.py:953
  244.2 10.8 %collective-permute-start.46 = (bf16[8,48,1536]{2,1,0:T(8,128)(2,1)S(1)}, bf16[8,48,1536]{2,1,0:T(8,128)(2,1)S(1)}, u32[]{:S(2)}, u32[]{:S(2)}) collective-permute-start(bf16[8,48,1536]{2,1,0:T(8,128)(2,1)S(1)} %pad_maximum_fusion.2.refs_3_), channel_id=1, source_target_pairs={{0,16},{16,0},{1,17},{17,1},{2,18},{18,2},{3,19},{19,3},{4,20},{20... | collective-permute-start | bytes 3538952 | tf_op jit(solution)/shard_map/ppermute | solution.py:939
  (21 other events, 126.2 us)
